TPU v7x, 32 devices: a whole 2x2x4 slice. The times are simulated.
32 devices in a mesh: seq: 8 (over z, x), chan: 4 (over y, core).
Axes of the slice: x: 2, y: 2, z: 4, core: 2. Of those that a mesh axis runs over, the one named last changes fastest.
Arguments:
- tokens: bfloat16 [1024, 4096], P('seq'), may hold values from -6 to 6
- w_inner: bfloat16 [4096, 4096], P('seq', 'chan'), may hold values from -0.09375 to 0.09375
- w_keyquery: bfloat16 [4096, 4, 32], P('seq', 'chan'), may hold values from -0.09375 to 0.09375
- rate: float32 [4096], P('chan'), may hold values from 0.00048828125 to 0.05
- grad_out: bfloat16 [1024, 4096], P('seq', 'chan'), may hold values from -6 to 6
Outputs:
- mixed: bfloat16 [1024, 4096], P('seq', 'chan')
- grad_tokens: bfloat16 [1024, 4096], P('seq', 'chan')
- grad_keyquery: float32 [4096, 4, 32], P('seq', 'chan')
All inputs are finite; a program needn't handle non-finite values.
Results may differ from a plain program's by a relative error of at most 0.0049.
Values may be sent and summed in bfloat16 or wider, within the bound.
No kernel may reach another device: no remote copies, remote signals or barrier semaphores. Data moves between devices by JAX's collectives and lax.ppermute only.
A program may use at most 128 MiB of HBM per device.

v0:
```python
import jax
import jax.numpy as jnp
from jax import lax
from jax.sharding import PartitionSpec as P

NS = 16


def shifted(value, axis, by):
    peers = lax.axis_size(axis)
    pairs = [(i, i + by) for i in range(peers) if 0 <= i + by < peers]
    return lax.ppermute(value, axis, pairs)


def step_sizes(keys, beta):
    sumsq = jnp.sum(keys * keys, axis=1)
    return beta[None, :] / (1.0 + beta[None, :] * sumsq[:, None])


def forward_totals(inner, keys, beta):
    eps = step_sizes(keys, beta)

    def forward_step(carry, row):
        state, factor = carry
        eps_row, xrow, krow = row
        decay = 1.0 - eps_row[None, :] * (krow * krow)[:, None]
        state = decay * state + (eps_row * xrow)[None, :] * krow[:, None]
        return ((state, factor * decay), None)

    zeros = jnp.zeros((keys.shape[1], inner.shape[1]), jnp.float32)
    ones = jnp.ones((keys.shape[1], inner.shape[1]), jnp.float32)
    totals, unused = lax.scan(forward_step, (zeros, ones), (eps, inner, keys))
    return totals


def full_pass(inner, keys, queries, beta, start_state):
    eps = step_sizes(keys, beta)

    def full_step(state, row):
        eps_row, xrow, krow, qrow = row
        decay = 1.0 - eps_row[None, :] * (krow * krow)[:, None]
        state = decay * state + (eps_row * xrow)[None, :] * krow[:, None]
        return (state, jnp.sum(state * qrow[:, None], axis=0))

    end_state, outputs = lax.scan(full_step, start_state, (eps, inner, keys, queries))
    return (outputs, end_state)


def local_adjoint_pass(keys, queries, cot_out, beta):
    eps = step_sizes(keys, beta)

    def local_step(lam, row):
        eps_row, krow, qrow, crow = row
        decay = 1.0 - eps_row[None, :] * (krow * krow)[:, None]
        lam = decay * (qrow[:, None] * crow[None, :] + lam)
        return (lam, None)

    start = jnp.zeros((keys.shape[1], cot_out.shape[1]), jnp.float32)
    result, unused = lax.scan(local_step, start, (eps, keys, queries, cot_out), reverse=True)
    return result


def doubling_prefix(decay_total, local_state, reverse):
    count = lax.axis_size("seq")
    index = lax.axis_index("seq")

    def move(pair, offset):
        if reverse:
            return shifted((pair[0], pair[1]), "seq", -offset)
        return shifted((pair[0], pair[1]), "seq", offset)

    factor, state = (decay_total, local_state)
    offset = 1
    while offset < count:
        far_factor, far_state = move((factor, state), offset)
        if reverse:
            valid = index + offset < count
        else:
            valid = index >= offset
        new_factor = jnp.where(valid, far_factor * factor, factor)
        state = jnp.where(valid, factor * far_state + state, state)
        factor = new_factor
        offset = offset * 2
    return move((factor, state), 1)[1]


def per_device(tokens, w_inner, w_keyquery, rate, grad_out):
    kq_cols = w_keyquery.shape[1] * w_keyquery.shape[2]
    full_inner, full_kq = (
        lax.all_gather(w_inner, "seq", axis=0, tiled=True),
        lax.all_gather(w_keyquery, "seq", axis=0, tiled=True),
    )
    full_kq = full_kq.reshape(full_kq.shape[0], kq_cols)
    inner = jnp.dot(tokens, full_inner, preferred_element_type=jnp.float32)
    keyquery = jnp.dot(tokens, full_kq, preferred_element_type=jnp.float32)
    keys = keyquery[:, :NS]
    queries = keyquery[:, NS:]
    cot_out = grad_out.astype(jnp.float32)
    alone_end, decay_total = forward_totals(inner, keys, rate)
    start_state = doubling_prefix(decay_total, alone_end, False)
    local_adjoint = local_adjoint_pass(keys, queries, cot_out, rate)
    end_adjoint = doubling_prefix(decay_total, local_adjoint, True)

    def run(inner_in, keys_in, queries_in):
        return full_pass(inner_in, keys_in, queries_in, rate, start_state)

    (outputs, end_state), vjp_full = jax.vjp(run, inner, keys, queries)
    mixed = outputs.astype(jnp.bfloat16)
    grads = vjp_full((cot_out, end_adjoint))
    inner_grad = grads[0].astype(jnp.bfloat16)
    kq_grad = jnp.concatenate([grads[1], grads[2]], axis=1).astype(jnp.bfloat16)
    partial_sum = jnp.einsum(
        "tc,dc->td", inner_grad, full_inner, preferred_element_type=jnp.float32
    )
    partial_sum = partial_sum + jnp.einsum(
        "tk,dk->td", kq_grad, full_kq, preferred_element_type=jnp.float32
    )
    grad_tokens = lax.psum_scatter(partial_sum, "chan", scatter_dimension=1, tiled=True).astype(
        jnp.bfloat16
    )
    grad_rows = lax.psum_scatter(
        jnp.einsum("td,tk->dk", tokens, kq_grad, preferred_element_type=jnp.float32),
        "seq",
        scatter_dimension=0,
        tiled=True,
    )
    grad_keyquery = grad_rows.reshape(w_keyquery.shape[0], w_keyquery.shape[1], w_keyquery.shape[2])
    return (mixed, grad_tokens, grad_keyquery)


def solution(mesh):
    return jax.shard_map(
        per_device,
        mesh=mesh,
        in_specs=(
            P("seq", None),
            P("seq", "chan"),
            P("seq", "chan", None),
            P("chan"),
            P("seq", "chan"),
        ),
        out_specs=(P("seq", "chan"), P("seq", "chan"), P("seq", "chan", None)),
        check_vma=False,
    )
```

profile of v0, /device:TPU:0, one launch (start us, length us, event | category | flops | bytes accessed | tf_op | source)
XLA Modules:
  0.0 1506.5 jit_solution(3874560191928998773)
XLA Ops:
  8.0 33.8 %all_gather.6 = bf16[4096,1,32]{0,2,1:T(8,128)(2,1)S(1)} all-gather(bf16[512,1,32]{0,2,1:T(8,128)(2,1)} %param.15), channel_id=1, replica_groups=mesh['seq'=8,'chan'=4] {'seq'}, dimensions={0}, use_global_device_ids=true | all-gather | bytes 294912 | tf_op jit(solution)/shard_map/all_gather | solution.py:91
  44.3 19.6 %while.81 = (s32[]{:T(128)}, f32[16,1024]{1,0:T(8,128)S(1)}, f32[128,1024]{1,0:T(8,128)S(1)}, f32[128,16]{1,0:T(8,128)S(1)}, f32[128,16]{1,0:T(8,128)S(1)}, /*in...) while((s32[]{:T(128)}, f32[16,1024]{1,0:T(8,128)S(1)}, f32[128,1024]{1,0:T(8,128)S(1)}, ...), condition=%wide.region_7.8_spmd.clone, body=%wide.region_6.7_spmd.clone.sunk | while | flops 98324 | bytes 156155 | solution.py:59
  65.3 74.4 %all-gather.2.cloned.1.call-done = bf16[4096,1024]{1,0:T(8,128)(2,1)} async-done(((bf16[512,1024]{1,0:T(8,128)(2,1)}), bf16[4096,1024]{1,0:T(8,128)(2,1)}) %all-gather.2.cloned.1.call-update) | async-done | bytes 8388624 | tf_op jit(solution)/shard_map/all_gather | solution.py:90
  139.7 4.6 fusion.31
  144.3 19.7 %while.80 = (s32[]{:T(128)}, f32[16,1024]{1,0:T(8,128)S(1)}, f32[16,1024]{1,0:T(8,128)S(1)}, f32[128,1024]{1,0:T(8,128)S(1)}, f32[128,16]{1,0:T(8,128)S(1)}, /*index=5*/f32[128,1024]{1,0:T(8,128)S(1)}, s32[]{:T(128)}, s32[]{:T(128)}) while((s32[]{:T(128)}, f32[16,1024]{1,0:T(8,128)S(1)}, f32[16,1024]{1,0:T(8,128)S(1)}, ...), condition=%wide.region_2.3_spmd.clone, body=%wide.region_1.2_spmd.clone.sunk | while | flops 132115 | bytes 287143 | solution.py:32
  166.6 4.5 collective-permute-start.2
  171.3 4.1 collective-permute-start
  175.4 3.9 collective-permute-start.3
  179.4 1.8 collective-permute-done.3
  181.3 4.3 collective-permute-start.1
  185.5 3.4 collective-permute-start.4
  192.2 3.3 collective-permute-start.5
  198.8 341.2 %while.78 = (s32[]{:T(128)}, f32[16,1024]{1,0:T(8,128)S(1)}, bf16[128,1024]{1,0:T(8,128)(2,1)S(1)}, f32[128,16,1]{1,2,0:T(1,128)S(1)}, f32[128,1,1024]{2,1,0:T(1...) while((s32[]{:T(128)}, f32[16,1024]{1,0:T(8,128)S(1)}, ...), condition=%wide.region_5.6_spmd, body=%wide.region_3.5_spmd.sunk | while | flops 148514 | bytes 461421 | solution.py:45
  540.7 847.6 %while.79 = (s32[]{:T(128)}, f32[16,1024]{1,0:T(8,128)S(1)}, f32[128,1024]{1,0:T(8,128)S(1)}, bf16[128,1024]{1,0:T(8,128)(2,1)S(1)}, f32[128,16]{1,0:T(8,128)S(1...) while((s32[]{:T(128)}, f32[16,1024]{1,0:T(8,128)S(1)}, ...), condition=%wide.region_14.15_spmd, body=%wide.region_8.14_spmd.sunk | while | flops 247811 | bytes 413081 | solution.py:45
  543.5 1.7 multiply_reduce_fusion.10
  550.2 1.7 multiply_reduce_fusion.10
  556.9 1.7 multiply_reduce_fusion.10
  563.6 1.7 multiply_reduce_fusion.10
  570.2 1.7 multiply_reduce_fusion.10
  576.9 1.7 multiply_reduce_fusion.10
  583.5 1.7 multiply_reduce_fusion.10
  590.1 1.7 multiply_reduce_fusion.10
  596.7 1.7 multiply_reduce_fusion.10
  603.3 1.7 multiply_reduce_fusion.10
  609.8 1.7 multiply_reduce_fusion.10
  616.4 1.7 multiply_reduce_fusion.10
  622.9 1.7 multiply_reduce_fusion.10
  629.4 1.7 multiply_reduce_fusion.10
  635.9 1.7 multiply_reduce_fusion.10
  642.4 1.7 multiply_reduce_fusion.10
  649.0 1.7 multiply_reduce_fusion.10
  655.6 1.7 multiply_reduce_fusion.10
  662.2 1.7 multiply_reduce_fusion.10
  668.8 1.7 multiply_reduce_fusion.10
  675.4 1.7 multiply_reduce_fusion.10
  682.1 1.7 multiply_reduce_fusion.10
  688.7 1.7 multiply_reduce_fusion.10
  695.4 1.7 multiply_reduce_fusion.10
  702.0 1.7 multiply_reduce_fusion.10
  708.6 1.7 multiply_reduce_fusion.10
  715.1 1.7 multiply_reduce_fusion.10
  721.7 1.7 multiply_reduce_fusion.10
  728.3 1.7 multiply_reduce_fusion.10
  734.9 1.7 multiply_reduce_fusion.10
  741.6 1.7 multiply_reduce_fusion.10
  748.2 1.7 multiply_reduce_fusion.10
  754.9 1.7 multiply_reduce_fusion.10
  761.5 1.7 multiply_reduce_fusion.10
  768.2 1.7 multiply_reduce_fusion.10
  774.8 1.7 multiply_reduce_fusion.10
  814.4 1.7 multiply_reduce_fusion.10
  861.0 1.7 multiply_reduce_fusion.10
  954.0 1.7 multiply_reduce_fusion.10
  987.4 1.7 multiply_reduce_fusion.10
  994.0 1.7 multiply_reduce_fusion.10
  1140.1 1.7 multiply_reduce_fusion.10
  1298.5 1.7 multiply_reduce_fusion.10
  1311.6 1.7 multiply_reduce_fusion.10
  1331.3 1.7 multiply_reduce_fusion.10
  1357.7 1.7 multiply_reduce_fusion.10
  1391.3 7.7 convolution_add_fusion
  1400.2 33.2 %reduce-scatter.3.cloned.1.call-done = f32[128,1024]{1,0:T(8,128)} async-done(((f32[128,4096]{1,0:T(8,128)}), f32[128,1024]{1,0:T(8,128)}) %reduce-scatter.3.cloned.1.call-update) | async-done | bytes 524304 | tf_op jit(solution)/shard_map/reduce_scatter | solution.py:118
  1433.3 1.8 convert_element_type.16
  1435.1 64.9 %reduce-scatter.5.cloned.1.call-done = f32[512,32]{0,1:T(8,128)} async-done(((f32[4096,32]{0,1:T(8,128)}), f32[512,32]{0,1:T(8,128)}) %reduce-scatter.5.cloned.1.call-update) | async-done | bytes 65552 | tf_op jit(solution)/shard_map/reduce_scatter | solution.py:121
  (3480 shorter events, 1152.8 us)
Async XLA Ops:
  7.2 34.6 %copy-start = (bf16[128,4096]{1,0:T(8,128)(2,1)S(1)}, bf16[128,4096]{1,0:T(8,128)(2,1)}, u32[]{:S(2)}) copy-start(bf16[128,4096]{1,0:T(8,128)(2,1)} %param.13) | copy-start | bytes 3145732
  7.2 132.5 %all-gather.2.cloned.1.call-start = ((), (), s32[]{:S(2)}) async-start(), calls=%async_computation.2 | async-start | bytes 9437184 | tf_op jit(solution)/shard_map/all_gather | solution.py:90
  7.9 1425.4 %reduce-scatter.3.cloned.1.call-start = ((), (), s32[]{:S(2)}) async-start(), calls=%async_computation.3 | async-start | bytes 2621440 | tf_op jit(solution)/shard_map/reduce_scatter | solution.py:118
  42.2 1.3 copy-start.3
  42.3 21.7 %copy-start.5 = (f32[128]{0:T(128)}, f32[128]{0:T(128)S(1)}, u32[]{:S(2)}) copy-start(f32[128]{0:T(128)S(1)} %get-tuple-element.828) | copy-start | bytes 1540
  63.9 1.3 copy-start.1
  64.0 101.4 %collective-permute-start.8 = (f32[16,1024]{1,0:T(8,128)S(1)}, f32[16,1024]{1,0:T(8,128)S(1)}, u32[]{:S(2)}, u32[]{:S(2)}) collective-permute-start(f32[16,1024]{1,0:T(8,128)S(1)} %get-tuple-element.599), channel_id=1, source_target_pairs={{4,0},{8,4},{12,8},{16,12},{20,16},{24,20},{28,24},{5,1},{9,5},{13... | collective-permute-start | bytes 196616 | tf_op jit(solution)/shard_map/ppermute | solution.py:12
  164.0 11.4 collective-permute-start.6
  165.3 10.0 collective-permute-start.9
  166.6 8.7 collective-permute-start.2
  171.3 8.1 collective-permute-start
  175.4 5.8 collective-permute-start.3
  181.3 10.9 collective-permute-start.1
  185.5 6.6 collective-permute-start.4
  189.5 7.3 collective-permute-start.10
  190.8 6.6 collective-permute-start.7
  192.2 6.6 collective-permute-start.5
  197.5 342.5 %collective-permute-start.11 = (f32[16,1024]{1,0:T(8,128)S(1)}, f32[16,1024]{1,0:T(8,128)S(1)}, u32[]{:S(2)}, u32[]{:S(2)}) collective-permute-start(f32[16,1024]{1,0:T(8,128)S(1)} %add_select_fusion), channel_id=1, source_target_pairs={{4,0},{8,4},{12,8},{16,12},{20,16},{24,20},{28,24},{5,1},{9,5},{13... | collective-permute-start | bytes 196616 | tf_op jit(solution)/shard_map/ppermute | solution.py:12
  540.0 0.6 copy-start.4
  540.0 0.6 copy-start.6
  540.0 859.0 %copy-start.2 = (bf16[128,1024]{1,0:T(8,128)(2,1)}, bf16[128,1024]{1,0:T(8,128)(2,1)S(1)}, u32[]{:S(2)}) copy-start(bf16[128,1024]{1,0:T(8,128)(2,1)S(1)} %get-tuple-element.598) | copy-start | bytes 786436
  1399.0 101.0 %reduce-scatter.5.cloned.1.call-start = ((), (), s32[]{:S(2)}) async-start(), calls=%async_computation.4 | async-start | bytes 589824 | tf_op jit(solution)/shard_map/reduce_scatter | solution.py:121
Sparse Core Ops, SparseCore 0:
  10.1 129.5 all-gather.1
  1399.1 34.1 reduce-scatter.2
  1437.6 62.3 reduce-scatter.4
where the time goes:
time: 1540 us; the launch traced here: 1510 us
  local copies, waits for them, and re-layouts  630 us (41%)
  other arithmetic  588 us (38%)
  waiting for transfers between devices  177 us (11%)
  blocking collectives  33.8 us (2%)
  starting transfers between devices  31.3 us (2%)
  loops' own time  17.8 us (1%)
    dynamic_update_slice x768, local copies, waits for them, and re-layouts, full_pass(): lax.scan(full_step, start_state, (eps, inner, keys, queries))  271 us
    dynamic_update_slice x384, other arithmetic, full_pass(): lax.scan(full_step, start_state, (eps, inner, keys, queries))  237 us
    reduce_sum x128, other arithmetic, full_step(): decay = 1.0 - eps_row[None, :] * (krow * krow)[:, None]  212 us
    dynamic_slice x256, local copies, waits for them, and re-layouts, forward_totals(): totals, unused = lax.scan(forward_step, (zeros, ones), (eps, inner, keys))  99.6 us
    add_any x256, other arithmetic, full_step(): decay = 1.0 - eps_row[None, :] * (krow * krow)[:, None]  90.2 us
    dynamic_slice x128, local copies, waits for them, and re-layouts, full_pass(): lax.scan(full_step, start_state, (eps, inner, keys, queries))  87.8 us
    mul x256, local copies, waits for them, and re-layouts, full_step(): return (state, jnp.sum(state * qrow[:, None], axis=0))  87.8 us
    mul x128, local copies, waits for them, and re-layouts, full_step(): decay = 1.0 - eps_row[None, :] * (krow * krow)[:, None]  81.4 us
  transfers between devices with their start and end apart: 15, of which 6 were waited for; matrix products, arithmetic and copies ran while one was open for 25% of the time, Pallas kernels for 0%

commit v1 on v0

v1 whole, which is shorter than its diff:
```python
import functools

import jax
import jax.numpy as jnp
from jax import lax
from jax.experimental import pallas as pl
from jax.experimental.pallas import tpu as pltpu
from jax.sharding import PartitionSpec as P

NS = 16
LANES = 128
UNROLL = 8
F32 = jnp.float32
BF16 = jnp.bfloat16


def lane_groups(width):
    return [slice(j * LANES, (j + 1) * LANES) for j in range(width // LANES)]


def tile(ref, first, cols):
    return ref[pl.ds(first, UNROLL), cols]


def place(rows, at, value):
    here = lax.broadcasted_iota(jnp.int32, rows.shape, 0) == at
    return jnp.where(here, jnp.broadcast_to(value, rows.shape), rows)


def to_float(src, dst):
    dst[...] = src[...].astype(F32)


def adjoint_totals_kernel(kq, eps, cot, lam_out, decay_out, cot_f):
    tokens, width = eps.shape
    groups = lane_groups(width)
    to_float(cot, cot_f)

    def block(i, carry):
        lams, decays = carry
        first = pl.multiple_of(tokens - (i + 1) * UNROLL, UNROLL)
        steps = [tile(eps, first, cols) for cols in groups]
        cots = [tile(cot_f, first, cols) for cols in groups]
        for j in reversed(range(UNROLL)):
            t = first + j
            keys = kq[t, :NS, :]
            queries = kq[t, NS:, :]
            square = keys * keys
            new_lams, new_decays = [], []
            for lam, total, step, cot_row in zip(lams, decays, steps, cots):
                decay = 1.0 - step[j : j + 1] * square
                new_lams.append(decay * (queries * cot_row[j : j + 1] + lam))
                new_decays.append(total * decay)
            lams, decays = new_lams, new_decays
        return (tuple(lams), tuple(decays))

    zeros = tuple(jnp.zeros((NS, LANES), F32) for _ in groups)
    ones = tuple(jnp.ones((NS, LANES), F32) for _ in groups)
    lams, decays = lax.fori_loop(0, tokens // UNROLL, block, (zeros, ones))
    for lam, total, cols in zip(lams, decays, groups):
        lam_out[:, cols] = lam
        decay_out[:, cols] = total


def adjoint_kernel(kq, eps, cot, start, adj_out, grad_out, cot_f, grad_f):
    tokens, width = eps.shape
    groups = lane_groups(width)
    to_float(cot, cot_f)

    def block(i, lams):
        first = pl.multiple_of(tokens - (i + 1) * UNROLL, UNROLL)
        steps = [tile(eps, first, cols) for cols in groups]
        cots = [tile(cot_f, first, cols) for cols in groups]
        grads = [jnp.zeros((UNROLL, LANES), F32) for _ in groups]
        for j in reversed(range(UNROLL)):
            t = first + j
            keys = kq[t, :NS, :]
            queries = kq[t, NS:, :]
            square = keys * keys
            new_lams = []
            for n, cols in enumerate(groups):
                adj = queries * cots[n][j : j + 1] + lams[n]
                adj_out[t, :, cols] = adj
                grads[n] = place(grads[n], j, jnp.sum(adj * keys, axis=0, keepdims=True))
                new_lams.append((1.0 - steps[n][j : j + 1] * square) * adj)
            lams = new_lams
        for n, cols in enumerate(groups):
            grad_f[pl.ds(first, UNROLL), cols] = steps[n] * grads[n]
        return tuple(lams)

    lax.fori_loop(0, tokens // UNROLL, block, tuple(start[:, cols] for cols in groups))
    grad_out[...] = grad_f[...].astype(BF16)


def state_total_kernel(kq, eps, inner, state_out):
    tokens, width = eps.shape
    groups = lane_groups(width)

    def block(i, states):
        first = pl.multiple_of(i * UNROLL, UNROLL)
        steps = [tile(eps, first, cols) for cols in groups]
        pushes = [tile(inner, first, cols) * step for cols, step in zip(groups, steps)]
        for j in range(UNROLL):
            t = first + j
            keys = kq[t, :NS, :]
            square = keys * keys
            states = [
                (1.0 - step[j : j + 1] * square) * state + push[j : j + 1] * keys
                for state, step, push in zip(states, steps, pushes)
            ]
        return tuple(states)

    zeros = tuple(jnp.zeros((NS, LANES), F32) for _ in groups)
    states = lax.fori_loop(0, tokens // UNROLL, block, zeros)
    for state, cols in zip(states, groups):
        state_out[:, cols] = state


def mixer_kernel(kq, eps, inner, cot, adj_in, start, mixed_out, gkq_out, cot_f, mixed_f, key_acc, query_acc):
    tokens, width = eps.shape
    groups = lane_groups(width)
    to_float(cot, cot_f)

    @pl.when(pl.program_id(0) == 0)
    def _():
        key_acc[...] = jnp.zeros_like(key_acc)
        query_acc[...] = jnp.zeros_like(query_acc)

    def block(i, states):
        first = pl.multiple_of(i * UNROLL, UNROLL)
        steps = [tile(eps, first, cols) for cols in groups]
        inners = [tile(inner, first, cols) for cols in groups]
        pushes = [step * x for step, x in zip(steps, inners)]
        squares = [step * step for step in steps]
        cots = [tile(cot_f, first, cols) for cols in groups]
        outs = [jnp.zeros((UNROLL, LANES), F32) for _ in groups]
        for j in range(UNROLL):
            t = first + j
            keys = kq[t, :NS, :]
            queries = kq[t, NS:, :]
            square = keys * keys
            new_states = []
            key_sum = jnp.zeros((NS, LANES), F32)
            step_sum = jnp.zeros((NS, LANES), F32)
            query_sum = jnp.zeros((NS, LANES), F32)
            for n, cols in enumerate(groups):
                step = steps[n][j : j + 1]
                adj = adj_in[t, :, cols]
                through_decay = keys * (adj * states[n])
                through_both = inners[n][j : j + 1] * adj - through_decay
                key_sum = key_sum + step * (through_both - through_decay)
                step_sum = step_sum + squares[n][j : j + 1] * through_both
                state = (1.0 - step * square) * states[n] + pushes[n][j : j + 1] * keys
                query_sum = query_sum + state * cots[n][j : j + 1]
                outs[n] = place(outs[n], j, jnp.sum(state * queries, axis=0, keepdims=True))
                new_states.append(state)
            states = new_states
            through_step = jnp.sum(keys * step_sum, axis=0, keepdims=True)
            key_acc[t] += key_sum - 2.0 * keys * through_step
            query_acc[t] += query_sum
        for n, cols in enumerate(groups):
            mixed_f[pl.ds(first, UNROLL), cols] = outs[n]
        return tuple(states)

    lax.fori_loop(0, tokens // UNROLL, block, tuple(start[:, cols] for cols in groups))
    mixed_out[...] = mixed_f[...].astype(BF16)

    @pl.when(pl.program_id(0) == pl.num_programs(0) - 1)
    def _():
        ones = jnp.ones((LANES, LANES), F32)
        lane = lax.broadcasted_iota(jnp.int32, (NS, LANES), 1)
        state = lax.broadcasted_iota(jnp.int32, (NS, LANES), 0)

        def spread(acc, first):
            total = jnp.dot(
                acc[...].reshape(tokens * NS, LANES),
                ones,
                preferred_element_type=F32,
                precision=lax.Precision.HIGHEST,
            )
            placed = jnp.where(
                (lane == state + first)[None], total.reshape(tokens, NS, LANES), 0.0
            )
            return jnp.sum(placed, axis=1)

        gkq_out[...] = spread(key_acc, 0) + spread(query_acc, NS)


def call(kernel, tokens, width, block, ins, outs, scratch, args, flops):
    def spec(kind):
        return {
            "kq": pl.BlockSpec((tokens, 2 * NS, LANES), lambda c: (0, 0, 0)),
            "rows": pl.BlockSpec((tokens, block), lambda c: (0, c)),
            "rows16": pl.BlockSpec((tokens, block), lambda c: (0, c)),
            "state": pl.BlockSpec((NS, block), lambda c: (0, c)),
            "states": pl.BlockSpec((tokens, NS, block), lambda c: (0, 0, c)),
            "gkq": pl.BlockSpec((tokens, LANES), lambda c: (0, 0)),
        }[kind]

    def shape(kind):
        return {
            "rows": jax.ShapeDtypeStruct((tokens, width), F32),
            "rows16": jax.ShapeDtypeStruct((tokens, width), BF16),
            "state": jax.ShapeDtypeStruct((NS, width), F32),
            "states": jax.ShapeDtypeStruct((tokens, NS, width), F32),
            "gkq": jax.ShapeDtypeStruct((tokens, LANES), F32),
        }[kind]

    return pl.pallas_call(
        kernel,
        grid=(width // block,),
        in_specs=[spec(kind) for kind in ins],
        out_specs=[spec(kind) for kind in outs],
        out_shape=[shape(kind) for kind in outs],
        scratch_shapes=scratch,
        compiler_params=pltpu.CompilerParams(vmem_limit_bytes=48 * 2**20),
        cost_estimate=pl.CostEstimate(
            flops=flops * tokens * NS * width,
            bytes_accessed=4 * tokens * width * (1 + NS * ("states" in ins + outs)),
            transcendentals=0,
        ),
    )(*args)


def shifted(value, axis, by):
    peers = lax.axis_size(axis)
    pairs = [(i, i + by) for i in range(peers) if 0 <= i + by < peers]
    return lax.ppermute(value, axis, pairs)


def carried(decay, total, sign):
    count = lax.axis_size("seq")
    window, radix = 1, 4
    inc_decay, inc_total = decay, total
    exc_decay, exc_total = None, None
    while window < count:
        last = window * radix >= count
        for j in range(1, radix):
            if window * j >= count:
                break
            far_total = shifted(inc_total, "seq", sign * window * j)
            far_decay = shifted(inc_decay, "seq", sign * window * j)
            if exc_total is None:
                exc_total, exc_decay = far_total, far_decay
            else:
                exc_total = exc_total + exc_decay * far_total
                exc_decay = exc_decay * far_decay
        if not last:
            inc_total = total + decay * exc_total
            inc_decay = decay * exc_decay
        window *= radix
    return exc_total


def gather_columns(value, axis):
    count = lax.axis_size(axis)
    parts = lax.all_to_all(
        jnp.broadcast_to(value[None], (count,) + value.shape), axis, 0, 0, tiled=True
    )
    return jnp.moveaxis(parts, 0, 1).reshape(value.shape[0], count * value.shape[1])


def scatter_sum_columns(value):
    count = lax.axis_size("chan")
    index = lax.axis_index("chan")
    if count & (count - 1):
        return lax.psum_scatter(value, "chan", scatter_dimension=1, tiled=True)
    blocks = jnp.moveaxis(value.reshape(value.shape[0], count, -1), 1, 0)
    offset = 1
    while offset < count:
        pairs = blocks.reshape((-1, 2) + blocks.shape[1:])
        bit = (index // offset) % 2
        mine = lax.dynamic_index_in_dim(pairs, bit, 1, keepdims=False)
        other = lax.dynamic_index_in_dim(pairs, 1 - bit, 1, keepdims=False)
        wire = other if offset == 1 else other.astype(BF16)
        swap = [(i, i ^ offset) for i in range(count)]
        blocks = mine + lax.ppermute(wire, "chan", swap).astype(F32)
        offset *= 2
    return blocks[0]


def per_device(tokens, w_inner, w_keyquery, rate, grad_out):
    count = tokens.shape[0]
    width = w_inner.shape[1]
    kq_cols = w_keyquery.shape[1] * w_keyquery.shape[2]
    seqs, chans = lax.axis_size("seq"), lax.axis_size("chan")
    block = min(width, 512)
    full_inner = lax.all_gather(w_inner, "seq", axis=0, tiled=True)
    full_kq = gather_columns(w_keyquery.reshape(-1, kq_cols).T, "seq")
    keyquery = lax.dot_general(
        tokens, full_kq, (((1,), (1,)), ((), ())), preferred_element_type=F32
    )
    keys = keyquery[:, :NS]
    sumsq = jnp.sum(keys * keys, axis=1)
    eps = rate[None, :] / (1.0 + rate[None, :] * sumsq[:, None])
    spread = jnp.broadcast_to(keyquery[:, :, None], (count, 2 * NS, LANES))
    rows_f = pltpu.VMEM((count, block), F32)
    run = functools.partial(call, tokens=count, width=width, block=block)

    lam, decay = run(
        adjoint_totals_kernel,
        ins=["kq", "rows", "rows16"], outs=["state", "state"], scratch=[rows_f],
        args=(spread, eps, grad_out), flops=8,
    )
    end_adjoint = carried(decay, lam, -1)
    adjoints, inner_grad = run(
        adjoint_kernel,
        ins=["kq", "rows", "rows16", "state"], outs=["states", "rows16"], scratch=[rows_f, rows_f],
        args=(spread, eps, grad_out, end_adjoint), flops=8,
    )
    inner = jnp.dot(tokens, full_inner, preferred_element_type=F32)
    partial_sum = lax.dot_general(
        inner_grad, full_inner, (((1,), (1,)), ((), ())), preferred_element_type=F32
    )
    tokens_sum = scatter_sum_columns(partial_sum)
    (alone_end,) = run(
        state_total_kernel,
        ins=["kq", "rows", "rows"], outs=["state"], scratch=[],
        args=(spread, eps, inner), flops=6,
    )
    start_state = carried(decay, alone_end, 1)
    acc = pltpu.VMEM((count, NS, LANES), F32)
    mixed, kq_grad = run(
        mixer_kernel,
        ins=["kq", "rows", "rows", "rows16", "states", "state"], outs=["rows16", "gkq"],
        scratch=[rows_f, rows_f, acc, acc],
        args=(spread, eps, inner, grad_out, adjoints, start_state), flops=20,
    )
    kq_grad = kq_grad[:, :kq_cols].astype(BF16)

    kq_rows = lax.all_to_all(
        jnp.moveaxis(full_kq.reshape(kq_cols, chans, -1), 1, 0), "chan", 0, 0, tiled=True
    )
    kq_rows = kq_rows.reshape(chans * kq_cols, -1)
    all_kq = gather_columns(kq_grad, "chan")
    grad_tokens = (
        tokens_sum + jnp.dot(all_kq, kq_rows, preferred_element_type=F32)
    ).astype(BF16)

    grad_cols = lax.dot_general(
        kq_grad, tokens, (((0,), (0,)), ((), ())), preferred_element_type=F32
    )
    grad_parts = lax.all_to_all(
        jnp.moveaxis(grad_cols.reshape(kq_cols, seqs, -1), 1, 0), "seq", 0, 0, tiled=True
    )
    grad_keyquery = jnp.sum(grad_parts, axis=0).T.reshape(w_keyquery.shape)
    return (mixed, grad_tokens, grad_keyquery)


def solution(mesh):
    return jax.shard_map(
        per_device,
        mesh=mesh,
        in_specs=(
            P("seq", None),
            P("seq", "chan"),
            P("seq", "chan", None),
            P("chan"),
            P("seq", "chan"),
        ),
        out_specs=(P("seq", "chan"), P("seq", "chan"), P("seq", "chan", None)),
        check_vma=False,
    )
```

time: 1540 us -> 273 us (0.18); the launches traced: 1510 us -> 271 us
  local copies, waits for them, and re-layouts: 630 us -> 27.7 us
  other arithmetic: 588 us -> 8.91 us
  waiting for transfers between devices: 177 us -> 123 us
  Pallas kernels: 0 us -> 21.1 us
  loops' own time: 17.8 us -> 0 us
  blocking collectives: 33.8 us -> 16.1 us
    dynamic_update_slice x768 -> x0, local copies, waits for them, and re-layouts: 271 us -> none  [full_pass(): lax.scan(full_step, start_state, (eps, inner, keys, queries))]
    dynamic_update_slice x384 -> x0, other arithmetic: 237 us -> none  [full_pass(): lax.scan(full_step, start_state, (eps, inner, keys, queries))]
    reduce_sum x257 -> x2, other arithmetic: 224 us -> 0.68 us  [the longest x1 0.67 us: per_device(): grad_keyquery = jnp.sum(grad_parts, axis=0).T.reshape(w_keyquery.shape)]
    dynamic_slice x384 -> x1, local copies, waits for them, and re-layouts: 187 us -> 5.37 us  [scatter_sum_columns(): mine = lax.dynamic_index_in_dim(pairs, bit, 1, keepdims=False)]
    mul x384 -> x0, local copies, waits for them, and re-layouts: 169 us -> none  [the longest x256 87.8 us: full_step(): return (state, jnp.sum(state * qrow[:, None], axis=0))]
    reduce_scatter x2 -> x0, waiting for transfers between devices: 98.1 us -> none  [the longest x1 64.9 us: per_device(): lax.psum_scatter(jnp.einsum('td,tk->dk', tokens, kq_grad, preferred_eleme...]
    add_any x256 -> x0, other arithmetic: 90.2 us -> none  [full_step(): decay = 1.0 - eps_row[None, :] * (krow * krow)[:, None]]
    all_gather x1 -> x0, blocking collectives: 33.8 us -> none  [per_device(): lax.all_gather(w_keyquery, 'seq', axis=0, tiled=True)]
  transfers between devices with their start and end apart: 15 -> 20, of which waited for: 6 -> 6; matrix products, arithmetic and copies ran while one was open for 25% -> 8% of each run, Pallas kernels for 0% -> 6%
where the time goes in v1:
time: 273 us; the launch traced here: 271 us
  waiting for transfers between devices  123 us (45%)
  starting transfers between devices  45.3 us (17%)
  local copies, waits for them, and re-layouts  27.7 us (10%)
  Pallas kernels  21.1 us (8%)
  blocking collectives  16.1 us (6%)
  between operations  14.5 us (5%)
  matrix products  14.2 us (5%)
  other arithmetic  8.91 us (3%)
    all_gather x1, waiting for transfers between devices, per_device(): full_inner = lax.all_gather(w_inner, 'seq', axis=0, tiled=True)  101 us
    ppermute x14, starting transfers between devices, shifted(): return lax.ppermute(value, axis, pairs)  34.2 us
    pallas_call x4, Pallas kernels, call(): pl.pallas_call(kernel, grid=(width // block,), in_specs=[spec(kind) for k...  21.1 us
    all_to_all x1, blocking collectives, gather_columns(): lax.all_to_all(jnp.broadcast_to(value[None], (count,) + value.shape), axi...  16.1 us
    all_to_all x1, waiting for transfers between devices, per_device(): lax.all_to_all(jnp.moveaxis(grad_cols.reshape(kq_cols, seqs, -1), 1, 0),...  11.3 us
    dot_general x1, matrix products, per_device(): lax.dot_general(inner_grad, full_inner, (((1,), (1,)), ((), ())), preferr...  7.59 us
    ppermute x14, waiting for transfers between devices, shifted(): return lax.ppermute(value, axis, pairs)  7.43 us
    unnamed x33, local copies, waits for them, and re-layouts  6.31 us
  transfers between devices with their start and end apart: 20, of which 6 were waited for; matrix products, arithmetic and copies ran while one was open for 8% of the time, Pallas kernels for 6%

profile of v1, /device:TPU:0, one launch (start us, length us, event | category | flops | bytes accessed | tf_op | source)
XLA Modules:
  0.0 271.3 jit_solution(6950323287606507940)
XLA Ops:
  7.2 0.0 copy-start
  7.2 0.0 all-gather.2.cloned.1.call-start
  7.2 0.7 all-gather.2.cloned.1.call-update
  7.9 0.8 broadcast_in_dim.6
  8.7 16.1 %all_to_all.20 = bf16[8,32,512]{2,1,0:T(8,128)(2,1)S(1)} all-to-all(bf16[8,32,512]{2,1,0:T(8,128)(2,1)S(1)} %broadcast_in_dim.6), channel_id=1, replica_groups=mesh['seq'=8,'chan'=4] {'seq'}, dimensions={0} | all-to-all | bytes 524288 | tf_op jit(solution)/shard_map/all_to_all | solution.py:257
  24.8 0.7 copy-done.9
  25.5 0.5 fusion.6
  26.0 0.1 copy.18
  26.1 0.8 add_divide_fusion.eps
  27.0 0.6 broadcast_in_dim.7.kq
  27.6 0.2 copy-done.1
  27.7 1.0 copy-done.7
  28.7 2.1 shard_map.76
  30.8 3.8 %collective-permute-start.8 = (f32[16,1024]{1,0:T(8,128)S(1)}, f32[16,1024]{1,0:T(8,128)}, u32[]{:S(2)}, u32[]{:S(2)}) collective-permute-start(f32[16,1024]{1,0:T(8,128)S(1)} %get-tuple-element.10), channel_id=1, source_target_pairs={{0,4},{4,8},{8,12},{12,16},{16,20},{20,24},{24,28},{1,5},{5,9},{9,... | collective-permute-start | bytes 196616 | tf_op jit(solution)/shard_map/ppermute | solution.py:228
  34.6 2.0 collective-permute-start.10
  36.6 1.3 collective-permute-start.1
  37.9 1.3 collective-permute-start.3
  39.2 0.0 copy-start.8
  39.2 1.4 collective-permute-start.4
  40.6 101.3 %all-gather.2.cloned.1.call-done = bf16[4096,1024]{1,0:T(8,128)(2,1)} async-done(((bf16[512,1024]{1,0:T(8,128)(2,1)}), bf16[4096,1024]{1,0:T(8,128)(2,1)}) %all-gather.2.cloned.1.call-update) | async-done | bytes 8388624 | tf_op jit(solution)/shard_map/all_gather | solution.py:288
  141.9 4.7 %fusion.7.inner = f32[128,1024]{1,0:T(8,128)S(1)} fusion(bf16[128,4096]{1,0:T(8,128)(2,1)S(1)} %copy-done, bf16[4096,1024]{1,0:T(8,128)(2,1)} %all-gather.2.cloned.1.call-done), kind=kOutput, calls=%fused_computation.25 | convolution fusion | flops 1073741824 | bytes 9961472 | tf_op jit(solution)/shard_map/dot_general | solution.py:311
  146.6 1.9 shard_map.78
  148.5 1.3 collective-permute-start
  149.8 1.3 collective-permute-start.2
  151.1 6.6 %collective-permute-start.11 = (f32[16,1024]{1,0:T(8,128)S(1)}, f32[16,1024]{1,0:T(8,128)S(1)}, u32[]{:S(2)}, u32[]{:S(2)}) collective-permute-start(f32[16,1024]{1,0:T(8,128)S(1)} %shard_map.78), channel_id=1, source_target_pairs={{0,12},{4,16},{8,20},{12,24},{16,28},{1,13},{5,17},{9,21},{13,25},... | collective-permute-start | bytes 196616 | tf_op jit(solution)/shard_map/ppermute | solution.py:228
  157.8 3.4 %collective-permute-start.7 = (f32[16,1024]{1,0:T(8,128)S(1)}, f32[16,1024]{1,0:T(8,128)S(1)}, u32[]{:S(2)}, u32[]{:S(2)}) collective-permute-start(f32[16,1024]{1,0:T(8,128)S(1)} %shard_map.78), channel_id=1, source_target_pairs={{0,4},{4,8},{8,12},{12,16},{16,20},{20,24},{24,28},{1,5},{5,9},{9,... | collective-permute-start | bytes 196616 | tf_op jit(solution)/shard_map/ppermute | solution.py:228
  161.2 2.0 collective-permute-start.9
  163.2 1.3 collective-permute-start.5
  164.5 0.5 collective-permute-done.9
  165.0 1.7 multiply_add_fusion.1
  166.7 1.3 collective-permute-start.6
  168.1 2.3 collective-permute-done.5
  170.3 4.6 %collective-permute-done.6 = f32[16,1024]{1,0:T(8,128)S(1)} collective-permute-done((f32[16,1024]{1,0:T(8,128)}, f32[16,1024]{1,0:T(8,128)S(1)}, u32[]{:S(2)}, u32[]{:S(2)}) %collective-permute-start.6) | collective-permute-done | bytes 65568 | tf_op jit(solution)/shard_map/ppermute | solution.py:228
  175.0 1.0 multiply_add_fusion.3.start
  176.0 1.0 copy-done.3
  177.0 5.4 %shard_map.77 = (f32[128,16,1024]{2,1,0:T(8,128)}, bf16[128,1024]{1,0:T(8,128)(2,1)S(1)}) custom-call(f32[128,32,128]{2,1,0:T(8,128)S(1)} %broadcast_in_dim.7.kq, f32[128,1024]{1,0:T(8,128)S(1)} %copy-done.3, bf16[128,1024]{1,0:T(8,128)(2,1)S(1)} %copy-done.8, f32[16,1024]{1,0:T(8,128)S(1)} %multiply_add_fusion.3.start), custom_call_target="tpu_custom_call" | custom-call | flops 16777216 | bytes 8912896 | tf_op jit(solution)/shard_map/pallas_call | solution.py:209
  182.4 7.6 %fusion.8 = f32[128,4096]{1,0:T(8,128)} fusion(bf16[128,1024]{1,0:T(8,128)(2,1)S(1)} %get-tuple-element.13, bf16[4096,1024]{1,0:T(8,128)(2,1)} %all-gather.2.cloned.1.call-done), kind=kOutput, calls=%fused_computation.26 | convolution fusion | flops 1073741824 | bytes 10747904 | tf_op jit(solution)/shard_map/dot_general | solution.py:312
  190.0 3.7 %reshape.40 = f32[128,4,1024]{2,1,0:T(4,128)} reshape(f32[128,4096]{1,0:T(8,128)} %fusion.8) | data formatting | bytes 4194304 | tf_op jit(solution)/shard_map/reshape | solution.py:268
  193.7 3.9 %reshape.41 = f32[2,2,128,1024]{3,1,0,2:T(2,128)} reshape(f32[4,128,1024]{2,0,1:T(4,128)} %bitcast.46) | data formatting | bytes 4194304 | tf_op jit(solution)/shard_map/reshape | solution.py:271
  197.6 5.4 %constant_dynamic-slice_fusion.1 = (f32[2,1,128,1024]{3,1,0,2:T(1,128)}, f32[2,1,128,1024]{3,1,0,2:T(1,128)S(1)}) fusion(f32[2,2,128,1024]{3,1,0,2:T(2,128)} %reshape.41, s32[]{:T(128)S(6)} %select_n.31, s32[]{:T(128)S(6)} %select_n.32), kind=kLoop, calls=%fused_computation.21 | loop fusion | bytes 4194312 | tf_op jit(solution)/shard_map/jit(dynamic_index_in_dim)/dynamic_slice | solution.py:273
  202.9 1.3 copy.35
  204.2 5.4 %collective-permute-start.12 = (f32[16,1024]{1,0:T(8,128)S(1)}, f32[16,1024]{1,0:T(8,128)}, u32[]{:S(2)}, u32[]{:S(2)}) collective-permute-start(f32[16,1024]{1,0:T(8,128)S(1)} %get-tuple-element.10), channel_id=1, source_target_pairs={{0,12},{4,16},{8,20},{12,24},{16,28},{1,13},{5,17},{9,21},{13,25},... | collective-permute-start | bytes 196616 | tf_op jit(solution)/shard_map/ppermute | solution.py:228
  209.6 1.9 collective-permute-start.13
  211.5 1.8 copy.17
  213.3 1.8 reshape_reshape.3
  215.1 1.7 copy.37
  216.9 4.2 %all-to-all-start.2 = ((bf16[4,32,1024]{2,1,0:T(8,128)(2,1)}), bf16[4,32,1024]{2,1,0:T(8,128)(2,1)}, u32[]{:S(2)}, u32[]{:S(2)}) async-start(bf16[4,32,1024]{2,1,0:T(8,128)(2,1)} %bitcast.50), calls=%async_computation.2 | async-start | bytes 524288 | tf_op jit(solution)/shard_map/all_to_all | solution.py:331
  221.1 1.0 multiply_add_fusion.start
  222.2 1.0 copy-done.4
  223.2 1.0 copy-done.6
  224.3 11.8 %shard_map.79 = (bf16[128,1024]{1,0:T(8,128)(2,1)}, f32[128,128]{1,0:T(8,128)S(1)}) custom-call(f32[128,32,128]{2,1,0:T(8,128)S(1)} %broadcast_in_dim.7.kq, f32[128,1024]{1,0:T(8,128)S(1)} %copy-done.4, f32[128,1024]{1,0:T(8,128)S(1)} %copy-done.6, bf16[128,1024]{1,0:T(8,128)(2,1)S(1)} %copy-done.8, f32[128,16,1024]{2,1,0:T(8,128)} %get-tuple-element.11.adj_in, ...), custom_call_target="tpu_custom_call" | custom-call | flops 41943040 | bytes 8912896 | tf_op jit(solution)/shard_map/pallas_call | solution.py:209
  236.0 0.1 copy.21
  236.1 0.6 broadcast_in_dim.8
  236.8 3.3 %all-to-all-start.1 = ((bf16[4,128,32]{1,2,0:T(8,128)(2,1)}), bf16[4,128,32]{1,2,0:T(8,128)(2,1)S(1)}, u32[]{:S(2)}, u32[]{:S(2)}) async-start(bf16[4,128,32]{1,2,0:T(8,128)(2,1)} %broadcast_in_dim.8), calls=%async_computation.1 | async-start | bytes 65536 | tf_op jit(solution)/shard_map/all_to_all | solution.py:257
  240.0 0.3 fusion.4
  240.3 0.8 copy.36
  241.2 2.8 %all-to-all-done.1 = bf16[4,128,32]{1,2,0:T(8,128)(2,1)S(1)} async-done(((bf16[4,128,32]{1,2,0:T(8,128)(2,1)}), bf16[4,128,32]{1,2,0:T(8,128)(2,1)S(1)}, u32[]{:S(2)}, u32[]{:S(2)}) %all-to-all-start.1) | async-done | bytes 32800 | tf_op jit(solution)/shard_map/all_to_all | solution.py:257
  243.9 3.5 %all-to-all-start.3 = ((f32[8,32,512]{2,1,0:T(8,128)}), f32[8,32,512]{2,1,0:T(8,128)S(1)}, u32[]{:S(2)}, u32[]{:S(2)}) async-start(f32[8,32,512]{2,1,0:T(8,128)} %bitcast.44), calls=%async_computation.3 | async-start | bytes 1048576 | tf_op jit(solution)/shard_map/all_to_all | solution.py:343
  247.5 1.9 fusion
  249.4 0.1 collective-permute-start.15
  249.5 1.2 convolution_bitcast_fusion
  250.7 11.3 %all-to-all-done.3 = f32[8,32,512]{2,1,0:T(8,128)S(1)} async-done(((f32[8,32,512]{2,1,0:T(8,128)}), f32[8,32,512]{2,1,0:T(8,128)S(1)}, u32[]{:S(2)}, u32[]{:S(2)}) %all-to-all-start.3) | async-done | bytes 524320 | tf_op jit(solution)/shard_map/all_to_all | solution.py:343
  262.0 0.7 reduce_sum.19
  262.7 1.7 fusion.1
  (43 shorter events, 0.2 us)
Async XLA Ops:
  7.2 18.3 %copy-start = (bf16[128,4096]{1,0:T(8,128)(2,1)S(1)}, bf16[128,4096]{1,0:T(8,128)(2,1)}, u32[]{:S(2)}) copy-start(bf16[128,4096]{1,0:T(8,128)(2,1)} %param.5) | copy-start | bytes 3145732
  7.2 134.7 %all-gather.2.cloned.1.call-start = ((), (), s32[]{:S(2)}) async-start(), calls=%async_computation.4 | async-start | bytes 9437184 | tf_op jit(solution)/shard_map/all_gather | solution.py:288
  24.8 0.7 copy-start.9
  26.9 0.8 copy-start.1
  27.7 1.0 copy-start.7
  30.8 117.7 %collective-permute-start.8 = (f32[16,1024]{1,0:T(8,128)S(1)}, f32[16,1024]{1,0:T(8,128)}, u32[]{:S(2)}, u32[]{:S(2)}) collective-permute-start(f32[16,1024]{1,0:T(8,128)S(1)} %get-tuple-element.10), channel_id=1, source_target_pairs={{0,4},{4,8},{8,12},{12,16},{16,20},{20,24},{24,28},{1,5},{5,9},{9,... | collective-permute-start | bytes 196616 | tf_op jit(solution)/shard_map/ppermute | solution.py:228
  34.6 115.2 %collective-permute-start.10 = (f32[16,1024]{1,0:T(8,128)S(1)}, f32[16,1024]{1,0:T(8,128)}, u32[]{:S(2)}, u32[]{:S(2)}) collective-permute-start(f32[16,1024]{1,0:T(8,128)S(1)} %get-tuple-element.10), channel_id=1, source_target_pairs={{0,8},{4,12},{8,16},{12,20},{16,24},{20,28},{1,9},{5,13},{9,17},{1... | collective-permute-start | bytes 196616 | tf_op jit(solution)/shard_map/ppermute | solution.py:228
  36.6 121.2 %collective-permute-start.1 = (f32[16,1024]{1,0:T(8,128)S(1)}, f32[16,1024]{1,0:T(8,128)}, u32[]{:S(2)}, u32[]{:S(2)}) collective-permute-start(f32[16,1024]{1,0:T(8,128)S(1)} %get-tuple-element.10), channel_id=1, source_target_pairs={{4,0},{8,4},{12,8},{16,12},{20,16},{24,20},{28,24},{5,1},{9,5},{13... | collective-permute-start | bytes 196616 | tf_op jit(solution)/shard_map/ppermute | solution.py:228
  37.9 123.3 %collective-permute-start.3 = (f32[16,1024]{1,0:T(8,128)S(1)}, f32[16,1024]{1,0:T(8,128)}, u32[]{:S(2)}, u32[]{:S(2)}) collective-permute-start(f32[16,1024]{1,0:T(8,128)S(1)} %get-tuple-element.10), channel_id=1, source_target_pairs={{8,0},{12,4},{16,8},{20,12},{24,16},{28,20},{9,1},{13,5},{17,9},{2... | collective-permute-start | bytes 196616 | tf_op jit(solution)/shard_map/ppermute | solution.py:228
  39.2 136.8 %copy-start.8 = (bf16[128,1024]{1,0:T(8,128)(2,1)S(1)}, bf16[128,1024]{1,0:T(8,128)(2,1)}, u32[]{:S(2)}) copy-start(bf16[128,1024]{1,0:T(8,128)(2,1)} %cot.5) | copy-start | bytes 786436
  39.2 111.9 %collective-permute-start.4 = (f32[16,1024]{1,0:T(8,128)S(1)}, f32[16,1024]{1,0:T(8,128)}, u32[]{:S(2)}, u32[]{:S(2)}) collective-permute-start(f32[16,1024]{1,0:T(8,128)S(1)} %get-tuple-element.9), channel_id=1, source_target_pairs={{12,0},{16,4},{20,8},{24,12},{28,16},{13,1},{17,5},{21,9},{25,13},... | collective-permute-start | bytes 196616 | tf_op jit(solution)/shard_map/ppermute | solution.py:228
  141.9 4.7 %copy-start.2 = (f32[128,1024]{1,0:T(8,128)S(1)}, f32[128,1024]{1,0:T(8,128)}, u32[]{:S(2)}) copy-start(f32[128,1024]{1,0:T(8,128)} %copy-done.1) | copy-start | bytes 1572868
  146.6 1.9 copy-start.5
  148.5 14.6 %collective-permute-start = (f32[16,1024]{1,0:T(8,128)S(1)}, f32[16,1024]{1,0:T(8,128)S(1)}, u32[]{:S(2)}, u32[]{:S(2)}) collective-permute-start(f32[16,1024]{1,0:T(8,128)S(1)} %get-tuple-element.9), channel_id=1, source_target_pairs={{4,0},{8,4},{12,8},{16,12},{20,16},{24,20},{28,24},{5,1},{9,5},{13... | collective-permute-start | bytes 196616 | tf_op jit(solution)/shard_map/ppermute | solution.py:228
  149.8 14.6 %collective-permute-start.2 = (f32[16,1024]{1,0:T(8,128)S(1)}, f32[16,1024]{1,0:T(8,128)S(1)}, u32[]{:S(2)}, u32[]{:S(2)}) collective-permute-start(f32[16,1024]{1,0:T(8,128)S(1)} %get-tuple-element.9), channel_id=1, source_target_pairs={{8,0},{12,4},{16,8},{20,12},{24,16},{28,20},{9,1},{13,5},{17,9},{2... | collective-permute-start | bytes 196616 | tf_op jit(solution)/shard_map/ppermute | solution.py:228
  151.1 13.4 %collective-permute-start.11 = (f32[16,1024]{1,0:T(8,128)S(1)}, f32[16,1024]{1,0:T(8,128)S(1)}, u32[]{:S(2)}, u32[]{:S(2)}) collective-permute-start(f32[16,1024]{1,0:T(8,128)S(1)} %shard_map.78), channel_id=1, source_target_pairs={{0,12},{4,16},{8,20},{12,24},{16,28},{1,13},{5,17},{9,21},{13,25},... | collective-permute-start | bytes 196616 | tf_op jit(solution)/shard_map/ppermute | solution.py:228
  157.8 6.7 %collective-permute-start.7 = (f32[16,1024]{1,0:T(8,128)S(1)}, f32[16,1024]{1,0:T(8,128)S(1)}, u32[]{:S(2)}, u32[]{:S(2)}) collective-permute-start(f32[16,1024]{1,0:T(8,128)S(1)} %shard_map.78), channel_id=1, source_target_pairs={{0,4},{4,8},{8,12},{12,16},{16,20},{20,24},{24,28},{1,5},{5,9},{9,... | collective-permute-start | bytes 196616 | tf_op jit(solution)/shard_map/ppermute | solution.py:228
  161.2 3.9 %collective-permute-start.9 = (f32[16,1024]{1,0:T(8,128)S(1)}, f32[16,1024]{1,0:T(8,128)S(1)}, u32[]{:S(2)}, u32[]{:S(2)}) collective-permute-start(f32[16,1024]{1,0:T(8,128)S(1)} %shard_map.78), channel_id=1, source_target_pairs={{0,8},{4,12},{8,16},{12,20},{16,24},{20,28},{1,9},{5,13},{9,17},{1... | collective-permute-start | bytes 196616 | tf_op jit(solution)/shard_map/ppermute | solution.py:228
  163.1 4.9 %copy-start.14 = (f32[16,1024]{1,0:T(8,128)}, f32[16,1024]{1,0:T(8,128)S(1)}, u32[]{:S(2)}) copy-start(f32[16,1024]{1,0:T(8,128)S(1)} %collective-permute-done) | copy-start | bytes 196612
  163.2 7.2 %collective-permute-start.5 = (f32[16,1024]{1,0:T(8,128)S(1)}, f32[16,1024]{1,0:T(8,128)}, u32[]{:S(2)}, u32[]{:S(2)}) collective-permute-start(f32[16,1024]{1,0:T(8,128)S(1)} %get-tuple-element.10), channel_id=1, source_target_pairs={{12,0},{16,4},{20,8},{24,12},{28,16},{13,1},{17,5},{21,9},{25,13},... | collective-permute-start | bytes 196616 | tf_op jit(solution)/shard_map/ppermute | solution.py:228
  164.5 3.6 %copy-start.15 = (f32[16,1024]{1,0:T(8,128)}, f32[16,1024]{1,0:T(8,128)S(1)}, u32[]{:S(2)}) copy-start(f32[16,1024]{1,0:T(8,128)S(1)} %collective-permute-done.2) | copy-start | bytes 196612
  164.5 2.2 copy-start.10
  164.5 2.2 copy-start.12
  165.0 3.0 %copy-start.13 = (f32[16,1024]{1,0:T(8,128)}, f32[16,1024]{1,0:T(8,128)S(1)}, u32[]{:S(2)}) copy-start(f32[16,1024]{1,0:T(8,128)S(1)} %collective-permute-done.9) | copy-start | bytes 196612
  166.7 8.2 %collective-permute-start.6 = (f32[16,1024]{1,0:T(8,128)}, f32[16,1024]{1,0:T(8,128)S(1)}, u32[]{:S(2)}, u32[]{:S(2)}) collective-permute-start(f32[16,1024]{1,0:T(8,128)} %get-tuple-element.18), channel_id=1, source_target_pairs={{16,0},{20,4},{24,8},{28,12},{17,1},{21,5},{25,9},{29,13},{18,2},{... | collective-permute-start | bytes 196616 | tf_op jit(solution)/shard_map/ppermute | solution.py:228
  176.0 1.0 copy-start.3
  190.0 31.1 %copy-start.11 = (f32[16,1024]{1,0:T(8,128)S(1)}, f32[16,1024]{1,0:T(8,128)}, u32[]{:S(2)}) copy-start(f32[16,1024]{1,0:T(8,128)} %copy-done.10) | copy-start | bytes 196612
  204.2 43.2 %collective-permute-start.14 = (f32[2,128,1024]{2,1,0:T(8,128)}, f32[2,128,1024]{2,1,0:T(8,128)}, u32[]{:S(2)}, u32[]{:S(2)}) collective-permute-start(f32[2,128,1024]{2,1,0:T(8,128)} %bitcast.42), channel_id=1, source_target_pairs={{0,1},{1,0},{2,3},{3,2},{4,5},{5,4},{6,7},{7,6},{8,9},{9,8},{10,11... | collective-permute-start | bytes 3145736 | tf_op jit(solution)/shard_map/ppermute | solution.py:277
  204.2 16.9 %collective-permute-start.12 = (f32[16,1024]{1,0:T(8,128)S(1)}, f32[16,1024]{1,0:T(8,128)}, u32[]{:S(2)}, u32[]{:S(2)}) collective-permute-start(f32[16,1024]{1,0:T(8,128)S(1)} %get-tuple-element.10), channel_id=1, source_target_pairs={{0,12},{4,16},{8,20},{12,24},{16,28},{1,13},{5,17},{9,21},{13,25},... | collective-permute-start | bytes 196616 | tf_op jit(solution)/shard_map/ppermute | solution.py:228
  209.6 11.5 %collective-permute-start.13 = (f32[16,1024]{1,0:T(8,128)}, f32[16,1024]{1,0:T(8,128)}, u32[]{:S(2)}, u32[]{:S(2)}) collective-permute-start(f32[16,1024]{1,0:T(8,128)} %get-tuple-element.17), channel_id=1, source_target_pairs={{0,16},{4,20},{8,24},{12,28},{1,17},{5,21},{9,25},{13,29},{2,18},{... | collective-permute-start | bytes 196616 | tf_op jit(solution)/shard_map/ppermute | solution.py:228
  216.9 19.2 %all-to-all-start.2 = ((bf16[4,32,1024]{2,1,0:T(8,128)(2,1)}), bf16[4,32,1024]{2,1,0:T(8,128)(2,1)}, u32[]{:S(2)}, u32[]{:S(2)}) async-start(bf16[4,32,1024]{2,1,0:T(8,128)(2,1)} %bitcast.50), calls=%async_computation.2 | async-start | bytes 524288 | tf_op jit(solution)/shard_map/all_to_all | solution.py:331
  222.2 1.0 copy-start.4
  223.2 1.0 copy-start.6
  236.8 7.2 %all-to-all-start.1 = ((bf16[4,128,32]{1,2,0:T(8,128)(2,1)}), bf16[4,128,32]{1,2,0:T(8,128)(2,1)S(1)}, u32[]{:S(2)}, u32[]{:S(2)}) async-start(bf16[4,128,32]{1,2,0:T(8,128)(2,1)} %broadcast_in_dim.8), calls=%async_computation.1 | async-start | bytes 65536 | tf_op jit(solution)/shard_map/all_to_all | solution.py:257
  243.9 18.1 %all-to-all-start.3 = ((f32[8,32,512]{2,1,0:T(8,128)}), f32[8,32,512]{2,1,0:T(8,128)S(1)}, u32[]{:S(2)}, u32[]{:S(2)}) async-start(f32[8,32,512]{2,1,0:T(8,128)} %bitcast.44), calls=%async_computation.3 | async-start | bytes 1048576 | tf_op jit(solution)/shard_map/all_to_all | solution.py:343
  249.4 13.2 %collective-permute-start.15 = (bf16[1,128,1024]{2,1,0:T(8,128)(2,1)S(1)}, bf16[1,128,1024]{2,1,0:T(8,128)(2,1)}, u32[]{:S(2)}, u32[]{:S(2)}) collective-permute-start(bf16[1,128,1024]{2,1,0:T(8,128)(2,1)S(1)} %dynamic-slice_convert_fusion), channel_id=1, source_target_pairs={{0,2},{1,3},{2,0},{3,1},{4,6},{5,7},{6,4},{7,5},{8,10},{9,11},{10,... | collective-permute-start | bytes 786440 | tf_op jit(solution)/shard_map/ppermute | solution.py:277
Sparse Core Ops, SparseCore 0:
  10.1 131.6 all-gather.1

commit v2 on v1

--- a/solution.py
+++ b/solution.py
@@ -31,7 +31,7 @@
     dst[...] = src[...].astype(F32)
 
 
-def adjoint_totals_kernel(kq, eps, cot, lam_out, decay_out, cot_f):
+def adjoint_totals_kernel(kq, eps, cot, pair_out, cot_f):
     tokens, width = eps.shape
     groups = lane_groups(width)
     to_float(cot, cot_f)
@@ -58,8 +58,8 @@
     ones = tuple(jnp.ones((NS, LANES), F32) for _ in groups)
     lams, decays = lax.fori_loop(0, tokens // UNROLL, block, (zeros, ones))
     for lam, total, cols in zip(lams, decays, groups):
-        lam_out[:, cols] = lam
-        decay_out[:, cols] = total
+        pair_out[:NS, cols] = lam
+        pair_out[NS:, cols] = total
 
 
 def adjoint_kernel(kq, eps, cot, start, adj_out, grad_out, cot_f, grad_f):
@@ -193,6 +193,7 @@
             "rows": pl.BlockSpec((tokens, block), lambda c: (0, c)),
             "rows16": pl.BlockSpec((tokens, block), lambda c: (0, c)),
             "state": pl.BlockSpec((NS, block), lambda c: (0, c)),
+            "pair": pl.BlockSpec((2 * NS, block), lambda c: (0, c)),
             "states": pl.BlockSpec((tokens, NS, block), lambda c: (0, 0, c)),
             "gkq": pl.BlockSpec((tokens, LANES), lambda c: (0, 0)),
         }[kind]
@@ -202,6 +203,7 @@
             "rows": jax.ShapeDtypeStruct((tokens, width), F32),
             "rows16": jax.ShapeDtypeStruct((tokens, width), BF16),
             "state": jax.ShapeDtypeStruct((NS, width), F32),
+            "pair": jax.ShapeDtypeStruct((2 * NS, width), F32),
             "states": jax.ShapeDtypeStruct((tokens, NS, width), F32),
             "gkq": jax.ShapeDtypeStruct((tokens, LANES), F32),
         }[kind]
@@ -228,18 +230,22 @@
     return lax.ppermute(value, axis, pairs)
 
 
-def carried(decay, total, sign):
+def carried(decay, total, sign, together):
     count = lax.axis_size("seq")
     window, radix = 1, 4
     inc_decay, inc_total = decay, total
     exc_decay, exc_total = None, None
     while window < count:
         last = window * radix >= count
-        for j in range(1, radix):
-            if window * j >= count:
-                break
-            far_total = shifted(inc_total, "seq", sign * window * j)
-            far_decay = shifted(inc_decay, "seq", sign * window * j)
+        joint = together and not last
+        pair = jnp.concatenate([inc_total, inc_decay], axis=0) if joint else None
+        for j in range(1, min(radix, -(-count // window))):
+            by = sign * window * j
+            if joint:
+                far = shifted(pair, "seq", by)
+                far_total, far_decay = far[:NS], far[NS:]
+            else:
+                far_total, far_decay = shifted(inc_total, "seq", by), shifted(inc_decay, "seq", by)
             if exc_total is None:
                 exc_total, exc_decay = far_total, far_decay
             else:
@@ -279,17 +285,111 @@
     return blocks[0]
 
 
+class Gathered:
+    def __init__(self, tokens, w_inner):
+        self.tokens = tokens
+        self.full = lax.all_gather(w_inner, "seq", axis=0, tiled=True)
+
+    def inner(self):
+        return jnp.dot(self.tokens, self.full, preferred_element_type=F32)
+
+    def grad_tokens(self, grad):
+        return scatter_sum_columns(dot_t(grad, self.full))
+
+
+class Exchanged:
+    def __init__(self, tokens, w_inner):
+        self.depth, self.width = w_inner.shape
+        self.count = tokens.shape[0]
+        seqs = lax.axis_size("seq")
+        self.rows = seqs // 2
+        index = lax.axis_index("seq")
+        self.row, self.side = index // 2, index % 2
+        self.first = lax.axis_index("chan") % 2 == 0
+        self.w_mine = w_inner
+        self.w_other = lax.ppermute(w_inner, "seq", [(i, i ^ 1) for i in range(seqs)])
+        half = jnp.where(self.first, self.side, 1 - self.side)
+        came = [
+            self.move(self.columns(tokens, (self.row + j) % self.rows, half), j)
+            for j in range(1, self.rows)
+        ]
+        came = jnp.concatenate(came, axis=0)
+        partner = self.swap(came)
+        self.far_mine = jnp.where(self.first, came, partner)
+        self.far_other = jnp.where(self.first, partner, came)
+        self.near_mine = self.columns(tokens, self.row, self.side)
+        self.near_other = self.columns(tokens, self.row, 1 - self.side)
+
+    def columns(self, tokens, row, side):
+        return lax.dynamic_slice_in_dim(tokens, (row * 2 + side) * self.depth, self.depth, 1)
+
+    def move(self, value, by):
+        pairs = [
+            (r * 2 + s, (r + by) % self.rows * 2 + s) for r in range(self.rows) for s in range(2)
+        ]
+        return lax.ppermute(value, "seq", pairs)
+
+    def swap(self, value):
+        chans = lax.axis_size("chan")
+        return lax.ppermute(value, "chan", [(i, i ^ 1) for i in range(chans)])
+
+    def inner(self):
+        def product(mine, other):
+            return jnp.dot(mine, self.w_mine, preferred_element_type=F32) + jnp.dot(
+                other, self.w_other, preferred_element_type=F32
+            )
+
+        far = product(self.far_mine, self.far_other).astype(BF16)
+        total = product(self.near_mine, self.near_other)
+        for j in range(1, self.rows):
+            block = far[(j - 1) * self.count : j * self.count]
+            total = total + self.move(block, -j).astype(F32)
+        return total
+
+    def grad_tokens(self, grad):
+        chans = lax.axis_size("chan")
+        pairs = chans // 2
+        blocks = [grad] + [self.move(grad, j) for j in range(1, self.rows)]
+        even = jnp.concatenate(blocks[0::2], axis=0)
+        odd = jnp.concatenate(blocks[1::2], axis=0)
+        keep = jnp.where(self.first, even, odd)
+        give = jnp.where(self.first, odd, even)
+        one, two = self.w_mine, self.w_other
+        full = jnp.concatenate(
+            [jnp.where(self.side == 0, one, two), jnp.where(self.side == 0, two, one)], axis=0
+        )
+        kept = dot_t(keep, full) + self.swap(dot_t(give, full))
+        pieces = kept.astype(BF16).reshape(pairs, self.count, -1)
+        y = lax.axis_index("chan") // 2
+        total = None
+        for m in range(pairs):
+            piece = lax.dynamic_index_in_dim(pieces, (y + m) % pairs, 0, keepdims=False)
+            route = []
+            for r in range(self.rows):
+                for s in range(2):
+                    for c in range(chans):
+                        p = (c // 2 + m) % pairs
+                        to = (r - c % 2 - 2 * p) % self.rows
+                        route.append(((r * 2 + s) * chans + c, (to * 2 + s) * chans + r))
+            piece = lax.ppermute(piece, ("seq", "chan"), route).astype(F32)
+            total = piece if total is None else total + piece
+        return total
+
+
+def dot_t(left, right):
+    return lax.dot_general(left, right, (((1,), (1,)), ((), ())), preferred_element_type=F32)
+
+
 def per_device(tokens, w_inner, w_keyquery, rate, grad_out):
     count = tokens.shape[0]
     width = w_inner.shape[1]
     kq_cols = w_keyquery.shape[1] * w_keyquery.shape[2]
     seqs, chans = lax.axis_size("seq"), lax.axis_size("chan")
     block = min(width, 512)
-    full_inner = lax.all_gather(w_inner, "seq", axis=0, tiled=True)
+    short = seqs == 2 * chans and chans % 2 == 0 and count * seqs <= w_inner.shape[0] * seqs
+    plan = (Exchanged if short else Gathered)(tokens, w_inner)
     full_kq = gather_columns(w_keyquery.reshape(-1, kq_cols).T, "seq")
-    keyquery = lax.dot_general(
-        tokens, full_kq, (((1,), (1,)), ((), ())), preferred_element_type=F32
-    )
+    keyquery = dot_t(tokens, full_kq)
     keys = keyquery[:, :NS]
     sumsq = jnp.sum(keys * keys, axis=1)
     eps = rate[None, :] / (1.0 + rate[None, :] * sumsq[:, None])
@@ -297,28 +397,26 @@
     rows_f = pltpu.VMEM((count, block), F32)
     run = functools.partial(call, tokens=count, width=width, block=block)
 
-    lam, decay = run(
+    (pair,) = run(
         adjoint_totals_kernel,
-        ins=["kq", "rows", "rows16"], outs=["state", "state"], scratch=[rows_f],
+        ins=["kq", "rows", "rows16"], outs=["pair"], scratch=[rows_f],
         args=(spread, eps, grad_out), flops=8,
     )
-    end_adjoint = carried(decay, lam, -1)
+    lam, decay = pair[:NS], pair[NS:]
+    end_adjoint = carried(decay, lam, -1, True)
     adjoints, inner_grad = run(
         adjoint_kernel,
         ins=["kq", "rows", "rows16", "state"], outs=["states", "rows16"], scratch=[rows_f, rows_f],
         args=(spread, eps, grad_out, end_adjoint), flops=8,
     )
-    inner = jnp.dot(tokens, full_inner, preferred_element_type=F32)
-    partial_sum = lax.dot_general(
-        inner_grad, full_inner, (((1,), (1,)), ((), ())), preferred_element_type=F32
-    )
-    tokens_sum = scatter_sum_columns(partial_sum)
+    inner = plan.inner()
     (alone_end,) = run(
         state_total_kernel,
         ins=["kq", "rows", "rows"], outs=["state"], scratch=[],
         args=(spread, eps, inner), flops=6,
     )
-    start_state = carried(decay, alone_end, 1)
+    start_state = carried(decay, alone_end, 1, False)
+    tokens_sum = plan.grad_tokens(inner_grad)
     acc = pltpu.VMEM((count, NS, LANES), F32)
     mixed, kq_grad = run(
         mixer_kernel,
@@ -341,9 +439,9 @@
         kq_grad, tokens, (((0,), (0,)), ((), ())), preferred_element_type=F32
     )
     grad_parts = lax.all_to_all(
-        jnp.moveaxis(grad_cols.reshape(kq_cols, seqs, -1), 1, 0), "seq", 0, 0, tiled=True
-    )
-    grad_keyquery = jnp.sum(grad_parts, axis=0).T.reshape(w_keyquery.shape)
+        jnp.moveaxis(grad_cols.astype(BF16).reshape(kq_cols, seqs, -1), 1, 0), "seq", 0, 0, tiled=True
+    )
+    grad_keyquery = jnp.sum(grad_parts.astype(F32), axis=0).T.reshape(w_keyquery.shape)
     return (mixed, grad_tokens, grad_keyquery)
 
 

time: 273 us -> 182 us (0.67)
  the two profiles are of different devices: /device:TPU:0 before, /device:TPU:17 now
where the time goes in v2:
time: 182 us; the launch traced here: 180 us
  starting transfers between devices  71.1 us (39%)
  waiting for transfers between devices  52.8 us (29%)
  Pallas kernels  21.1 us (12%)
  local copies, waits for them, and re-layouts  16.4 us (9%)
  matrix products  13.2 us (7%)
  other arithmetic  4.45 us (2%)
    ppermute x9, waiting for transfers between devices, move(): return lax.ppermute(value, 'seq', pairs)  33.6 us
    ppermute x11, starting transfers between devices, shifted(): return lax.ppermute(value, axis, pairs)  28.7 us
    pallas_call x4, Pallas kernels, call(): pl.pallas_call(kernel, grid=(width // block,), in_specs=[spec(kind) for k...  21.1 us
    ppermute x2, waiting for transfers between devices, grad_tokens(): piece = lax.ppermute(piece, ('seq', 'chan'), route).astype(F32)  11.6 us
    ppermute x9, starting transfers between devices, move(): return lax.ppermute(value, 'seq', pairs)  10.1 us
    all_to_all x2, starting transfers between devices, gather_columns(): lax.all_to_all(jnp.broadcast_to(value[None], (count,) + value.shape), axi...  9.08 us
    all_to_all x1, starting transfers between devices, per_device(): lax.all_to_all(jnp.moveaxis(grad_cols.astype(BF16).reshape(kq_cols, seqs,...  7.15 us
    ppermute x2, starting transfers between devices, grad_tokens(): piece = lax.ppermute(piece, ('seq', 'chan'), route).astype(F32)  5.58 us
  transfers between devices with their start and end apart: 29, of which 14 were waited for; matrix products, arithmetic and copies ran while one was open for 14% of the time, Pallas kernels for 9%

profile of v2, /device:TPU:17, one launch (start us, length us, event | category | flops | bytes accessed | tf_op | source)
XLA Modules:
  0.0 180.3 jit_solution(3189718763197401404)
XLA Ops:
  0.7 1.3 collective-permute-start
  1.9 1.8 constant_dynamic-slice_fusion
  3.7 1.3 collective-permute-start.1
  5.1 1.5 broadcast_in_dim.6
  6.5 5.6 %all-to-all-start = ((bf16[8,32,512]{2,1,0:T(8,128)(2,1)}), bf16[8,32,512]{2,1,0:T(8,128)(2,1)S(1)}, u32[]{:S(2)}, u32[]{:S(2)}) async-start(bf16[8,32,512]{2,1,0:T(8,128)(2,1)} %broadcast_in_dim.6), calls=%async_computation | async-start | bytes 524288 | tf_op jit(solution)/shard_map/all_to_all | solution.py:263
  12.5 1.6 constant_dynamic-update-slice_fusion.2
  14.7 7.0 %collective-permute-done.3 = bf16[128,512]{1,0:T(8,128)(2,1)} collective-permute-done((bf16[128,512]{1,0:T(8,128)(2,1)}, bf16[128,512]{1,0:T(8,128)(2,1)}, u32[]{:S(2)}, u32[]{:S(2)}) %collective-permute-start.3) | collective-permute-done | bytes 131104 | tf_op jit(solution)/shard_map/ppermute | solution.py:330
  21.7 1.6 constant_dynamic-update-slice_fusion
  23.3 1.1 collective-permute-start.4
  24.4 1.1 fusion.15
  25.5 2.3 %all-to-all-done = bf16[8,32,512]{2,1,0:T(8,128)(2,1)S(1)} async-done(((bf16[8,32,512]{2,1,0:T(8,128)(2,1)}), bf16[8,32,512]{2,1,0:T(8,128)(2,1)S(1)}, u32[]{:S(2)}, u32[]{:S(2)}) %all-to-all-start) | async-done | bytes 262176 | tf_op jit(solution)/shard_map/all_to_all | solution.py:263
  28.3 1.9 %fusion.9 = f32[384,1024]{1,0:T(8,128)S(1)} fusion(bf16[512,1024]{1,0:T(8,128)(2,1)S(1)} %collective-permute-done, bf16[384,512]{1,0:T(8,128)(2,1)} %collective-permute-done.4, bf16[384,512]{1,0:T(8,128)(2,1)} %constant_dynamic-update-slice_fusion, pred[]{:T(512)S(6)} %eq.15), kind=kOutput, calls=%fused_computation.20 | convolution fusion | flops 402849792 | bytes 3407873 | tf_op jit(solution)/shard_map/dot_general | solution.py:338
  30.2 1.6 add_convert_fusion
  31.8 0.9 fusion.28
  32.7 1.3 collective-permute-start.7
  34.1 1.1 collective-permute-start.5
  36.1 2.1 %shard_map.76 = f32[32,1024]{1,0:T(8,128)S(1)} custom-call(f32[128,32,128]{2,1,0:T(8,128)S(1)} %broadcast_in_dim.7.kq, f32[128,1024]{1,0:T(8,128)S(1)} %add_divide_fusion.eps, bf16[128,1024]{1,0:T(8,128)(2,1)S(1)} %copy-done), custom_call_target="tpu_custom_call" | custom-call | flops 16777216 | bytes 524288 | tf_op jit(solution)/shard_map/pallas_call | solution.py:211
  38.2 5.1 %collective-permute-start.10 = (f32[32,1024]{1,0:T(8,128)S(1)}, f32[32,1024]{1,0:T(8,128)S(1)}, u32[]{:S(2)}, u32[]{:S(2)}) collective-permute-start(f32[32,1024]{1,0:T(8,128)S(1)} %shard_map.76), channel_id=1, source_target_pairs={{12,0},{16,4},{20,8},{24,12},{28,16},{13,1},{17,5},{21,9},{25,13},... | collective-permute-start | bytes 393224 | tf_op jit(solution)/shard_map/ppermute | solution.py:230
  43.3 1.9 %collective-permute-start.9 = (f32[32,1024]{1,0:T(8,128)S(1)}, f32[32,1024]{1,0:T(8,128)S(1)}, u32[]{:S(2)}, u32[]{:S(2)}) collective-permute-start(f32[32,1024]{1,0:T(8,128)S(1)} %shard_map.76), channel_id=1, source_target_pairs={{8,0},{12,4},{16,8},{20,12},{24,16},{28,20},{9,1},{13,5},{17,9},{2... | collective-permute-start | bytes 393224 | tf_op jit(solution)/shard_map/ppermute | solution.py:230
  45.9 2.2 %collective-permute-start.8 = (f32[32,1024]{1,0:T(8,128)S(1)}, f32[32,1024]{1,0:T(8,128)S(1)}, u32[]{:S(2)}, u32[]{:S(2)}) collective-permute-start(f32[32,1024]{1,0:T(8,128)S(1)} %shard_map.76), channel_id=1, source_target_pairs={{4,0},{8,4},{12,8},{16,12},{20,16},{24,20},{28,24},{5,1},{9,5},{13... | collective-permute-start | bytes 393224 | tf_op jit(solution)/shard_map/ppermute | solution.py:230
  48.0 4.6 %collective-permute-done.6 = bf16[128,1024]{1,0:T(8,128)(2,1)S(1)} collective-permute-done((bf16[128,1024]{1,0:T(8,128)(2,1)}, bf16[128,1024]{1,0:T(8,128)(2,1)S(1)}, u32[]{:S(2)}, u32[]{:S(2)}) %collective-permute-start.6) | collective-permute-done | bytes 262176 | tf_op jit(solution)/shard_map/ppermute | solution.py:330
  52.6 1.9 %collective-permute-start.13 = (f32[16,1024]{1,0:T(8,128)}, f32[16,1024]{1,0:T(8,128)S(1)}, u32[]{:S(2)}, u32[]{:S(2)}) collective-permute-start(f32[16,1024]{1,0:T(8,128)} %slice.65), channel_id=1, source_target_pairs={{0,4},{4,8},{8,12},{12,16},{16,20},{20,24},{24,28},{1,5},{5,9},{9,... | collective-permute-start | bytes 196616 | tf_op jit(solution)/shard_map/ppermute | solution.py:230
  54.5 5.3 %collective-permute-done.5 = bf16[128,1024]{1,0:T(8,128)(2,1)} collective-permute-done((bf16[128,1024]{1,0:T(8,128)(2,1)}, bf16[128,1024]{1,0:T(8,128)(2,1)}, u32[]{:S(2)}, u32[]{:S(2)}) %collective-permute-start.5) | collective-permute-done | bytes 262176 | tf_op jit(solution)/shard_map/ppermute | solution.py:330
  59.9 2.4 %collective-permute-start.15 = (f32[16,1024]{1,0:T(8,128)}, f32[16,1024]{1,0:T(8,128)S(1)}, u32[]{:S(2)}, u32[]{:S(2)}) collective-permute-start(f32[16,1024]{1,0:T(8,128)} %slice.65), channel_id=1, source_target_pairs={{0,8},{4,12},{8,16},{12,20},{16,24},{20,28},{1,9},{5,13},{9,17},{1... | collective-permute-start | bytes 196616 | tf_op jit(solution)/shard_map/ppermute | solution.py:230
  62.3 1.5 fusion.4.inner
  63.9 1.9 %shard_map.78 = f32[16,1024]{1,0:T(8,128)S(1)} custom-call(f32[128,32,128]{2,1,0:T(8,128)S(1)} %broadcast_in_dim.7.kq, f32[128,1024]{1,0:T(8,128)S(1)} %add_divide_fusion.eps, f32[128,1024]{1,0:T(8,128)S(1)} %fusion.4.inner), custom_call_target="tpu_custom_call" | custom-call | flops 12582912 | bytes 524288 | tf_op jit(solution)/shard_map/pallas_call | solution.py:211
  65.8 1.9 %collective-permute-start.16 = (f32[16,1024]{1,0:T(8,128)S(1)}, f32[16,1024]{1,0:T(8,128)S(1)}, u32[]{:S(2)}, u32[]{:S(2)}) collective-permute-start(f32[16,1024]{1,0:T(8,128)S(1)} %shard_map.78), channel_id=1, source_target_pairs={{0,12},{4,16},{8,20},{12,24},{16,28},{1,13},{5,17},{9,21},{13,25},... | collective-permute-start | bytes 196616 | tf_op jit(solution)/shard_map/ppermute | solution.py:230
  67.7 1.9 %collective-permute-start.12 = (f32[16,1024]{1,0:T(8,128)S(1)}, f32[16,1024]{1,0:T(8,128)S(1)}, u32[]{:S(2)}, u32[]{:S(2)}) collective-permute-start(f32[16,1024]{1,0:T(8,128)S(1)} %shard_map.78), channel_id=1, source_target_pairs={{0,4},{4,8},{8,12},{12,16},{16,20},{20,24},{24,28},{1,5},{5,9},{9,... | collective-permute-start | bytes 196616 | tf_op jit(solution)/shard_map/ppermute | solution.py:230
  69.7 1.9 %collective-permute-start.14 = (f32[16,1024]{1,0:T(8,128)S(1)}, f32[16,1024]{1,0:T(8,128)S(1)}, u32[]{:S(2)}, u32[]{:S(2)}) collective-permute-start(f32[16,1024]{1,0:T(8,128)S(1)} %shard_map.78), channel_id=1, source_target_pairs={{0,8},{4,12},{8,16},{12,20},{16,24},{20,28},{1,9},{5,13},{9,17},{1... | collective-permute-start | bytes 196616 | tf_op jit(solution)/shard_map/ppermute | solution.py:230
  71.6 0.9 collective-permute-done.16
  72.6 1.5 collective-permute-done.12
  74.1 0.9 collective-permute-done.14
  75.0 0.7 slice_add_fusion
  75.7 3.4 %collective-permute-start.11 = (f32[16,1024]{1,0:T(8,128)}, f32[16,1024]{1,0:T(8,128)}, u32[]{:S(2)}, u32[]{:S(2)}) collective-permute-start(f32[16,1024]{1,0:T(8,128)} %get-tuple-element.11), channel_id=1, source_target_pairs={{16,0},{20,4},{24,8},{28,12},{17,1},{21,5},{25,9},{29,13},{18,2},{... | collective-permute-start | bytes 196616 | tf_op jit(solution)/shard_map/ppermute | solution.py:230
  79.1 1.0 collective-permute-done.11
  80.1 1.0 fusion.18.start
  81.1 5.4 %shard_map.77 = (f32[128,16,1024]{2,1,0:T(8,128)}, bf16[128,1024]{1,0:T(8,128)(2,1)S(1)}) custom-call(f32[128,32,128]{2,1,0:T(8,128)S(1)} %broadcast_in_dim.7.kq, f32[128,1024]{1,0:T(8,128)S(1)} %add_divide_fusion.eps, bf16[128,1024]{1,0:T(8,128)(2,1)S(1)} %copy-done, f32[16,1024]{1,0:T(8,128)S(1)} %fusion.18.start), custom_call_target="tpu_custom_call" | custom-call | flops 16777216 | bytes 8912896 | tf_op jit(solution)/shard_map/pallas_call | solution.py:211
  86.5 1.8 collective-permute-start.20
  88.3 1.5 collective-permute-start.21
  89.9 2.7 %collective-permute-start.19 = (bf16[128,1024]{1,0:T(8,128)(2,1)S(1)}, bf16[128,1024]{1,0:T(8,128)(2,1)S(1)}, u32[]{:S(2)}, u32[]{:S(2)}) collective-permute-start(bf16[128,1024]{1,0:T(8,128)(2,1)S(1)} %get-tuple-element.9), channel_id=1, source_target_pairs={{0,16},{4,20},{8,24},{12,28},{16,0},{20,4},{24,8},{28,12},{1,17},{... | collective-permute-start | bytes 786440 | tf_op jit(solution)/shard_map/ppermute | solution.py:330
  92.7 0.8 collective-permute-done.20
  93.5 3.4 %collective-permute-done.21 = bf16[128,1024]{1,0:T(8,128)(2,1)S(1)} collective-permute-done((bf16[128,1024]{1,0:T(8,128)(2,1)S(1)}, bf16[128,1024]{1,0:T(8,128)(2,1)S(1)}, u32[]{:S(2)}, u32[]{:S(2)}) %collective-permute-start.21) | collective-permute-done | bytes 262176 | tf_op jit(solution)/shard_map/ppermute | solution.py:330
  97.0 12.4 %collective-permute-done.19 = bf16[128,1024]{1,0:T(8,128)(2,1)S(1)} collective-permute-done((bf16[128,1024]{1,0:T(8,128)(2,1)S(1)}, bf16[128,1024]{1,0:T(8,128)(2,1)S(1)}, u32[]{:S(2)}, u32[]{:S(2)}) %collective-permute-start.19) | collective-permute-done | bytes 262176 | tf_op jit(solution)/shard_map/ppermute | solution.py:330
  109.5 1.8 %fusion = f32[256,1024]{1,0:T(8,128)} fusion(bf16[512,1024]{1,0:T(8,128)(2,1)S(1)} %get-tuple-element.14, bf16[512,1024]{1,0:T(8,128)(2,1)S(1)} %get-tuple-element.13, bf16[256,1024]{1,0:T(8,128)(2,1)S(1)} %constant_dynamic-update-slice_fusion.5, bf16[256,1024]{1,0:T(8,128)(2,1)S(1)} %constant_dynamic-update-slice_fusion.3, pred[]{:T(512)S(6)} %eq.15), kind=kOutput, calls=%fused_computation.4 | convolution fusion | flops 541327360 | bytes 4194305 | tf_op jit(solution)/shard_map/dot_general | solution.py:380
  111.3 3.8 %collective-permute-start.22 = (f32[256,1024]{1,0:T(8,128)}, f32[256,1024]{1,0:T(8,128)}, u32[]{:S(2)}, u32[]{:S(2)}) collective-permute-start(f32[256,1024]{1,0:T(8,128)} %fusion), channel_id=1, source_target_pairs={{0,1},{1,0},{2,3},{3,2},{4,5},{5,4},{6,7},{7,6},{8,9},{9,8},{10,11... | collective-permute-start | bytes 3145736 | tf_op jit(solution)/shard_map/ppermute | solution.py:334
  115.1 4.8 %collective-permute-start.17 = (f32[16,1024]{1,0:T(8,128)}, f32[16,1024]{1,0:T(8,128)}, u32[]{:S(2)}, u32[]{:S(2)}) collective-permute-start(f32[16,1024]{1,0:T(8,128)} %slice.65), channel_id=1, source_target_pairs={{0,12},{4,16},{8,20},{12,24},{16,28},{1,13},{5,17},{9,21},{13,25},... | collective-permute-start | bytes 196616 | tf_op jit(solution)/shard_map/ppermute | solution.py:230
  119.9 1.3 collective-permute-start.18
  121.2 1.8 copy.13
  123.0 1.8 %reshape_reshape.3 = bf16[32,4,1024]{2,1,0:T(4,128)(2,1)} reshape(bf16[32,8,512]{2,1,0:T(8,128)(2,1)} %copy.13) | data formatting | bytes 524288 | tf_op jit(solution)/shard_map/reshape;reshape | solution.py:430
  124.9 1.7 copy.24
  126.6 4.3 %all-to-all-start.2 = ((bf16[4,32,1024]{2,1,0:T(8,128)(2,1)}), bf16[4,32,1024]{2,1,0:T(8,128)(2,1)}, u32[]{:S(2)}, u32[]{:S(2)}) async-start(bf16[4,32,1024]{2,1,0:T(8,128)(2,1)} %bitcast.39), calls=%async_computation.2 | async-start | bytes 524288 | tf_op jit(solution)/shard_map/all_to_all | solution.py:429
  130.9 1.0 multiply_add_fusion.start
  131.9 11.8 %shard_map.79 = (bf16[128,1024]{1,0:T(8,128)(2,1)}, f32[128,128]{1,0:T(8,128)S(1)}) custom-call(f32[128,32,128]{2,1,0:T(8,128)S(1)} %broadcast_in_dim.7.kq, f32[128,1024]{1,0:T(8,128)S(1)} %add_divide_fusion.eps, f32[128,1024]{1,0:T(8,128)S(1)} %fusion.4.inner, bf16[128,1024]{1,0:T(8,128)(2,1)S(1)} %copy-done, f32[128,16,1024]{2,1,0:T(8,128)} %get-tuple-element.7.adj_in, ...), custom_call_target="tpu_custom_call" | custom-call | flops 41943040 | bytes 8912896 | tf_op jit(solution)/shard_map/pallas_call | solution.py:211
  144.4 3.4 %all-to-all-start.1 = ((bf16[4,128,32]{1,2,0:T(8,128)(2,1)}), bf16[4,128,32]{1,2,0:T(8,128)(2,1)S(1)}, u32[]{:S(2)}, u32[]{:S(2)}) async-start(bf16[4,128,32]{1,2,0:T(8,128)(2,1)} %broadcast_in_dim.8), calls=%async_computation.1 | async-start | bytes 65536 | tf_op jit(solution)/shard_map/all_to_all | solution.py:263
  147.9 1.5 convolution_convert_fusion
  150.1 0.9 all-to-all-done.1
  151.1 7.2 %all-to-all-start.3 = ((bf16[8,32,512]{2,1,0:T(8,128)(2,1)}), bf16[8,32,512]{2,1,0:T(8,128)(2,1)S(1)}, u32[]{:S(2)}, u32[]{:S(2)}) async-start(bf16[8,32,512]{2,1,0:T(8,128)(2,1)} %bitcast.35), calls=%async_computation.3 | async-start | bytes 524288 | tf_op jit(solution)/shard_map/all_to_all | solution.py:441
  158.2 2.1 %fusion.1 = bf16[256,1024]{1,0:T(8,128)(2,1)S(1)} fusion(f32[256,1024]{1,0:T(8,128)} %collective-permute-done.22, bf16[512,1024]{1,0:T(8,128)(2,1)S(1)} %copy-done.12, bf16[512,1024]{1,0:T(8,128)(2,1)S(1)} %copy-done.10, bf16[256,1024]{1,0:T(8,128)(2,1)S(1)} %copy-done.24, bf16[256,1024]{1,0:T(8,128)(2,1)} %copy-done.25, pred[]{:T(512)S(6)} %eq.15), kind=kOutput, calls=%fused_computation.5 | convolution fusion | flops 541851648 | bytes 4718593 | tf_op jit(solution)/shard_map/dot_general | solution.py:380
  160.4 3.7 %collective-permute-start.24 = (bf16[128,1024]{1,0:T(8,128)(2,1)S(1)}, bf16[128,1024]{1,0:T(8,128)(2,1)S(1)}, u32[]{:S(2)}, u32[]{:S(2)}) collective-permute-start(bf16[128,1024]{1,0:T(8,128)(2,1)S(1)} %get-tuple-element.22), channel_id=1, source_target_pairs={{0,16},{1,8},{2,0},{3,24},{4,20},{5,12},{6,4},{7,28},{8,25},{9,17}... | collective-permute-start | bytes 786440 | tf_op jit(solution)/shard_map/ppermute | solution.py:374
  164.1 1.9 %collective-permute-start.23 = (bf16[128,1024]{1,0:T(8,128)(2,1)S(1)}, bf16[128,1024]{1,0:T(8,128)(2,1)S(1)}, u32[]{:S(2)}, u32[]{:S(2)}) collective-permute-start(bf16[128,1024]{1,0:T(8,128)(2,1)S(1)} %get-tuple-element.21), channel_id=1, source_target_pairs={{0,0},{1,24},{2,16},{3,8},{4,4},{5,28},{6,20},{7,12},{8,9},{9,1},{... | collective-permute-start | bytes 786440 | tf_op jit(solution)/shard_map/ppermute | solution.py:374
  166.0 1.2 convolution_bitcast_fusion
  167.9 7.3 %collective-permute-done.24 = bf16[128,1024]{1,0:T(8,128)(2,1)S(1)} collective-permute-done((bf16[128,1024]{1,0:T(8,128)(2,1)S(1)}, bf16[128,1024]{1,0:T(8,128)(2,1)S(1)}, u32[]{:S(2)}, u32[]{:S(2)}) %collective-permute-start.24) | collective-permute-done | bytes 262176 | tf_op jit(solution)/shard_map/ppermute | solution.py:374
  175.3 4.3 %collective-permute-done.23 = bf16[128,1024]{1,0:T(8,128)(2,1)S(1)} collective-permute-done((bf16[128,1024]{1,0:T(8,128)(2,1)S(1)}, bf16[128,1024]{1,0:T(8,128)(2,1)S(1)}, u32[]{:S(2)}, u32[]{:S(2)}) %collective-permute-start.23) | collective-permute-done | bytes 262176 | tf_op jit(solution)/shard_map/ppermute | solution.py:374
  179.5 0.8 add_convert_fusion.1
  (93 shorter events, 5.6 us)
Async XLA Ops:
  0.6 23.8 %copy-start.1 = (bf16[512,1024]{1,0:T(8,128)(2,1)S(1)}, bf16[512,1024]{1,0:T(8,128)(2,1)}, u32[]{:S(2)}) copy-start(bf16[512,1024]{1,0:T(8,128)(2,1)} %param.6) | copy-start | bytes 3145732
  0.6 23.8 %copy-start.6 = (bf16[128,4096]{1,0:T(8,128)(2,1)S(1)}, bf16[128,4096]{1,0:T(8,128)(2,1)}, u32[]{:S(2)}) copy-start(bf16[128,4096]{1,0:T(8,128)(2,1)} %param.5) | copy-start | bytes 3145732
  0.7 27.6 %collective-permute-start = (bf16[512,1024]{1,0:T(8,128)(2,1)}, bf16[512,1024]{1,0:T(8,128)(2,1)S(1)}, u32[]{:S(2)}, u32[]{:S(2)}) collective-permute-start(bf16[512,1024]{1,0:T(8,128)(2,1)} %param.6), channel_id=1, source_target_pairs={{0,4},{4,0},{8,12},{12,8},{16,20},{20,16},{24,28},{28,24},{1,5},{5... | collective-permute-start | bytes 3145736 | tf_op jit(solution)/shard_map/ppermute | solution.py:310
  3.7 8.8 %collective-permute-start.1 = (bf16[128,512]{1,0:T(8,128)(2,1)}, bf16[128,512]{1,0:T(8,128)(2,1)}, u32[]{:S(2)}, u32[]{:S(2)}) collective-permute-start(bf16[128,512]{1,0:T(8,128)(2,1)} %get-tuple-element.17), channel_id=1, source_target_pairs={{0,8},{4,12},{8,16},{12,20},{16,24},{20,28},{24,0},{28,4},{1,9},{5... | collective-permute-start | bytes 393224 | tf_op jit(solution)/shard_map/ppermute | solution.py:330
  5.0 9.0 %collective-permute-start.2 = (bf16[128,512]{1,0:T(8,128)(2,1)}, bf16[128,512]{1,0:T(8,128)(2,1)S(1)}, u32[]{:S(2)}, u32[]{:S(2)}) collective-permute-start(bf16[128,512]{1,0:T(8,128)(2,1)} %get-tuple-element.16), channel_id=1, source_target_pairs={{0,16},{4,20},{8,24},{12,28},{16,0},{20,4},{24,8},{28,12},{1,17},{... | collective-permute-start | bytes 393224 | tf_op jit(solution)/shard_map/ppermute | solution.py:330
  6.5 21.2 %all-to-all-start = ((bf16[8,32,512]{2,1,0:T(8,128)(2,1)}), bf16[8,32,512]{2,1,0:T(8,128)(2,1)S(1)}, u32[]{:S(2)}, u32[]{:S(2)}) async-start(bf16[8,32,512]{2,1,0:T(8,128)(2,1)} %broadcast_in_dim.6), calls=%async_computation | async-start | bytes 524288 | tf_op jit(solution)/shard_map/all_to_all | solution.py:263
  12.2 9.6 %collective-permute-start.3 = (bf16[128,512]{1,0:T(8,128)(2,1)}, bf16[128,512]{1,0:T(8,128)(2,1)}, u32[]{:S(2)}, u32[]{:S(2)}) collective-permute-start(bf16[128,512]{1,0:T(8,128)(2,1)} %get-tuple-element.15), channel_id=1, source_target_pairs={{0,24},{4,28},{8,0},{12,4},{16,8},{20,12},{24,16},{28,20},{1,25},{... | collective-permute-start | bytes 393224 | tf_op jit(solution)/shard_map/ppermute | solution.py:330
  23.3 5.0 %collective-permute-start.4 = (bf16[384,512]{1,0:T(8,128)(2,1)}, bf16[384,512]{1,0:T(8,128)(2,1)}, u32[]{:S(2)}, u32[]{:S(2)}) collective-permute-start(bf16[384,512]{1,0:T(8,128)(2,1)} %constant_dynamic-update-slice_fusion), channel_id=1, source_target_pairs={{0,1},{1,0},{2,3},{3,2},{4,5},{5,4},{6,7},{7,6},{8,9},{9,8},{10,11... | collective-permute-start | bytes 1179656 | tf_op jit(solution)/shard_map/ppermute | solution.py:334
  27.8 2.4 %copy-start.7 = (bf16[8,32,512]{2,1,0:T(8,128)(2,1)}, bf16[8,32,512]{2,1,0:T(8,128)(2,1)S(1)}, u32[]{:S(2)}) copy-start(bf16[8,32,512]{2,1,0:T(8,128)(2,1)S(1)} %all-to-all-done) | copy-start | bytes 786436
  28.3 3.5 %copy-start.3 = (bf16[512,1024]{1,0:T(8,128)(2,1)}, bf16[512,1024]{1,0:T(8,128)(2,1)S(1)}, u32[]{:S(2)}) copy-start(bf16[512,1024]{1,0:T(8,128)(2,1)S(1)} %collective-permute-done) | copy-start | bytes 3145732
  30.2 5.2 %copy-start.27 = (f32[1024]{0:T(1024)S(1)}, f32[1024]{0:T(1024)}, u32[]{:S(2)}) copy-start(f32[1024]{0:T(1024)} %param.8) | copy-start | bytes 12292
  31.8 4.3 %copy-start = (bf16[128,1024]{1,0:T(8,128)(2,1)S(1)}, bf16[128,1024]{1,0:T(8,128)(2,1)}, u32[]{:S(2)}) copy-start(bf16[128,1024]{1,0:T(8,128)(2,1)} %cot.5) | copy-start | bytes 786436
  32.7 13.1 %collective-permute-start.7 = (bf16[128,1024]{1,0:T(8,128)(2,1)}, bf16[128,1024]{1,0:T(8,128)(2,1)S(1)}, u32[]{:S(2)}, u32[]{:S(2)}) collective-permute-start(bf16[128,1024]{1,0:T(8,128)(2,1)} %get-tuple-element.19), channel_id=1, source_target_pairs={{0,8},{4,12},{8,16},{12,20},{16,24},{20,28},{24,0},{28,4},{1,9},{5... | collective-permute-start | bytes 786440 | tf_op jit(solution)/shard_map/ppermute | solution.py:330
  34.0 18.6 %collective-permute-start.6 = (bf16[128,1024]{1,0:T(8,128)(2,1)}, bf16[128,1024]{1,0:T(8,128)(2,1)S(1)}, u32[]{:S(2)}, u32[]{:S(2)}) collective-permute-start(bf16[128,1024]{1,0:T(8,128)(2,1)} %get-tuple-element.20), channel_id=1, source_target_pairs={{0,16},{4,20},{8,24},{12,28},{16,0},{20,4},{24,8},{28,12},{1,17},{... | collective-permute-start | bytes 786440 | tf_op jit(solution)/shard_map/ppermute | solution.py:330
  34.1 25.8 %collective-permute-start.5 = (bf16[128,1024]{1,0:T(8,128)(2,1)}, bf16[128,1024]{1,0:T(8,128)(2,1)}, u32[]{:S(2)}, u32[]{:S(2)}) collective-permute-start(bf16[128,1024]{1,0:T(8,128)(2,1)} %get-tuple-element.18), channel_id=1, source_target_pairs={{0,24},{4,28},{8,0},{12,4},{16,8},{20,12},{24,16},{28,20},{1,25},{... | collective-permute-start | bytes 786440 | tf_op jit(solution)/shard_map/ppermute | solution.py:330
  36.1 26.2 %copy-start.4 = (bf16[512,1024]{1,0:T(8,128)(2,1)S(1)}, bf16[512,1024]{1,0:T(8,128)(2,1)}, u32[]{:S(2)}) copy-start(bf16[512,1024]{1,0:T(8,128)(2,1)} %copy-done.3) | copy-start | bytes 3145732
  36.1 26.2 %copy-start.8 = (f32[128,1024]{1,0:T(8,128)S(1)}, f32[128,1024]{1,0:T(8,128)}, u32[]{:S(2)}) copy-start(f32[128,1024]{1,0:T(8,128)} %fusion.15) | copy-start | bytes 1572868
  38.2 31.4 %collective-permute-start.10 = (f32[32,1024]{1,0:T(8,128)S(1)}, f32[32,1024]{1,0:T(8,128)S(1)}, u32[]{:S(2)}, u32[]{:S(2)}) collective-permute-start(f32[32,1024]{1,0:T(8,128)S(1)} %shard_map.76), channel_id=1, source_target_pairs={{12,0},{16,4},{20,8},{24,12},{28,16},{13,1},{17,5},{21,9},{25,13},... | collective-permute-start | bytes 393224 | tf_op jit(solution)/shard_map/ppermute | solution.py:230
  43.3 28.3 %collective-permute-start.9 = (f32[32,1024]{1,0:T(8,128)S(1)}, f32[32,1024]{1,0:T(8,128)S(1)}, u32[]{:S(2)}, u32[]{:S(2)}) collective-permute-start(f32[32,1024]{1,0:T(8,128)S(1)} %shard_map.76), channel_id=1, source_target_pairs={{8,0},{12,4},{16,8},{20,12},{24,16},{28,20},{9,1},{13,5},{17,9},{2... | collective-permute-start | bytes 393224 | tf_op jit(solution)/shard_map/ppermute | solution.py:230
  45.9 14.0 %copy-start.14 = (bf16[128,1024]{1,0:T(8,128)(2,1)}, bf16[128,1024]{1,0:T(8,128)(2,1)S(1)}, u32[]{:S(2)}) copy-start(bf16[128,1024]{1,0:T(8,128)(2,1)S(1)} %collective-permute-done.7) | copy-start | bytes 786436
  45.9 25.8 %collective-permute-start.8 = (f32[32,1024]{1,0:T(8,128)S(1)}, f32[32,1024]{1,0:T(8,128)S(1)}, u32[]{:S(2)}, u32[]{:S(2)}) collective-permute-start(f32[32,1024]{1,0:T(8,128)S(1)} %shard_map.76), channel_id=1, source_target_pairs={{4,0},{8,4},{12,8},{16,12},{20,16},{24,20},{28,24},{5,1},{9,5},{13... | collective-permute-start | bytes 393224 | tf_op jit(solution)/shard_map/ppermute | solution.py:230
  52.6 7.2 %copy-start.15 = (bf16[128,1024]{1,0:T(8,128)(2,1)}, bf16[128,1024]{1,0:T(8,128)(2,1)S(1)}, u32[]{:S(2)}) copy-start(bf16[128,1024]{1,0:T(8,128)(2,1)S(1)} %collective-permute-done.6) | copy-start | bytes 786436
  52.6 13.1 %collective-permute-start.13 = (f32[16,1024]{1,0:T(8,128)}, f32[16,1024]{1,0:T(8,128)S(1)}, u32[]{:S(2)}, u32[]{:S(2)}) collective-permute-start(f32[16,1024]{1,0:T(8,128)} %slice.65), channel_id=1, source_target_pairs={{0,4},{4,8},{8,12},{12,16},{16,20},{20,24},{24,28},{1,5},{5,9},{9,... | collective-permute-start | bytes 196616 | tf_op jit(solution)/shard_map/ppermute | solution.py:230
  59.9 7.8 %collective-permute-start.15 = (f32[16,1024]{1,0:T(8,128)}, f32[16,1024]{1,0:T(8,128)S(1)}, u32[]{:S(2)}, u32[]{:S(2)}) collective-permute-start(f32[16,1024]{1,0:T(8,128)} %slice.65), channel_id=1, source_target_pairs={{0,8},{4,12},{8,16},{12,20},{16,24},{20,28},{1,9},{5,13},{9,17},{1... | collective-permute-start | bytes 196616 | tf_op jit(solution)/shard_map/ppermute | solution.py:230
  65.8 9.9 %copy-start.16 = (f32[16,1024]{1,0:T(8,128)}, f32[16,1024]{1,0:T(8,128)S(1)}, u32[]{:S(2)}) copy-start(f32[16,1024]{1,0:T(8,128)S(1)} %collective-permute-done.13) | copy-start | bytes 196612
  65.8 6.8 %collective-permute-start.16 = (f32[16,1024]{1,0:T(8,128)S(1)}, f32[16,1024]{1,0:T(8,128)S(1)}, u32[]{:S(2)}, u32[]{:S(2)}) collective-permute-start(f32[16,1024]{1,0:T(8,128)S(1)} %shard_map.78), channel_id=1, source_target_pairs={{0,12},{4,16},{8,20},{12,24},{16,28},{1,13},{5,17},{9,21},{13,25},... | collective-permute-start | bytes 196616 | tf_op jit(solution)/shard_map/ppermute | solution.py:230
  67.7 8.0 %copy-start.18 = (f32[16,1024]{1,0:T(8,128)}, f32[16,1024]{1,0:T(8,128)S(1)}, u32[]{:S(2)}) copy-start(f32[16,1024]{1,0:T(8,128)S(1)} %collective-permute-done.15) | copy-start | bytes 196612
  67.7 6.3 %collective-permute-start.12 = (f32[16,1024]{1,0:T(8,128)S(1)}, f32[16,1024]{1,0:T(8,128)S(1)}, u32[]{:S(2)}, u32[]{:S(2)}) collective-permute-start(f32[16,1024]{1,0:T(8,128)S(1)} %shard_map.78), channel_id=1, source_target_pairs={{0,4},{4,8},{8,12},{12,16},{16,20},{20,24},{24,28},{1,5},{5,9},{9,... | collective-permute-start | bytes 196616 | tf_op jit(solution)/shard_map/ppermute | solution.py:230
  69.7 6.0 %copy-start.26 = (f32[32,1024]{1,0:T(8,128)}, f32[32,1024]{1,0:T(8,128)S(1)}, u32[]{:S(2)}) copy-start(f32[32,1024]{1,0:T(8,128)S(1)} %collective-permute-done.10) | copy-start | bytes 393220
  69.7 5.3 %collective-permute-start.14 = (f32[16,1024]{1,0:T(8,128)S(1)}, f32[16,1024]{1,0:T(8,128)S(1)}, u32[]{:S(2)}, u32[]{:S(2)}) collective-permute-start(f32[16,1024]{1,0:T(8,128)S(1)} %shard_map.78), channel_id=1, source_target_pairs={{0,8},{4,12},{8,16},{12,20},{16,24},{20,28},{1,9},{5,13},{9,17},{1... | collective-permute-start | bytes 196616 | tf_op jit(solution)/shard_map/ppermute | solution.py:230
  71.6 4.1 %copy-start.13 = (f32[32,1024]{1,0:T(8,128)}, f32[32,1024]{1,0:T(8,128)S(1)}, u32[]{:S(2)}) copy-start(f32[32,1024]{1,0:T(8,128)S(1)} %collective-permute-done.8) | copy-start | bytes 393220
  72.6 3.1 %copy-start.20 = (f32[16,1024]{1,0:T(8,128)}, f32[16,1024]{1,0:T(8,128)S(1)}, u32[]{:S(2)}) copy-start(f32[16,1024]{1,0:T(8,128)S(1)} %collective-permute-done.16) | copy-start | bytes 196612
  74.1 1.7 copy-start.21
  74.9 0.8 copy-start.22
  75.7 4.4 %collective-permute-start.11 = (f32[16,1024]{1,0:T(8,128)}, f32[16,1024]{1,0:T(8,128)}, u32[]{:S(2)}, u32[]{:S(2)}) collective-permute-start(f32[16,1024]{1,0:T(8,128)} %get-tuple-element.11), channel_id=1, source_target_pairs={{16,0},{20,4},{24,8},{28,12},{17,1},{21,5},{25,9},{29,13},{18,2},{... | collective-permute-start | bytes 196616 | tf_op jit(solution)/shard_map/ppermute | solution.py:230
  79.1 10.6 %copy-start.2 = (bf16[512,1024]{1,0:T(8,128)(2,1)S(1)}, bf16[512,1024]{1,0:T(8,128)(2,1)}, u32[]{:S(2)}) copy-start(bf16[512,1024]{1,0:T(8,128)(2,1)} %param.6) | copy-start | bytes 3145732
  79.1 10.6 %copy-start.5 = (bf16[512,1024]{1,0:T(8,128)(2,1)S(1)}, bf16[512,1024]{1,0:T(8,128)(2,1)}, u32[]{:S(2)}) copy-start(bf16[512,1024]{1,0:T(8,128)(2,1)} %copy-done.3) | copy-start | bytes 3145732
  86.5 7.0 %collective-permute-start.20 = (bf16[128,1024]{1,0:T(8,128)(2,1)S(1)}, bf16[128,1024]{1,0:T(8,128)(2,1)S(1)}, u32[]{:S(2)}, u32[]{:S(2)}) collective-permute-start(bf16[128,1024]{1,0:T(8,128)(2,1)S(1)} %get-tuple-element.9), channel_id=1, source_target_pairs={{0,8},{4,12},{8,16},{12,20},{16,24},{20,28},{24,0},{28,4},{1,9},{5... | collective-permute-start | bytes 786440 | tf_op jit(solution)/shard_map/ppermute | solution.py:330
  88.3 8.7 %collective-permute-start.21 = (bf16[128,1024]{1,0:T(8,128)(2,1)S(1)}, bf16[128,1024]{1,0:T(8,128)(2,1)S(1)}, u32[]{:S(2)}, u32[]{:S(2)}) collective-permute-start(bf16[128,1024]{1,0:T(8,128)(2,1)S(1)} %get-tuple-element.9), channel_id=1, source_target_pairs={{0,24},{4,28},{8,0},{12,4},{16,8},{20,12},{24,16},{28,20},{1,25},{... | collective-permute-start | bytes 786440 | tf_op jit(solution)/shard_map/ppermute | solution.py:330
  89.9 21.4 %copy-start.9 = (bf16[512,1024]{1,0:T(8,128)(2,1)}, bf16[512,1024]{1,0:T(8,128)(2,1)S(1)}, u32[]{:S(2)}) copy-start(bf16[512,1024]{1,0:T(8,128)(2,1)S(1)} %get-tuple-element.13) | copy-start | bytes 3145732
  89.9 21.4 %copy-start.11 = (bf16[512,1024]{1,0:T(8,128)(2,1)}, bf16[512,1024]{1,0:T(8,128)(2,1)S(1)}, u32[]{:S(2)}) copy-start(bf16[512,1024]{1,0:T(8,128)(2,1)S(1)} %get-tuple-element.14) | copy-start | bytes 3145732
  89.9 19.5 %collective-permute-start.19 = (bf16[128,1024]{1,0:T(8,128)(2,1)S(1)}, bf16[128,1024]{1,0:T(8,128)(2,1)S(1)}, u32[]{:S(2)}, u32[]{:S(2)}) collective-permute-start(bf16[128,1024]{1,0:T(8,128)(2,1)S(1)} %get-tuple-element.9), channel_id=1, source_target_pairs={{0,16},{4,20},{8,24},{12,28},{16,0},{20,4},{24,8},{28,12},{1,17},{... | collective-permute-start | bytes 786440 | tf_op jit(solution)/shard_map/ppermute | solution.py:330
  97.0 14.3 %copy-start.25 = (bf16[256,1024]{1,0:T(8,128)(2,1)}, bf16[256,1024]{1,0:T(8,128)(2,1)S(1)}, u32[]{:S(2)}) copy-start(bf16[256,1024]{1,0:T(8,128)(2,1)S(1)} %constant_dynamic-update-slice_fusion.5) | copy-start | bytes 1572868
  109.4 1.8 %copy-start.23 = (bf16[256,1024]{1,0:T(8,128)(2,1)}, bf16[256,1024]{1,0:T(8,128)(2,1)S(1)}, u32[]{:S(2)}) copy-start(bf16[256,1024]{1,0:T(8,128)(2,1)S(1)} %constant_dynamic-update-slice_fusion.3) | copy-start | bytes 1572868
  111.3 19.6 %copy-start.17 = (f32[16,1024]{1,0:T(8,128)S(1)}, f32[16,1024]{1,0:T(8,128)}, u32[]{:S(2)}) copy-start(f32[16,1024]{1,0:T(8,128)} %copy-done.16) | copy-start | bytes 196612
  111.3 19.6 %copy-start.19 = (f32[16,1024]{1,0:T(8,128)S(1)}, f32[16,1024]{1,0:T(8,128)}, u32[]{:S(2)}) copy-start(f32[16,1024]{1,0:T(8,128)} %copy-done.18) | copy-start | bytes 196612
  111.3 46.9 %collective-permute-start.22 = (f32[256,1024]{1,0:T(8,128)}, f32[256,1024]{1,0:T(8,128)}, u32[]{:S(2)}, u32[]{:S(2)}) collective-permute-start(f32[256,1024]{1,0:T(8,128)} %fusion), channel_id=1, source_target_pairs={{0,1},{1,0},{2,3},{3,2},{4,5},{5,4},{6,7},{7,6},{8,9},{9,8},{10,11... | collective-permute-start | bytes 3145736 | tf_op jit(solution)/shard_map/ppermute | solution.py:334
  115.1 15.8 %collective-permute-start.17 = (f32[16,1024]{1,0:T(8,128)}, f32[16,1024]{1,0:T(8,128)}, u32[]{:S(2)}, u32[]{:S(2)}) collective-permute-start(f32[16,1024]{1,0:T(8,128)} %slice.65), channel_id=1, source_target_pairs={{0,12},{4,16},{8,20},{12,24},{16,28},{1,13},{5,17},{9,21},{13,25},... | collective-permute-start | bytes 196616 | tf_op jit(solution)/shard_map/ppermute | solution.py:230
  119.9 11.0 %collective-permute-start.18 = (f32[16,1024]{1,0:T(8,128)}, f32[16,1024]{1,0:T(8,128)}, u32[]{:S(2)}, u32[]{:S(2)}) collective-permute-start(f32[16,1024]{1,0:T(8,128)} %get-tuple-element.23), channel_id=1, source_target_pairs={{0,16},{4,20},{8,24},{12,28},{1,17},{5,21},{9,25},{13,29},{2,18},{... | collective-permute-start | bytes 196616 | tf_op jit(solution)/shard_map/ppermute | solution.py:230
  126.6 17.2 %all-to-all-start.2 = ((bf16[4,32,1024]{2,1,0:T(8,128)(2,1)}), bf16[4,32,1024]{2,1,0:T(8,128)(2,1)}, u32[]{:S(2)}, u32[]{:S(2)}) async-start(bf16[4,32,1024]{2,1,0:T(8,128)(2,1)} %bitcast.39), calls=%async_computation.2 | async-start | bytes 524288 | tf_op jit(solution)/shard_map/all_to_all | solution.py:429
  143.7 14.5 %copy-start.10 = (bf16[512,1024]{1,0:T(8,128)(2,1)S(1)}, bf16[512,1024]{1,0:T(8,128)(2,1)}, u32[]{:S(2)}) copy-start(bf16[512,1024]{1,0:T(8,128)(2,1)} %copy-done.9) | copy-start | bytes 3145732
  143.7 14.5 %copy-start.12 = (bf16[512,1024]{1,0:T(8,128)(2,1)S(1)}, bf16[512,1024]{1,0:T(8,128)(2,1)}, u32[]{:S(2)}) copy-start(bf16[512,1024]{1,0:T(8,128)(2,1)} %copy-done.11) | copy-start | bytes 3145732
  143.7 14.5 %copy-start.24 = (bf16[256,1024]{1,0:T(8,128)(2,1)S(1)}, bf16[256,1024]{1,0:T(8,128)(2,1)}, u32[]{:S(2)}) copy-start(bf16[256,1024]{1,0:T(8,128)(2,1)} %copy-done.23) | copy-start | bytes 1572868
  144.4 6.6 %all-to-all-start.1 = ((bf16[4,128,32]{1,2,0:T(8,128)(2,1)}), bf16[4,128,32]{1,2,0:T(8,128)(2,1)S(1)}, u32[]{:S(2)}, u32[]{:S(2)}) async-start(bf16[4,128,32]{1,2,0:T(8,128)(2,1)} %broadcast_in_dim.8), calls=%async_computation.1 | async-start | bytes 65536 | tf_op jit(solution)/shard_map/all_to_all | solution.py:263
  151.1 16.2 %all-to-all-start.3 = ((bf16[8,32,512]{2,1,0:T(8,128)(2,1)}), bf16[8,32,512]{2,1,0:T(8,128)(2,1)S(1)}, u32[]{:S(2)}, u32[]{:S(2)}) async-start(bf16[8,32,512]{2,1,0:T(8,128)(2,1)} %bitcast.35), calls=%async_computation.3 | async-start | bytes 524288 | tf_op jit(solution)/shard_map/all_to_all | solution.py:441
  160.4 14.8 %collective-permute-start.24 = (bf16[128,1024]{1,0:T(8,128)(2,1)S(1)}, bf16[128,1024]{1,0:T(8,128)(2,1)S(1)}, u32[]{:S(2)}, u32[]{:S(2)}) collective-permute-start(bf16[128,1024]{1,0:T(8,128)(2,1)S(1)} %get-tuple-element.22), channel_id=1, source_target_pairs={{0,16},{1,8},{2,0},{3,24},{4,20},{5,12},{6,4},{7,28},{8,25},{9,17}... | collective-permute-start | bytes 786440 | tf_op jit(solution)/shard_map/ppermute | solution.py:374
  164.1 15.4 %collective-permute-start.23 = (bf16[128,1024]{1,0:T(8,128)(2,1)S(1)}, bf16[128,1024]{1,0:T(8,128)(2,1)S(1)}, u32[]{:S(2)}, u32[]{:S(2)}) collective-permute-start(bf16[128,1024]{1,0:T(8,128)(2,1)S(1)} %get-tuple-element.21), channel_id=1, source_target_pairs={{0,0},{1,24},{2,16},{3,8},{4,4},{5,28},{6,20},{7,12},{8,9},{9,1},{... | collective-permute-start | bytes 786440 | tf_op jit(solution)/shard_map/ppermute | solution.py:374

commit v3 on v2

--- a/solution.py
+++ b/solution.py
@@ -10,6 +10,8 @@
 NS = 16
 LANES = 128
 UNROLL = 8
+ROWS = 4
+WORK = 1
 F32 = jnp.float32
 BF16 = jnp.bfloat16
 
@@ -186,7 +188,7 @@
         gkq_out[...] = spread(key_acc, 0) + spread(query_acc, NS)
 
 
-def call(kernel, tokens, width, block, ins, outs, scratch, args, flops):
+def call(kernel, tokens, width, block, ins, outs, scratch, args, work):
     def spec(kind):
         return {
             "kq": pl.BlockSpec((tokens, 2 * NS, LANES), lambda c: (0, 0, 0)),
@@ -217,8 +219,8 @@
         scratch_shapes=scratch,
         compiler_params=pltpu.CompilerParams(vmem_limit_bytes=48 * 2**20),
         cost_estimate=pl.CostEstimate(
-            flops=flops * tokens * NS * width,
-            bytes_accessed=4 * tokens * width * (1 + NS * ("states" in ins + outs)),
+            flops=work * WORK * tokens * NS * width,
+            bytes_accessed=1024,
             transcendentals=0,
         ),
     )(*args)
@@ -230,40 +232,42 @@
     return lax.ppermute(value, axis, pairs)
 
 
-def carried(decay, total, sign, together):
+def carried(pair, sign):
     count = lax.axis_size("seq")
     window, radix = 1, 4
-    inc_decay, inc_total = decay, total
-    exc_decay, exc_total = None, None
+    total, decay = pair[:NS], pair[NS:]
+    inc, exc_total, exc_decay, ready = pair, None, None, None
     while window < count:
         last = window * radix >= count
-        joint = together and not last
-        pair = jnp.concatenate([inc_total, inc_decay], axis=0) if joint else None
+        if last and window * 2 >= count:
+            inc = inc[:NS]
+        wire = ready = inc.astype(BF16)
         for j in range(1, min(radix, -(-count // window))):
-            by = sign * window * j
-            if joint:
-                far = shifted(pair, "seq", by)
-                far_total, far_decay = far[:NS], far[NS:]
-            else:
-                far_total, far_decay = shifted(inc_total, "seq", by), shifted(inc_decay, "seq", by)
+            far = shifted(wire, "seq", sign * window * j).astype(F32)
+            far_total, far_decay = far[:NS], far[NS:]
             if exc_total is None:
                 exc_total, exc_decay = far_total, far_decay
             else:
                 exc_total = exc_total + exc_decay * far_total
-                exc_decay = exc_decay * far_decay
-        if not last:
-            inc_total = total + decay * exc_total
-            inc_decay = decay * exc_decay
+                if far_decay.shape[0]:
+                    exc_decay = exc_decay * far_decay
+        inc = jnp.concatenate([total + decay * exc_total, decay * exc_decay], axis=0)
         window *= radix
-    return exc_total
-
-
-def gather_columns(value, axis):
-    count = lax.axis_size(axis)
-    parts = lax.all_to_all(
-        jnp.broadcast_to(value[None], (count,) + value.shape), axis, 0, 0, tiled=True
-    )
-    return jnp.moveaxis(parts, 0, 1).reshape(value.shape[0], count * value.shape[1])
+    return exc_total, ready
+
+
+def along_chan(value, by):
+    count = lax.axis_size("chan")
+    return lax.ppermute(value, "chan", [(i, (i + by) % count) for i in range(count)]) if by else value
+
+
+def gathered(value, axis):
+    copies = jnp.broadcast_to(value[None], (lax.axis_size(axis),) + value.shape)
+    return lax.all_to_all(copies, axis, 0, 0, tiled=True)
+
+
+def side_by_side(parts):
+    return jnp.moveaxis(parts, 0, 1).reshape(parts.shape[1], -1)
 
 
 def scatter_sum_columns(value):
@@ -290,10 +294,16 @@
         self.tokens = tokens
         self.full = lax.all_gather(w_inner, "seq", axis=0, tiled=True)
 
-    def inner(self):
-        return jnp.dot(self.tokens, self.full, preferred_element_type=F32)
-
-    def grad_tokens(self, grad):
+    def partials(self, before):
+        return jnp.dot(self.tokens, self.full, preferred_element_type=F32), None, None, before
+
+    def inner(self, near, far, beside):
+        return near
+
+    def grads(self, grad):
+        return None
+
+    def grad_tokens(self, grad, far, after):
         return scatter_sum_columns(dot_t(grad, self.full))
 
 
@@ -301,76 +311,71 @@
     def __init__(self, tokens, w_inner):
         self.depth, self.width = w_inner.shape
         self.count = tokens.shape[0]
-        seqs = lax.axis_size("seq")
-        self.rows = seqs // 2
         index = lax.axis_index("seq")
         self.row, self.side = index // 2, index % 2
         self.first = lax.axis_index("chan") % 2 == 0
         self.w_mine = w_inner
-        self.w_other = lax.ppermute(w_inner, "seq", [(i, i ^ 1) for i in range(seqs)])
+        self.w_other = self.trade(w_inner, "seq", 1)
         half = jnp.where(self.first, self.side, 1 - self.side)
         came = [
-            self.move(self.columns(tokens, (self.row + j) % self.rows, half), j)
-            for j in range(1, self.rows)
+            self.trade(self.columns(tokens, self.row ^ m, half), "seq", 2 * m) for m in (1, 3, 2)
         ]
-        came = jnp.concatenate(came, axis=0)
-        partner = self.swap(came)
-        self.far_mine = jnp.where(self.first, came, partner)
-        self.far_other = jnp.where(self.first, partner, came)
+        self.came = jnp.concatenate(came, axis=0)
         self.near_mine = self.columns(tokens, self.row, self.side)
         self.near_other = self.columns(tokens, self.row, 1 - self.side)
 
     def columns(self, tokens, row, side):
         return lax.dynamic_slice_in_dim(tokens, (row * 2 + side) * self.depth, self.depth, 1)
 
-    def move(self, value, by):
-        pairs = [
-            (r * 2 + s, (r + by) % self.rows * 2 + s) for r in range(self.rows) for s in range(2)
-        ]
-        return lax.ppermute(value, "seq", pairs)
-
-    def swap(self, value):
-        chans = lax.axis_size("chan")
-        return lax.ppermute(value, "chan", [(i, i ^ 1) for i in range(chans)])
-
-    def inner(self):
+    def trade(self, value, axis, mask):
+        pairs = [(i, i ^ mask) for i in range(lax.axis_size(axis))]
+        return lax.ppermute(value, axis, pairs)
+
+    def partials(self, before):
         def product(mine, other):
             return jnp.dot(mine, self.w_mine, preferred_element_type=F32) + jnp.dot(
                 other, self.w_other, preferred_element_type=F32
             )
 
-        far = product(self.far_mine, self.far_other).astype(BF16)
-        total = product(self.near_mine, self.near_other)
-        for j in range(1, self.rows):
-            block = far[(j - 1) * self.count : j * self.count]
-            total = total + self.move(block, -j).astype(F32)
-        return total
-
-    def grad_tokens(self, grad):
+        partner = self.trade(self.came, "chan", 1)
+        mine = jnp.where(self.first, self.came, partner)
+        other = jnp.where(self.first, partner, self.came)
+        two = 2 * self.count
+        beside = product(mine[:two], other[:two]).astype(BF16)
+        beside, before = lax.optimization_barrier((beside, before))
+        near = product(self.near_mine, self.near_other)
+        return near, product(mine[two:], other[two:]), self.trade(beside, "seq", 2), before
+
+    def inner(self, near, far, beside):
+        far = far + beside[self.count :].astype(F32)
+        return near + beside[: self.count].astype(F32) + self.trade(far.astype(BF16), "seq", 4).astype(F32)
+
+    def grads(self, grad):
+        return self.trade(grad, "seq", 4)
+
+    def grad_tokens(self, grad, far, after):
         chans = lax.axis_size("chan")
-        pairs = chans // 2
-        blocks = [grad] + [self.move(grad, j) for j in range(1, self.rows)]
-        even = jnp.concatenate(blocks[0::2], axis=0)
-        odd = jnp.concatenate(blocks[1::2], axis=0)
+        even = jnp.concatenate([grad, far], axis=0)
+        odd = self.trade(even, "seq", 2)
+        odd, after = lax.optimization_barrier((odd, after))
         keep = jnp.where(self.first, even, odd)
         give = jnp.where(self.first, odd, even)
         one, two = self.w_mine, self.w_other
         full = jnp.concatenate(
             [jnp.where(self.side == 0, one, two), jnp.where(self.side == 0, two, one)], axis=0
         )
-        kept = dot_t(keep, full) + self.swap(dot_t(give, full))
-        pieces = kept.astype(BF16).reshape(pairs, self.count, -1)
+        kept = dot_t(keep, full) + self.trade(dot_t(give, full), "chan", 1)
+        pieces = kept.astype(BF16).reshape(2, self.count, -1)
         y = lax.axis_index("chan") // 2
         total = None
-        for m in range(pairs):
-            piece = lax.dynamic_index_in_dim(pieces, (y + m) % pairs, 0, keepdims=False)
-            route = []
-            for r in range(self.rows):
-                for s in range(2):
-                    for c in range(chans):
-                        p = (c // 2 + m) % pairs
-                        to = (r - c % 2 - 2 * p) % self.rows
-                        route.append(((r * 2 + s) * chans + c, (to * 2 + s) * chans + r))
+        for m in range(2):
+            piece = lax.dynamic_index_in_dim(pieces, y ^ m, 0, keepdims=False)
+            route = [
+                (((r * 2 + s) * chans + c), ((r ^ (c % 2 + 2 * (c // 2 ^ m))) * 2 + s) * chans + r)
+                for r in range(ROWS)
+                for s in range(2)
+                for c in range(chans)
+            ]
             piece = lax.ppermute(piece, ("seq", "chan"), route).astype(F32)
             total = piece if total is None else total + piece
         return total
@@ -386,9 +391,17 @@
     kq_cols = w_keyquery.shape[1] * w_keyquery.shape[2]
     seqs, chans = lax.axis_size("seq"), lax.axis_size("chan")
     block = min(width, 512)
-    short = seqs == 2 * chans and chans % 2 == 0 and count * seqs <= w_inner.shape[0] * seqs
+    short = seqs == 2 * ROWS and chans == ROWS and count <= w_inner.shape[0]
     plan = (Exchanged if short else Gathered)(tokens, w_inner)
-    full_kq = gather_columns(w_keyquery.reshape(-1, kq_cols).T, "seq")
+    kq_parts = gathered(w_keyquery.reshape(-1, kq_cols).T, "seq")
+    full_kq = side_by_side(kq_parts)
+    group = lax.axis_index("chan")
+    kq_rows = []
+    for m in range(chans):
+        rows = lax.dynamic_slice_in_dim(
+            full_kq, (group + m) % chans * (full_kq.shape[1] // chans), full_kq.shape[1] // chans, 1
+        )
+        kq_rows.append(along_chan(rows, m))
     keyquery = dot_t(tokens, full_kq)
     keys = keyquery[:, :NS]
     sumsq = jnp.sum(keys * keys, axis=1)
@@ -400,37 +413,39 @@
     (pair,) = run(
         adjoint_totals_kernel,
         ins=["kq", "rows", "rows16"], outs=["pair"], scratch=[rows_f],
-        args=(spread, eps, grad_out), flops=8,
-    )
-    lam, decay = pair[:NS], pair[NS:]
-    end_adjoint = carried(decay, lam, -1, True)
+        args=(spread, eps, grad_out), work=4,
+    )
+    if short:
+        pair, plan.came = lax.optimization_barrier((pair, plan.came))
+    end_adjoint, _ = carried(pair, -1)
+    near, far, beside, end_adjoint = plan.partials(end_adjoint)
     adjoints, inner_grad = run(
         adjoint_kernel,
         ins=["kq", "rows", "rows16", "state"], outs=["states", "rows16"], scratch=[rows_f, rows_f],
-        args=(spread, eps, grad_out, end_adjoint), flops=8,
-    )
-    inner = plan.inner()
+        args=(spread, eps, grad_out, end_adjoint), work=10,
+    )
+    beside, _ = lax.optimization_barrier((beside, inner_grad))
+    far_grad = plan.grads(inner_grad)
+    inner, far_grad, kq_rows = lax.optimization_barrier(
+        (plan.inner(near, far, beside), far_grad, jnp.concatenate(kq_rows, axis=0))
+    )
     (alone_end,) = run(
         state_total_kernel,
         ins=["kq", "rows", "rows"], outs=["state"], scratch=[],
-        args=(spread, eps, inner), flops=6,
-    )
-    start_state = carried(decay, alone_end, 1, False)
-    tokens_sum = plan.grad_tokens(inner_grad)
+        args=(spread, eps, inner), work=4,
+    )
+    start_state, _ = carried(jnp.concatenate([alone_end, pair[NS:]], axis=0), 1)
+    tokens_sum = plan.grad_tokens(inner_grad, far_grad, start_state)
     acc = pltpu.VMEM((count, NS, LANES), F32)
     mixed, kq_grad = run(
         mixer_kernel,
         ins=["kq", "rows", "rows", "rows16", "states", "state"], outs=["rows16", "gkq"],
         scratch=[rows_f, rows_f, acc, acc],
-        args=(spread, eps, inner, grad_out, adjoints, start_state), flops=20,
+        args=(spread, eps, inner, grad_out, adjoints, start_state), work=22,
     )
     kq_grad = kq_grad[:, :kq_cols].astype(BF16)
 
-    kq_rows = lax.all_to_all(
-        jnp.moveaxis(full_kq.reshape(kq_cols, chans, -1), 1, 0), "chan", 0, 0, tiled=True
-    )
-    kq_rows = kq_rows.reshape(chans * kq_cols, -1)
-    all_kq = gather_columns(kq_grad, "chan")
+    all_kq = jnp.concatenate([along_chan(kq_grad, m) for m in range(chans)], axis=1)
     grad_tokens = (
         tokens_sum + jnp.dot(all_kq, kq_rows, preferred_element_type=F32)
     ).astype(BF16)

time: 182 us -> 158 us (0.87)
  the two profiles are of different devices: /device:TPU:17 before, /device:TPU:6 now
where the time goes in v3:
time: 158 us; the launch traced here: 157 us
  waiting for transfers between devices  59.1 us (37%)
  starting transfers between devices  49.1 us (31%)
  Pallas kernels  21.2 us (13%)
  matrix products  15.8 us (10%)
  local copies, waits for them, and re-layouts  5.89 us (4%)
  other arithmetic  4.83 us (3%)
    ppermute x10, waiting for transfers between devices, trade(): return lax.ppermute(value, axis, pairs)  30 us
    pallas_call x4, Pallas kernels, call(): pl.pallas_call(kernel, grid=(width // block,), in_specs=[spec(kind) for k...  21.2 us
    ppermute x8, waiting for transfers between devices, shifted(): return lax.ppermute(value, axis, pairs)  19.8 us
    ppermute x8, starting transfers between devices, shifted(): return lax.ppermute(value, axis, pairs)  16.3 us
    ppermute x10, starting transfers between devices, trade(): return lax.ppermute(value, axis, pairs)  9.74 us
    ppermute x2, starting transfers between devices, grad_tokens(): piece = lax.ppermute(piece, ('seq', 'chan'), route).astype(F32)  7.64 us
    ppermute x2, waiting for transfers between devices, grad_tokens(): piece = lax.ppermute(piece, ('seq', 'chan'), route).astype(F32)  6.47 us
    all_to_all x1, starting transfers between devices, gathered(): return lax.all_to_all(copies, axis, 0, 0, tiled=True)  6.47 us
  transfers between devices with their start and end apart: 28, of which 14 were waited for; matrix products, arithmetic and copies ran while one was open for 12% of the time, Pallas kernels for 12%

profile of v3, /device:TPU:6, one launch (start us, length us, event | category | flops | bytes accessed | tf_op | source)
XLA Modules:
  0.0 157.0 jit_solution(11861707478179540651)
XLA Ops:
  0.6 1.6 broadcast_in_dim.4
  2.2 6.5 %all-to-all-start = ((bf16[8,32,512]{2,1,0:T(8,128)(2,1)}), bf16[8,32,512]{2,1,0:T(8,128)(2,1)S(1)}, u32[]{:S(2)}, u32[]{:S(2)}) async-start(bf16[8,32,512]{2,1,0:T(8,128)(2,1)} %broadcast_in_dim.4), calls=%async_computation | async-start | bytes 524288 | tf_op jit(solution)/shard_map/all_to_all | solution.py:266
  8.7 1.1 constant_dynamic-slice_fusion.6
  9.7 2.4 %collective-permute-start.3 = (bf16[128,512]{1,0:T(8,128)(2,1)S(1)}, bf16[128,512]{1,0:T(8,128)(2,1)S(1)}, u32[]{:S(2)}, u32[]{:S(2)}) collective-permute-start(bf16[128,512]{1,0:T(8,128)(2,1)S(1)} %get-tuple-element.37), channel_id=1, source_target_pairs={{0,16},{4,20},{8,24},{12,28},{16,0},{20,4},{24,8},{28,12},{1,17},{... | collective-permute-start | bytes 393224 | tf_op jit(solution)/shard_map/ppermute | solution.py:332
  12.2 1.5 collective-permute-start.2
  13.6 0.6 collective-permute-start
  14.2 12.3 %collective-permute-done.3 = bf16[128,512]{1,0:T(8,128)(2,1)S(1)} collective-permute-done((bf16[128,512]{1,0:T(8,128)(2,1)S(1)}, bf16[128,512]{1,0:T(8,128)(2,1)S(1)}, u32[]{:S(2)}, u32[]{:S(2)}) %collective-permute-start.3) | collective-permute-done | bytes 131104 | tf_op jit(solution)/shard_map/ppermute | solution.py:332
  26.5 0.8 pad_maximum_fusion.5
  27.4 0.4 fusion.47
  27.8 0.1 copy.11
  27.9 0.1 add_divide_fusion.eps
  28.1 0.6 broadcast_in_dim.5.kq
  28.7 2.1 %shard_map.76 = f32[32,1024]{1,0:T(8,128)S(1)} custom-call(f32[128,32,128]{2,1,0:T(8,128)S(1)} %broadcast_in_dim.5.kq, f32[128,1024]{1,0:T(8,128)S(1)} %add_divide_fusion.eps, bf16[128,1024]{1,0:T(8,128)(2,1)S(1)} %copy-done), custom_call_target="tpu_custom_call" | custom-call | flops 8388608 | bytes 1024 | tf_op jit(solution)/shard_map/pallas_call | solution.py:213
  30.8 1.3 collective-permute-start.7
  32.1 1.3 collective-permute-start.6
  33.4 2.8 %collective-permute-start.5 = (bf16[32,1024]{1,0:T(8,128)(2,1)S(1)}, bf16[32,1024]{1,0:T(8,128)(2,1)S(1)}, u32[]{:S(2)}, u32[]{:S(2)}) collective-permute-start(bf16[32,1024]{1,0:T(8,128)(2,1)S(1)} %convert_element_type.69), channel_id=1, source_target_pairs={{4,0},{8,4},{12,8},{16,12},{20,16},{24,20},{28,24},{5,1},{9,5},{13... | collective-permute-start | bytes 196616 | tf_op jit(solution)/shard_map/ppermute | solution.py:232
  36.2 0.1 collective-permute-start.4
  36.3 3.1 %collective-permute-done.7 = bf16[32,1024]{1,0:T(8,128)(2,1)S(1)} collective-permute-done((bf16[32,1024]{1,0:T(8,128)(2,1)S(1)}, bf16[32,1024]{1,0:T(8,128)(2,1)S(1)}, u32[]{:S(2)}, u32[]{:S(2)}) %collective-permute-start.7) | collective-permute-done | bytes 65568 | tf_op jit(solution)/shard_map/ppermute | solution.py:232
  39.5 1.3 collective-permute-done.5
  40.8 1.3 collective-permute-start.8
  42.1 6.6 %collective-permute-done.8 = bf16[16,1024]{1,0:T(8,128)(2,1)S(1)} collective-permute-done((bf16[16,1024]{1,0:T(8,128)(2,1)S(1)}, bf16[16,1024]{1,0:T(8,128)(2,1)S(1)}, u32[]{:S(2)}, u32[]{:S(2)}) %collective-permute-start.8) | collective-permute-done | bytes 32800 | tf_op jit(solution)/shard_map/ppermute | solution.py:232
  48.9 2.0 %fusion.11 = f32[256,1024]{1,0:T(8,128)S(1)} fusion(bf16[512,1024]{1,0:T(8,128)(2,1)} %collective-permute-done, bf16[384,512]{1,0:T(8,128)(2,1)S(1)} %get-tuple-element.39), kind=kOutput, calls=%fused_computation.26 | convolution fusion | flops 268435456 | bytes 2359296 | tf_op jit(solution)/shard_map/dot_general | solution.py:336
  50.9 1.2 fusion.2
  52.1 2.1 %collective-permute-start.9 = (bf16[256,1024]{1,0:T(8,128)(2,1)}, bf16[256,1024]{1,0:T(8,128)(2,1)}, u32[]{:S(2)}, u32[]{:S(2)}) collective-permute-start(bf16[256,1024]{1,0:T(8,128)(2,1)} %fusion.2), channel_id=1, source_target_pairs={{0,8},{4,12},{8,0},{12,4},{16,24},{20,28},{24,16},{28,20},{1,9},{5... | collective-permute-start | bytes 1572872 | tf_op jit(solution)/shard_map/ppermute | solution.py:332
  54.2 0.6 constant_dynamic-slice_fusion.3
  54.9 0.5 collective-permute-start.13
  55.4 0.2 collective-permute-start.12
  55.6 5.4 %shard_map.77 = (f32[128,16,1024]{2,1,0:T(8,128)}, bf16[128,1024]{1,0:T(8,128)(2,1)}) custom-call(f32[128,32,128]{2,1,0:T(8,128)S(1)} %broadcast_in_dim.5.kq, f32[128,1024]{1,0:T(8,128)S(1)} %add_divide_fusion.eps, bf16[128,1024]{1,0:T(8,128)(2,1)S(1)} %copy-done, f32[16,1024]{1,0:T(8,128)S(1)} %fusion.25.start), custom_call_target="tpu_custom_call" | custom-call | flops 20971520 | bytes 1024 | tf_op jit(solution)/shard_map/pallas_call | solution.py:213
  61.0 1.6 %fusion.14 = f32[128,1024]{1,0:T(8,128)S(1)} fusion(bf16[512,1024]{1,0:T(8,128)(2,1)} %collective-permute-done, bf16[384,512]{1,0:T(8,128)(2,1)} %copy-done.7), kind=kOutput, calls=%fused_computation.32 | convolution fusion | flops 134217728 | bytes 1703936 | tf_op jit(solution)/shard_map/dot_general | solution.py:336
  62.6 1.1 collective-permute-done.9
  63.7 1.3 fusion.6
  65.1 0.1 collective-permute-start.10
  65.2 2.0 %fusion.18 = f32[128,1024]{1,0:T(8,128)} fusion(bf16[512,1024]{1,0:T(8,128)(2,1)S(1)} %copy-done.2, bf16[128,4096]{1,0:T(8,128)(2,1)} %param.5, s32[]{:T(128)S(6)} %select_n.109), kind=kOutput, calls=%fused_computation.36 | convolution fusion | flops 134217728 | bytes 1703940 | tf_op jit(solution)/shard_map/dot_general | solution.py:336
  67.2 1.6 %pad_maximum_fusion.6 = bf16[128,1024]{1,0:T(8,128)(2,1)} fusion(bf16[32,1024]{1,0:T(8,128)(2,1)} %collective-permute-done.14, bf16[32,1024]{1,0:T(8,128)(2,1)} %collective-permute-done.13, bf16[32,1024]{1,0:T(8,128)(2,1)} %collective-permute-done.12, bf16[32,1024]{1,0:T(8,128)(2,1)S(1)} %get-tuple-element.42), kind=kLoop, calls=%fused_computation.29 | loop fusion | flops 1048576 | bytes 524288 | tf_op jit(solution)/shard_map/concatenate | solution.py:430
  68.8 2.9 %collective-permute-start.11 = (bf16[128,1024]{1,0:T(8,128)(2,1)}, bf16[128,1024]{1,0:T(8,128)(2,1)S(1)}, u32[]{:S(2)}, u32[]{:S(2)}) collective-permute-start(bf16[128,1024]{1,0:T(8,128)(2,1)} %get-tuple-element.20), channel_id=1, source_target_pairs={{0,16},{4,20},{8,24},{12,28},{16,0},{20,4},{24,8},{28,12},{1,17},{... | collective-permute-start | bytes 786440 | tf_op jit(solution)/shard_map/ppermute | solution.py:332
  71.7 1.0 constant_dynamic-update-slice_fusion.1
  72.7 12.7 %collective-permute-done.10 = bf16[128,1024]{1,0:T(8,128)(2,1)} collective-permute-done((bf16[128,1024]{1,0:T(8,128)(2,1)S(1)}, bf16[128,1024]{1,0:T(8,128)(2,1)}, u32[]{:S(2)}, u32[]{:S(2)}) %collective-permute-start.10) | collective-permute-done | bytes 262176 | tf_op jit(solution)/shard_map/ppermute | solution.py:332
  85.5 1.9 %fusion.4.inner = f32[128,1024]{1,0:T(8,128)S(1)} fusion(f32[128,1024]{1,0:T(8,128)} %fusion.18, bf16[512,1024]{1,0:T(8,128)(2,1)} %collective-permute-done, bf16[128,1024]{1,0:T(8,128)(2,1)} %collective-permute-done.10, bf16[256,1024]{1,0:T(8,128)(2,1)} %collective-permute-done.9, bf16[128,4096]{1,0:T(8,128)(2,1)} %param.5, s32[]{:T(128)S(6)} %select_n.110), kind=kOutput, calls=%fused_computation.10 | convolution fusion | flops 134873088 | bytes 2752516 | tf_op jit(solution)/shard_map/dot_general | solution.py:336
  87.4 3.6 %collective-permute-done.11 = bf16[128,1024]{1,0:T(8,128)(2,1)S(1)} collective-permute-done((bf16[128,1024]{1,0:T(8,128)(2,1)}, bf16[128,1024]{1,0:T(8,128)(2,1)S(1)}, u32[]{:S(2)}, u32[]{:S(2)}) %collective-permute-start.11) | collective-permute-done | bytes 262176 | tf_op jit(solution)/shard_map/ppermute | solution.py:332
  90.9 1.9 %shard_map.78 = f32[16,1024]{1,0:T(8,128)S(1)} custom-call(f32[128,32,128]{2,1,0:T(8,128)S(1)} %broadcast_in_dim.5.kq, f32[128,1024]{1,0:T(8,128)S(1)} %add_divide_fusion.eps, f32[128,1024]{1,0:T(8,128)S(1)} %fusion.4.inner), custom_call_target="tpu_custom_call" | custom-call | flops 8388608 | bytes 1024 | tf_op jit(solution)/shard_map/pallas_call | solution.py:213
  92.8 1.3 collective-permute-start.17
  94.1 2.4 %collective-permute-start.16 = (bf16[32,1024]{1,0:T(8,128)(2,1)S(1)}, bf16[32,1024]{1,0:T(8,128)(2,1)S(1)}, u32[]{:S(2)}, u32[]{:S(2)}) collective-permute-start(bf16[32,1024]{1,0:T(8,128)(2,1)S(1)} %pad_maximum_fusion.7), channel_id=1, source_target_pairs={{0,8},{4,12},{8,16},{12,20},{16,24},{20,28},{1,9},{5,13},{9,17},{1... | collective-permute-start | bytes 196616 | tf_op jit(solution)/shard_map/ppermute | solution.py:232
  96.6 4.3 %collective-permute-start.15 = (bf16[32,1024]{1,0:T(8,128)(2,1)S(1)}, bf16[32,1024]{1,0:T(8,128)(2,1)S(1)}, u32[]{:S(2)}, u32[]{:S(2)}) collective-permute-start(bf16[32,1024]{1,0:T(8,128)(2,1)S(1)} %pad_maximum_fusion.7), channel_id=1, source_target_pairs={{0,4},{4,8},{8,12},{12,16},{16,20},{20,24},{24,28},{1,5},{5,9},{9,... | collective-permute-start | bytes 196616 | tf_op jit(solution)/shard_map/ppermute | solution.py:232
  100.9 0.1 collective-permute-start.19
  101.1 2.4 %collective-permute-done.15 = bf16[32,1024]{1,0:T(8,128)(2,1)S(1)} collective-permute-done((bf16[32,1024]{1,0:T(8,128)(2,1)S(1)}, bf16[32,1024]{1,0:T(8,128)(2,1)S(1)}, u32[]{:S(2)}, u32[]{:S(2)}) %collective-permute-start.15) | collective-permute-done | bytes 65568 | tf_op jit(solution)/shard_map/ppermute | solution.py:232
  103.5 1.6 %collective-permute-start.18 = (bf16[16,1024]{1,0:T(8,128)(2,1)S(1)}, bf16[16,1024]{1,0:T(8,128)(2,1)S(1)}, u32[]{:S(2)}, u32[]{:S(2)}) collective-permute-start(bf16[16,1024]{1,0:T(8,128)(2,1)S(1)} %get-tuple-element.29), channel_id=1, source_target_pairs={{0,16},{4,20},{8,24},{12,28},{1,17},{5,21},{9,25},{13,29},{2,18},{... | collective-permute-start | bytes 98312 | tf_op jit(solution)/shard_map/ppermute | solution.py:232
  105.1 1.4 broadcast_select_fusion.1
  106.5 6.4 %collective-permute-done.18 = bf16[16,1024]{1,0:T(8,128)(2,1)S(1)} collective-permute-done((bf16[16,1024]{1,0:T(8,128)(2,1)S(1)}, bf16[16,1024]{1,0:T(8,128)(2,1)S(1)}, u32[]{:S(2)}, u32[]{:S(2)}) %collective-permute-start.18) | collective-permute-done | bytes 32800 | tf_op jit(solution)/shard_map/ppermute | solution.py:232
  112.9 0.2 collective-permute-done.19
  113.1 1.8 %fusion = f32[256,1024]{1,0:T(8,128)} fusion(bf16[512,1024]{1,0:T(8,128)(2,1)S(1)} %get-tuple-element.34, bf16[512,1024]{1,0:T(8,128)(2,1)S(1)} %get-tuple-element.33, bf16[256,1024]{1,0:T(8,128)(2,1)S(1)} %collective-permute-done.19, bf16[256,1024]{1,0:T(8,128)(2,1)S(1)} %constant_dynamic-update-slice_fusion, pred[]{:T(512)S(6)} %eq.14), kind=kOutput, calls=%fused_computation.4 | convolution fusion | flops 541327360 | bytes 4194305 | tf_op jit(solution)/shard_map/dot_general | solution.py:385
  115.1 11.9 %shard_map.79 = (bf16[128,1024]{1,0:T(8,128)(2,1)}, f32[128,128]{1,0:T(8,128)S(1)}) custom-call(f32[128,32,128]{2,1,0:T(8,128)S(1)} %broadcast_in_dim.5.kq, f32[128,1024]{1,0:T(8,128)S(1)} %add_divide_fusion.eps, f32[128,1024]{1,0:T(8,128)S(1)} %fusion.4.inner, bf16[128,1024]{1,0:T(8,128)(2,1)S(1)} %copy-done, f32[128,16,1024]{2,1,0:T(8,128)} %get-tuple-element.23.adj_in, ...), custom_call_target="tpu_custom_call" | custom-call | flops 46137344 | bytes 1024 | tf_op jit(solution)/shard_map/pallas_call | solution.py:213
  126.9 0.3 convolution_convert_fusion
  127.2 0.7 copy.16
  128.0 5.9 %all-to-all-start.1 = ((bf16[8,32,512]{2,1,0:T(8,128)(2,1)}), bf16[8,32,512]{2,1,0:T(8,128)(2,1)S(1)}, u32[]{:S(2)}, u32[]{:S(2)}) async-start(bf16[8,32,512]{2,1,0:T(8,128)(2,1)} %bitcast.30), calls=%async_computation.1 | async-start | bytes 524288 | tf_op jit(solution)/shard_map/all_to_all | solution.py:456
  133.9 2.2 %fusion.1 = bf16[256,1024]{1,0:T(8,128)(2,1)S(1)} fusion(f32[256,1024]{1,0:T(8,128)} %collective-permute-done.20, bf16[512,1024]{1,0:T(8,128)(2,1)S(1)} %copy-done.12, bf16[512,1024]{1,0:T(8,128)(2,1)S(1)} %copy-done.10, bf16[256,1024]{1,0:T(8,128)(2,1)} %copy-done.14, bf16[256,1024]{1,0:T(8,128)(2,1)} %copy-done.16, pred[]{:T(512)S(6)} %eq.14), kind=kOutput, calls=%fused_computation.5 | convolution fusion | flops 541851648 | bytes 4718593 | tf_op jit(solution)/shard_map/dot_general | solution.py:385
  136.2 2.4 %collective-permute-start.22 = (bf16[128,1024]{1,0:T(8,128)(2,1)S(1)}, bf16[128,1024]{1,0:T(8,128)(2,1)S(1)}, u32[]{:S(2)}, u32[]{:S(2)}) collective-permute-start(bf16[128,1024]{1,0:T(8,128)(2,1)S(1)} %get-tuple-element.41), channel_id=1, source_target_pairs={{0,16},{1,24},{2,0},{3,8},{4,20},{5,28},{6,4},{7,12},{8,25},{9,17}... | collective-permute-start | bytes 786440 | tf_op jit(solution)/shard_map/ppermute | solution.py:379
  138.6 5.2 %collective-permute-start.21 = (bf16[128,1024]{1,0:T(8,128)(2,1)S(1)}, bf16[128,1024]{1,0:T(8,128)(2,1)S(1)}, u32[]{:S(2)}, u32[]{:S(2)}) collective-permute-start(bf16[128,1024]{1,0:T(8,128)(2,1)S(1)} %get-tuple-element.40), channel_id=1, source_target_pairs={{0,0},{1,8},{2,16},{3,24},{4,4},{5,12},{6,20},{7,28},{8,9},{9,1},{... | collective-permute-start | bytes 786440 | tf_op jit(solution)/shard_map/ppermute | solution.py:379
  143.9 2.1 %collective-permute-start.24 = (bf16[128,32]{1,0:T(8,128)(2,1)S(1)}, bf16[128,32]{1,0:T(8,128)(2,1)S(1)}, u32[]{:S(2)}, u32[]{:S(2)}) collective-permute-start(bf16[128,32]{1,0:T(8,128)(2,1)S(1)} %slice.176), channel_id=1, source_target_pairs={{0,2},{1,3},{2,0},{3,1},{4,6},{5,7},{6,4},{7,5},{8,10},{9,11},{10,... | collective-permute-start | bytes 24584 | tf_op jit(solution)/shard_map/ppermute | solution.py:261
  146.1 0.7 convert_reduce_fusion
  146.7 2.2 %collective-permute-done.24 = bf16[128,32]{1,0:T(8,128)(2,1)S(1)} collective-permute-done((bf16[128,32]{1,0:T(8,128)(2,1)S(1)}, bf16[128,32]{1,0:T(8,128)(2,1)S(1)}, u32[]{:S(2)}, u32[]{:S(2)}) %collective-permute-start.24) | collective-permute-done | bytes 8224 | tf_op jit(solution)/shard_map/ppermute | solution.py:261
  149.0 0.6 collective-permute-done.23
  149.5 4.5 %collective-permute-done.22 = bf16[128,1024]{1,0:T(8,128)(2,1)S(1)} collective-permute-done((bf16[128,1024]{1,0:T(8,128)(2,1)S(1)}, bf16[128,1024]{1,0:T(8,128)(2,1)S(1)}, u32[]{:S(2)}, u32[]{:S(2)}) %collective-permute-start.22) | collective-permute-done | bytes 262176 | tf_op jit(solution)/shard_map/ppermute | solution.py:379
  154.1 1.9 %collective-permute-done.21 = bf16[128,1024]{1,0:T(8,128)(2,1)S(1)} collective-permute-done((bf16[128,1024]{1,0:T(8,128)(2,1)S(1)}, bf16[128,1024]{1,0:T(8,128)(2,1)S(1)}, u32[]{:S(2)}, u32[]{:S(2)}) %collective-permute-start.21) | collective-permute-done | bytes 262176 | tf_op jit(solution)/shard_map/ppermute | solution.py:379
  156.0 1.0 add_convert_fusion
  (73 shorter events, 0.6 us)
Async XLA Ops:
  0.6 26.7 %copy-start.4 = (bf16[128,4096]{1,0:T(8,128)(2,1)S(1)}, bf16[128,4096]{1,0:T(8,128)(2,1)}, u32[]{:S(2)}) copy-start(bf16[128,4096]{1,0:T(8,128)(2,1)} %param.5) | copy-start | bytes 3145732
  2.2 25.7 %copy-start.15 = (f32[1024]{0:T(1024)S(1)}, f32[1024]{0:T(1024)}, u32[]{:S(2)}) copy-start(f32[1024]{0:T(1024)} %param.8) | copy-start | bytes 12292
  2.2 25.1 %all-to-all-start = ((bf16[8,32,512]{2,1,0:T(8,128)(2,1)}), bf16[8,32,512]{2,1,0:T(8,128)(2,1)S(1)}, u32[]{:S(2)}, u32[]{:S(2)}) async-start(bf16[8,32,512]{2,1,0:T(8,128)(2,1)} %broadcast_in_dim.4), calls=%async_computation | async-start | bytes 524288 | tf_op jit(solution)/shard_map/all_to_all | solution.py:266
  9.7 16.8 %collective-permute-start.3 = (bf16[128,512]{1,0:T(8,128)(2,1)S(1)}, bf16[128,512]{1,0:T(8,128)(2,1)S(1)}, u32[]{:S(2)}, u32[]{:S(2)}) collective-permute-start(bf16[128,512]{1,0:T(8,128)(2,1)S(1)} %get-tuple-element.37), channel_id=1, source_target_pairs={{0,16},{4,20},{8,24},{12,28},{16,0},{20,4},{24,8},{28,12},{1,17},{... | collective-permute-start | bytes 393224 | tf_op jit(solution)/shard_map/ppermute | solution.py:332
  12.2 14.4 %collective-permute-start.2 = (bf16[128,512]{1,0:T(8,128)(2,1)S(1)}, bf16[128,512]{1,0:T(8,128)(2,1)S(1)}, u32[]{:S(2)}, u32[]{:S(2)}) collective-permute-start(bf16[128,512]{1,0:T(8,128)(2,1)S(1)} %get-tuple-element.36), channel_id=1, source_target_pairs={{0,24},{4,28},{8,16},{12,20},{16,8},{20,12},{24,0},{28,4},{1,25},{... | collective-permute-start | bytes 393224 | tf_op jit(solution)/shard_map/ppermute | solution.py:332
  13.6 12.9 %collective-permute-start.1 = (bf16[128,512]{1,0:T(8,128)(2,1)S(1)}, bf16[128,512]{1,0:T(8,128)(2,1)S(1)}, u32[]{:S(2)}, u32[]{:S(2)}) collective-permute-start(bf16[128,512]{1,0:T(8,128)(2,1)S(1)} %get-tuple-element.35), channel_id=1, source_target_pairs={{0,8},{4,12},{8,0},{12,4},{16,24},{20,28},{24,16},{28,20},{1,9},{5... | collective-permute-start | bytes 393224 | tf_op jit(solution)/shard_map/ppermute | solution.py:332
  13.6 35.2 %collective-permute-start = (bf16[512,1024]{1,0:T(8,128)(2,1)}, bf16[512,1024]{1,0:T(8,128)(2,1)}, u32[]{:S(2)}, u32[]{:S(2)}) collective-permute-start(bf16[512,1024]{1,0:T(8,128)(2,1)} %param.6), channel_id=1, source_target_pairs={{0,4},{4,0},{8,12},{12,8},{16,20},{20,16},{24,28},{28,24},{1,5},{5... | collective-permute-start | bytes 3145736 | tf_op jit(solution)/shard_map/ppermute | solution.py:332
  27.3 1.4 copy-start
  28.7 7.5 %copy-start.6 = (bf16[384,512]{1,0:T(8,128)(2,1)S(1)}, bf16[384,512]{1,0:T(8,128)(2,1)}, u32[]{:S(2)}) copy-start(bf16[384,512]{1,0:T(8,128)(2,1)} %pad_maximum_fusion.5) | copy-start | bytes 1179652
  30.8 8.6 %collective-permute-start.7 = (bf16[32,1024]{1,0:T(8,128)(2,1)S(1)}, bf16[32,1024]{1,0:T(8,128)(2,1)S(1)}, u32[]{:S(2)}, u32[]{:S(2)}) collective-permute-start(bf16[32,1024]{1,0:T(8,128)(2,1)S(1)} %convert_element_type.69), channel_id=1, source_target_pairs={{12,0},{16,4},{20,8},{24,12},{28,16},{13,1},{17,5},{21,9},{25,13},... | collective-permute-start | bytes 196616 | tf_op jit(solution)/shard_map/ppermute | solution.py:232
  32.1 7.4 %collective-permute-start.6 = (bf16[32,1024]{1,0:T(8,128)(2,1)S(1)}, bf16[32,1024]{1,0:T(8,128)(2,1)S(1)}, u32[]{:S(2)}, u32[]{:S(2)}) collective-permute-start(bf16[32,1024]{1,0:T(8,128)(2,1)S(1)} %convert_element_type.69), channel_id=1, source_target_pairs={{8,0},{12,4},{16,8},{20,12},{24,16},{28,20},{9,1},{13,5},{17,9},{2... | collective-permute-start | bytes 196616 | tf_op jit(solution)/shard_map/ppermute | solution.py:232
  33.4 7.4 %collective-permute-start.5 = (bf16[32,1024]{1,0:T(8,128)(2,1)S(1)}, bf16[32,1024]{1,0:T(8,128)(2,1)S(1)}, u32[]{:S(2)}, u32[]{:S(2)}) collective-permute-start(bf16[32,1024]{1,0:T(8,128)(2,1)S(1)} %convert_element_type.69), channel_id=1, source_target_pairs={{4,0},{8,4},{12,8},{16,12},{20,16},{24,20},{28,24},{5,1},{9,5},{13... | collective-permute-start | bytes 196616 | tf_op jit(solution)/shard_map/ppermute | solution.py:232
  36.2 12.5 %collective-permute-start.4 = (bf16[384,512]{1,0:T(8,128)(2,1)S(1)}, bf16[384,512]{1,0:T(8,128)(2,1)S(1)}, u32[]{:S(2)}, u32[]{:S(2)}) collective-permute-start(bf16[384,512]{1,0:T(8,128)(2,1)S(1)} %copy-done.6), channel_id=1, source_target_pairs={{0,1},{1,0},{2,3},{3,2},{4,5},{5,4},{6,7},{7,6},{8,9},{9,8},{10,11... | collective-permute-start | bytes 1179656 | tf_op jit(solution)/shard_map/ppermute | solution.py:332
  40.8 7.9 %collective-permute-start.8 = (bf16[16,1024]{1,0:T(8,128)(2,1)S(1)}, bf16[16,1024]{1,0:T(8,128)(2,1)S(1)}, u32[]{:S(2)}, u32[]{:S(2)}) collective-permute-start(bf16[16,1024]{1,0:T(8,128)(2,1)S(1)} %get-tuple-element.31), channel_id=1, source_target_pairs={{16,0},{20,4},{24,8},{28,12},{17,1},{21,5},{25,9},{29,13},{18,2},{... | collective-permute-start | bytes 98312 | tf_op jit(solution)/shard_map/ppermute | solution.py:232
  48.7 2.1 %copy-start.1 = (bf16[512,1024]{1,0:T(8,128)(2,1)S(1)}, bf16[512,1024]{1,0:T(8,128)(2,1)}, u32[]{:S(2)}) copy-start(bf16[512,1024]{1,0:T(8,128)(2,1)} %param.6) | copy-start | bytes 3145732
  48.8 3.3 %copy-start.7 = (bf16[384,512]{1,0:T(8,128)(2,1)}, bf16[384,512]{1,0:T(8,128)(2,1)S(1)}, u32[]{:S(2)}) copy-start(bf16[384,512]{1,0:T(8,128)(2,1)S(1)} %get-tuple-element.39) | copy-start | bytes 1179652
  48.9 3.3 %copy-start.8 = (bf16[384,512]{1,0:T(8,128)(2,1)}, bf16[384,512]{1,0:T(8,128)(2,1)S(1)}, u32[]{:S(2)}) copy-start(bf16[384,512]{1,0:T(8,128)(2,1)S(1)} %get-tuple-element.38) | copy-start | bytes 1179652
  52.1 11.6 %collective-permute-start.9 = (bf16[256,1024]{1,0:T(8,128)(2,1)}, bf16[256,1024]{1,0:T(8,128)(2,1)}, u32[]{:S(2)}, u32[]{:S(2)}) collective-permute-start(bf16[256,1024]{1,0:T(8,128)(2,1)} %fusion.2), channel_id=1, source_target_pairs={{0,8},{4,12},{8,0},{12,4},{16,24},{20,28},{24,16},{28,20},{1,9},{5... | collective-permute-start | bytes 1572872 | tf_op jit(solution)/shard_map/ppermute | solution.py:332
  54.9 12.3 %collective-permute-start.14 = (bf16[32,1024]{1,0:T(8,128)(2,1)}, bf16[32,1024]{1,0:T(8,128)(2,1)}, u32[]{:S(2)}, u32[]{:S(2)}) collective-permute-start(bf16[32,1024]{1,0:T(8,128)(2,1)} %get-tuple-element.43), channel_id=1, source_target_pairs={{0,3},{1,0},{2,1},{3,2},{4,7},{5,4},{6,5},{7,6},{8,11},{9,8},{10,9... | collective-permute-start | bytes 196616 | tf_op jit(solution)/shard_map/ppermute | solution.py:261
  54.9 12.3 %collective-permute-start.13 = (bf16[32,1024]{1,0:T(8,128)(2,1)S(1)}, bf16[32,1024]{1,0:T(8,128)(2,1)}, u32[]{:S(2)}, u32[]{:S(2)}) collective-permute-start(bf16[32,1024]{1,0:T(8,128)(2,1)S(1)} %get-tuple-element.44), channel_id=1, source_target_pairs={{0,2},{1,3},{2,0},{3,1},{4,6},{5,7},{6,4},{7,5},{8,10},{9,11},{10,... | collective-permute-start | bytes 196616 | tf_op jit(solution)/shard_map/ppermute | solution.py:261
  55.4 8.4 %copy-start.2 = (bf16[512,1024]{1,0:T(8,128)(2,1)S(1)}, bf16[512,1024]{1,0:T(8,128)(2,1)}, u32[]{:S(2)}) copy-start(bf16[512,1024]{1,0:T(8,128)(2,1)} %param.6) | copy-start | bytes 3145732
  55.4 11.8 %collective-permute-start.12 = (bf16[32,1024]{1,0:T(8,128)(2,1)S(1)}, bf16[32,1024]{1,0:T(8,128)(2,1)}, u32[]{:S(2)}, u32[]{:S(2)}) collective-permute-start(bf16[32,1024]{1,0:T(8,128)(2,1)S(1)} %get-tuple-element.45), channel_id=1, source_target_pairs={{0,1},{1,2},{2,3},{3,0},{4,5},{5,6},{6,7},{7,4},{8,9},{9,10},{10,1... | collective-permute-start | bytes 196616 | tf_op jit(solution)/shard_map/ppermute | solution.py:261
  65.1 20.4 %collective-permute-start.10 = (bf16[128,1024]{1,0:T(8,128)(2,1)S(1)}, bf16[128,1024]{1,0:T(8,128)(2,1)}, u32[]{:S(2)}, u32[]{:S(2)}) collective-permute-start(bf16[128,1024]{1,0:T(8,128)(2,1)S(1)} %fusion.6), channel_id=1, source_target_pairs={{0,16},{4,20},{8,24},{12,28},{16,0},{20,4},{24,8},{28,12},{1,17},{... | collective-permute-start | bytes 786440 | tf_op jit(solution)/shard_map/ppermute | solution.py:332
  68.8 22.1 %collective-permute-start.11 = (bf16[128,1024]{1,0:T(8,128)(2,1)}, bf16[128,1024]{1,0:T(8,128)(2,1)S(1)}, u32[]{:S(2)}, u32[]{:S(2)}) collective-permute-start(bf16[128,1024]{1,0:T(8,128)(2,1)} %get-tuple-element.20), channel_id=1, source_target_pairs={{0,16},{4,20},{8,24},{12,28},{16,0},{20,4},{24,8},{28,12},{1,17},{... | collective-permute-start | bytes 786440 | tf_op jit(solution)/shard_map/ppermute | solution.py:332
  87.3 17.8 %copy-start.3 = (bf16[512,1024]{1,0:T(8,128)(2,1)S(1)}, bf16[512,1024]{1,0:T(8,128)(2,1)}, u32[]{:S(2)}) copy-start(bf16[512,1024]{1,0:T(8,128)(2,1)} %param.6) | copy-start | bytes 3145732
  92.8 8.2 %collective-permute-start.17 = (bf16[32,1024]{1,0:T(8,128)(2,1)S(1)}, bf16[32,1024]{1,0:T(8,128)(2,1)S(1)}, u32[]{:S(2)}, u32[]{:S(2)}) collective-permute-start(bf16[32,1024]{1,0:T(8,128)(2,1)S(1)} %pad_maximum_fusion.7), channel_id=1, source_target_pairs={{0,12},{4,16},{8,20},{12,24},{16,28},{1,13},{5,17},{9,21},{13,25},... | collective-permute-start | bytes 196616 | tf_op jit(solution)/shard_map/ppermute | solution.py:232
  94.1 6.9 %collective-permute-start.16 = (bf16[32,1024]{1,0:T(8,128)(2,1)S(1)}, bf16[32,1024]{1,0:T(8,128)(2,1)S(1)}, u32[]{:S(2)}, u32[]{:S(2)}) collective-permute-start(bf16[32,1024]{1,0:T(8,128)(2,1)S(1)} %pad_maximum_fusion.7), channel_id=1, source_target_pairs={{0,8},{4,12},{8,16},{12,20},{16,24},{20,28},{1,9},{5,13},{9,17},{1... | collective-permute-start | bytes 196616 | tf_op jit(solution)/shard_map/ppermute | solution.py:232
  96.6 6.9 %collective-permute-start.15 = (bf16[32,1024]{1,0:T(8,128)(2,1)S(1)}, bf16[32,1024]{1,0:T(8,128)(2,1)S(1)}, u32[]{:S(2)}, u32[]{:S(2)}) collective-permute-start(bf16[32,1024]{1,0:T(8,128)(2,1)S(1)} %pad_maximum_fusion.7), channel_id=1, source_target_pairs={{0,4},{4,8},{8,12},{12,16},{16,20},{20,24},{24,28},{1,5},{5,9},{9,... | collective-permute-start | bytes 196616 | tf_op jit(solution)/shard_map/ppermute | solution.py:232
  100.9 12.2 %copy-start.14 = (bf16[256,1024]{1,0:T(8,128)(2,1)}, bf16[256,1024]{1,0:T(8,128)(2,1)S(1)}, u32[]{:S(2)}) copy-start(bf16[256,1024]{1,0:T(8,128)(2,1)S(1)} %constant_dynamic-update-slice_fusion) | copy-start | bytes 1572868
  100.9 12.2 %collective-permute-start.19 = (bf16[256,1024]{1,0:T(8,128)(2,1)S(1)}, bf16[256,1024]{1,0:T(8,128)(2,1)S(1)}, u32[]{:S(2)}, u32[]{:S(2)}) collective-permute-start(bf16[256,1024]{1,0:T(8,128)(2,1)S(1)} %constant_dynamic-update-slice_fusion), channel_id=1, source_target_pairs={{0,8},{4,12},{8,0},{12,4},{16,24},{20,28},{24,16},{28,20},{1,9},{5... | collective-permute-start | bytes 1572872 | tf_op jit(solution)/shard_map/ppermute | solution.py:332
  103.5 9.4 %collective-permute-start.18 = (bf16[16,1024]{1,0:T(8,128)(2,1)S(1)}, bf16[16,1024]{1,0:T(8,128)(2,1)S(1)}, u32[]{:S(2)}, u32[]{:S(2)}) collective-permute-start(bf16[16,1024]{1,0:T(8,128)(2,1)S(1)} %get-tuple-element.29), channel_id=1, source_target_pairs={{0,16},{4,20},{8,24},{12,28},{1,17},{5,21},{9,25},{13,29},{2,18},{... | collective-permute-start | bytes 98312 | tf_op jit(solution)/shard_map/ppermute | solution.py:232
  106.5 8.4 %copy-start.9 = (bf16[512,1024]{1,0:T(8,128)(2,1)}, bf16[512,1024]{1,0:T(8,128)(2,1)S(1)}, u32[]{:S(2)}) copy-start(bf16[512,1024]{1,0:T(8,128)(2,1)S(1)} %get-tuple-element.33) | copy-start | bytes 3145732
  106.5 8.4 %copy-start.11 = (bf16[512,1024]{1,0:T(8,128)(2,1)}, bf16[512,1024]{1,0:T(8,128)(2,1)S(1)}, u32[]{:S(2)}) copy-start(bf16[512,1024]{1,0:T(8,128)(2,1)S(1)} %get-tuple-element.34) | copy-start | bytes 3145732
  113.1 1.8 %copy-start.16 = (bf16[256,1024]{1,0:T(8,128)(2,1)}, bf16[256,1024]{1,0:T(8,128)(2,1)S(1)}, u32[]{:S(2)}) copy-start(bf16[256,1024]{1,0:T(8,128)(2,1)S(1)} %collective-permute-done.19) | copy-start | bytes 1572868
  114.9 19.0 %collective-permute-start.20 = (f32[256,1024]{1,0:T(8,128)}, f32[256,1024]{1,0:T(8,128)}, u32[]{:S(2)}, u32[]{:S(2)}) collective-permute-start(f32[256,1024]{1,0:T(8,128)} %fusion), channel_id=1, source_target_pairs={{0,1},{1,0},{2,3},{3,2},{4,5},{5,4},{6,7},{7,6},{8,9},{9,8},{10,11... | collective-permute-start | bytes 3145736 | tf_op jit(solution)/shard_map/ppermute | solution.py:332
  115.0 11.9 %copy-start.5 = (bf16[128,4096]{1,0:T(8,128)(2,1)S(1)}, bf16[128,4096]{1,0:T(8,128)(2,1)}, u32[]{:S(2)}) copy-start(bf16[128,4096]{1,0:T(8,128)(2,1)} %param.5) | copy-start | bytes 3145732
  126.9 7.0 %copy-start.10 = (bf16[512,1024]{1,0:T(8,128)(2,1)S(1)}, bf16[512,1024]{1,0:T(8,128)(2,1)}, u32[]{:S(2)}) copy-start(bf16[512,1024]{1,0:T(8,128)(2,1)} %copy-done.9) | copy-start | bytes 3145732
  126.9 7.0 %copy-start.12 = (bf16[512,1024]{1,0:T(8,128)(2,1)S(1)}, bf16[512,1024]{1,0:T(8,128)(2,1)}, u32[]{:S(2)}) copy-start(bf16[512,1024]{1,0:T(8,128)(2,1)} %copy-done.11) | copy-start | bytes 3145732
  128.0 18.1 %all-to-all-start.1 = ((bf16[8,32,512]{2,1,0:T(8,128)(2,1)}), bf16[8,32,512]{2,1,0:T(8,128)(2,1)S(1)}, u32[]{:S(2)}, u32[]{:S(2)}) async-start(bf16[8,32,512]{2,1,0:T(8,128)(2,1)} %bitcast.30), calls=%async_computation.1 | async-start | bytes 524288 | tf_op jit(solution)/shard_map/all_to_all | solution.py:456
  133.9 22.1 %copy-start.13 = (bf16[128,1024]{1,0:T(8,128)(2,1)S(1)}, bf16[128,1024]{1,0:T(8,128)(2,1)}, u32[]{:S(2)}) copy-start(bf16[128,1024]{1,0:T(8,128)(2,1)} %pad_maximum_fusion.6) | copy-start | bytes 786436
  136.2 17.9 %collective-permute-start.22 = (bf16[128,1024]{1,0:T(8,128)(2,1)S(1)}, bf16[128,1024]{1,0:T(8,128)(2,1)S(1)}, u32[]{:S(2)}, u32[]{:S(2)}) collective-permute-start(bf16[128,1024]{1,0:T(8,128)(2,1)S(1)} %get-tuple-element.41), channel_id=1, source_target_pairs={{0,16},{1,24},{2,0},{3,8},{4,20},{5,28},{6,4},{7,12},{8,25},{9,17}... | collective-permute-start | bytes 786440 | tf_op jit(solution)/shard_map/ppermute | solution.py:379
  138.6 17.4 %collective-permute-start.21 = (bf16[128,1024]{1,0:T(8,128)(2,1)S(1)}, bf16[128,1024]{1,0:T(8,128)(2,1)S(1)}, u32[]{:S(2)}, u32[]{:S(2)}) collective-permute-start(bf16[128,1024]{1,0:T(8,128)(2,1)S(1)} %get-tuple-element.40), channel_id=1, source_target_pairs={{0,0},{1,8},{2,16},{3,24},{4,4},{5,12},{6,20},{7,28},{8,9},{9,1},{... | collective-permute-start | bytes 786440 | tf_op jit(solution)/shard_map/ppermute | solution.py:379
  143.8 2.9 %collective-permute-start.25 = (bf16[128,32]{1,0:T(8,128)(2,1)S(1)}, bf16[128,32]{1,0:T(8,128)(2,1)S(1)}, u32[]{:S(2)}, u32[]{:S(2)}) collective-permute-start(bf16[128,32]{1,0:T(8,128)(2,1)S(1)} %slice.176), channel_id=1, source_target_pairs={{0,3},{1,0},{2,1},{3,2},{4,7},{5,4},{6,5},{7,6},{8,11},{9,8},{10,9... | collective-permute-start | bytes 24584 | tf_op jit(solution)/shard_map/ppermute | solution.py:261
  143.9 5.1 %collective-permute-start.24 = (bf16[128,32]{1,0:T(8,128)(2,1)S(1)}, bf16[128,32]{1,0:T(8,128)(2,1)S(1)}, u32[]{:S(2)}, u32[]{:S(2)}) collective-permute-start(bf16[128,32]{1,0:T(8,128)(2,1)S(1)} %slice.176), channel_id=1, source_target_pairs={{0,2},{1,3},{2,0},{3,1},{4,6},{5,7},{6,4},{7,5},{8,10},{9,11},{10,... | collective-permute-start | bytes 24584 | tf_op jit(solution)/shard_map/ppermute | solution.py:261
  146.1 3.5 %collective-permute-start.23 = (bf16[128,32]{1,0:T(8,128)(2,1)S(1)}, bf16[128,32]{1,0:T(8,128)(2,1)S(1)}, u32[]{:S(2)}, u32[]{:S(2)}) collective-permute-start(bf16[128,32]{1,0:T(8,128)(2,1)S(1)} %slice.176), channel_id=1, source_target_pairs={{0,1},{1,2},{2,3},{3,0},{4,5},{5,6},{6,7},{7,4},{8,9},{9,10},{10,1... | collective-permute-start | bytes 24584 | tf_op jit(solution)/shard_map/ppermute | solution.py:261

commit v4 on v3

--- a/solution.py
+++ b/solution.py
@@ -232,16 +232,18 @@
     return lax.ppermute(value, axis, pairs)
 
 
-def carried(pair, sign):
+def carried(pair, sign, early=None):
     count = lax.axis_size("seq")
     window, radix = 1, 4
     total, decay = pair[:NS], pair[NS:]
-    inc, exc_total, exc_decay, ready = pair, None, None, None
+    inc, exc_total, exc_decay = pair, None, None
     while window < count:
         last = window * radix >= count
         if last and window * 2 >= count:
             inc = inc[:NS]
-        wire = ready = inc.astype(BF16)
+        wire = inc.astype(BF16)
+        if last and early is not None:
+            wire, early = lax.optimization_barrier((wire, early))
         for j in range(1, min(radix, -(-count // window))):
             far = shifted(wire, "seq", sign * window * j).astype(F32)
             far_total, far_decay = far[:NS], far[NS:]
@@ -253,7 +255,7 @@
                     exc_decay = exc_decay * far_decay
         inc = jnp.concatenate([total + decay * exc_total, decay * exc_decay], axis=0)
         window *= radix
-    return exc_total, ready
+    return exc_total, early
 
 
 def along_chan(value, by):
@@ -291,20 +293,20 @@
 
 class Gathered:
     def __init__(self, tokens, w_inner):
-        self.tokens = tokens
+        self.tokens, self.came = tokens, None
         self.full = lax.all_gather(w_inner, "seq", axis=0, tiled=True)
 
-    def partials(self, before):
-        return jnp.dot(self.tokens, self.full, preferred_element_type=F32), None, None, before
-
-    def inner(self, near, far, beside):
-        return near
-
-    def grads(self, grad):
-        return None
-
-    def grad_tokens(self, grad, far, after):
-        return scatter_sum_columns(dot_t(grad, self.full))
+    def partials(self):
+        return None, None
+
+    def spread(self, beside, rest):
+        return jnp.dot(self.tokens, self.full, preferred_element_type=F32), None, None
+
+    def inner(self, near, far, beside, grad):
+        return near, grad, grad
+
+    def grad_tokens(self, even, odd, before):
+        return scatter_sum_columns(dot_t(even, self.full)), before
 
 
 class Exchanged:
@@ -331,33 +333,33 @@
         pairs = [(i, i ^ mask) for i in range(lax.axis_size(axis))]
         return lax.ppermute(value, axis, pairs)
 
-    def partials(self, before):
-        def product(mine, other):
-            return jnp.dot(mine, self.w_mine, preferred_element_type=F32) + jnp.dot(
-                other, self.w_other, preferred_element_type=F32
-            )
-
+    def partials(self):
         partner = self.trade(self.came, "chan", 1)
         mine = jnp.where(self.first, self.came, partner)
         other = jnp.where(self.first, partner, self.came)
         two = 2 * self.count
-        beside = product(mine[:two], other[:two]).astype(BF16)
-        beside, before = lax.optimization_barrier((beside, before))
-        near = product(self.near_mine, self.near_other)
-        return near, product(mine[two:], other[two:]), self.trade(beside, "seq", 2), before
-
-    def inner(self, near, far, beside):
-        far = far + beside[self.count :].astype(F32)
-        return near + beside[: self.count].astype(F32) + self.trade(far.astype(BF16), "seq", 4).astype(F32)
-
-    def grads(self, grad):
-        return self.trade(grad, "seq", 4)
-
-    def grad_tokens(self, grad, far, after):
+        beside = self.product(mine[:two], other[:two]).astype(BF16)
+        return beside, (mine[two:], other[two:])
+
+    def product(self, mine, other):
+        return jnp.dot(mine, self.w_mine, preferred_element_type=F32) + jnp.dot(
+            other, self.w_other, preferred_element_type=F32
+        )
+
+    def spread(self, beside, rest):
+        near = self.product(self.near_mine, self.near_other)
+        return near, self.product(*rest), self.trade(beside, "seq", 2)
+
+    def inner(self, near, far, beside, grad):
+        wire = (far + beside[self.count :].astype(F32)).astype(BF16)
+        wire, far_grad = lax.optimization_barrier((wire, self.trade(grad, "seq", 4)))
+        even = jnp.concatenate([grad, far_grad], axis=0)
+        odd = self.trade(even, "seq", 2)
+        total = near + beside[: self.count].astype(F32) + self.trade(wire, "seq", 4).astype(F32)
+        return total, even, odd
+
+    def grad_tokens(self, even, odd, before):
         chans = lax.axis_size("chan")
-        even = jnp.concatenate([grad, far], axis=0)
-        odd = self.trade(even, "seq", 2)
-        odd, after = lax.optimization_barrier((odd, after))
         keep = jnp.where(self.first, even, odd)
         give = jnp.where(self.first, odd, even)
         one, two = self.w_mine, self.w_other
@@ -366,6 +368,7 @@
         )
         kept = dot_t(keep, full) + self.trade(dot_t(give, full), "chan", 1)
         pieces = kept.astype(BF16).reshape(2, self.count, -1)
+        pieces, before = lax.optimization_barrier((pieces, before))
         y = lax.axis_index("chan") // 2
         total = None
         for m in range(2):
@@ -378,7 +381,7 @@
             ]
             piece = lax.ppermute(piece, ("seq", "chan"), route).astype(F32)
             total = piece if total is None else total + piece
-        return total
+        return total, before
 
 
 def dot_t(left, right):
@@ -415,27 +418,24 @@
         ins=["kq", "rows", "rows16"], outs=["pair"], scratch=[rows_f],
         args=(spread, eps, grad_out), work=4,
     )
-    if short:
-        pair, plan.came = lax.optimization_barrier((pair, plan.came))
-    end_adjoint, _ = carried(pair, -1)
-    near, far, beside, end_adjoint = plan.partials(end_adjoint)
+    end_adjoint, plan.came = carried(pair, -1, plan.came)
+    beside, rest = plan.partials()
+    near, far, beside = plan.spread(beside, rest)
     adjoints, inner_grad = run(
         adjoint_kernel,
         ins=["kq", "rows", "rows16", "state"], outs=["states", "rows16"], scratch=[rows_f, rows_f],
         args=(spread, eps, grad_out, end_adjoint), work=10,
     )
     beside, _ = lax.optimization_barrier((beside, inner_grad))
-    far_grad = plan.grads(inner_grad)
-    inner, far_grad, kq_rows = lax.optimization_barrier(
-        (plan.inner(near, far, beside), far_grad, jnp.concatenate(kq_rows, axis=0))
-    )
+    inner, even, odd = plan.inner(near, far, beside, inner_grad)
+    inner, kq_rows = lax.optimization_barrier((inner, jnp.concatenate(kq_rows, axis=0)))
     (alone_end,) = run(
         state_total_kernel,
         ins=["kq", "rows", "rows"], outs=["state"], scratch=[],
         args=(spread, eps, inner), work=4,
     )
-    start_state, _ = carried(jnp.concatenate([alone_end, pair[NS:]], axis=0), 1)
-    tokens_sum = plan.grad_tokens(inner_grad, far_grad, start_state)
+    start_state, odd = carried(jnp.concatenate([alone_end, pair[NS:]], axis=0), 1, odd)
+    tokens_sum, start_state = plan.grad_tokens(even, odd, start_state)
     acc = pltpu.VMEM((count, NS, LANES), F32)
     mixed, kq_grad = run(
         mixer_kernel,

time: 158 us -> 153 us (0.968)
  the two profiles are of different devices: /device:TPU:6 before, /device:TPU:0 now
where the time goes in v4:
time: 153 us; the launch traced here: 152 us
  starting transfers between devices  54.7 us (36%)
  waiting for transfers between devices  45.7 us (30%)
  Pallas kernels  21.2 us (14%)
  matrix products  14.5 us (9%)
  other arithmetic  8.44 us (6%)
  local copies, waits for them, and re-layouts  5.77 us (4%)
    ppermute x10, waiting for transfers between devices, trade(): return lax.ppermute(value, axis, pairs)  26.3 us
    pallas_call x4, Pallas kernels, call(): pl.pallas_call(kernel, grid=(width // block,), in_specs=[spec(kind) for k...  21.2 us
    ppermute x8, starting transfers between devices, shifted(): return lax.ppermute(value, axis, pairs)  17.1 us
    ppermute x10, starting transfers between devices, trade(): return lax.ppermute(value, axis, pairs)  14.8 us
    ppermute x8, waiting for transfers between devices, shifted(): return lax.ppermute(value, axis, pairs)  11.2 us
    ppermute x2, starting transfers between devices, grad_tokens(): piece = lax.ppermute(piece, ('seq', 'chan'), route).astype(F32)  8.45 us
    all_to_all x1, starting transfers between devices, gathered(): return lax.all_to_all(copies, axis, 0, 0, tiled=True)  7.25 us
    dot_general x3, matrix products, dot_t(): lax.dot_general(left, right, (((1,), (1,)), ((), ())), preferred_element_...  5.01 us
  transfers between devices with their start and end apart: 28, of which 12 were waited for; matrix products, arithmetic and copies ran while one was open for 14% of the time, Pallas kernels for 14%

profile of v4, /device:TPU:0, one launch (start us, length us, event | category | flops | bytes accessed | tf_op | source)
XLA Modules:
  0.0 151.6 jit_solution(4090181282083686946)
XLA Ops:
  0.7 1.6 %broadcast_in_dim.4 = bf16[8,32,512]{2,1,0:T(8,128)(2,1)} broadcast(bf16[32,512]{1,0:T(8,128)(2,1)} %bitcast.37), dimensions={1,2} | broadcast | bytes 294912 | tf_op jit(solution)/shard_map/broadcast_in_dim | solution.py:267
  2.2 7.3 %all-to-all-start = ((bf16[8,32,512]{2,1,0:T(8,128)(2,1)}), bf16[8,32,512]{2,1,0:T(8,128)(2,1)S(1)}, u32[]{:S(2)}, u32[]{:S(2)}) async-start(bf16[8,32,512]{2,1,0:T(8,128)(2,1)} %broadcast_in_dim.4), calls=%async_computation | async-start | bytes 524288 | tf_op jit(solution)/shard_map/all_to_all | solution.py:268
  9.5 1.7 %constant_dynamic-slice_fusion.6 = (bf16[128,512]{1,0:T(8,128)(2,1)}, bf16[128,512]{1,0:T(8,128)(2,1)}, bf16[128,512]{1,0:T(8,128)(2,1)S(1)}) fusion(bf16[128,4096]{1,0:T(8,128)(2,1)} %param.5, s32[]{:T(128)S(6)} %select_n.114, s32[]{:T(128)S(6)} %select_n.115, s32[]{:T(128)S(6)} %select_n.116), kind=kLoop, calls=%fused_computation.78 | loop fusion | bytes 786444 | tf_op jit(solution)/shard_map/dynamic_slice | solution.py:330
  11.2 2.0 %collective-permute-start.4 = (bf16[128,512]{1,0:T(8,128)(2,1)}, bf16[128,512]{1,0:T(8,128)(2,1)S(1)}, u32[]{:S(2)}, u32[]{:S(2)}) collective-permute-start(bf16[128,512]{1,0:T(8,128)(2,1)} %get-tuple-element.39), channel_id=1, source_target_pairs={{0,8},{4,12},{8,0},{12,4},{16,24},{20,28},{24,16},{28,20},{1,9},{5... | collective-permute-start | bytes 393224 | tf_op jit(solution)/shard_map/ppermute | solution.py:334
  13.2 2.4 %collective-permute-start.5 = (bf16[128,512]{1,0:T(8,128)(2,1)}, bf16[128,512]{1,0:T(8,128)(2,1)}, u32[]{:S(2)}, u32[]{:S(2)}) collective-permute-start(bf16[128,512]{1,0:T(8,128)(2,1)} %get-tuple-element.40), channel_id=1, source_target_pairs={{0,24},{4,28},{8,16},{12,20},{16,8},{20,12},{24,0},{28,4},{1,25},{... | collective-permute-start | bytes 393224 | tf_op jit(solution)/shard_map/ppermute | solution.py:334
  15.6 1.5 collective-permute-start
  17.1 2.5 %all-to-all-done = bf16[8,32,512]{2,1,0:T(8,128)(2,1)S(1)} async-done(((bf16[8,32,512]{2,1,0:T(8,128)(2,1)}), bf16[8,32,512]{2,1,0:T(8,128)(2,1)S(1)}, u32[]{:S(2)}, u32[]{:S(2)}) %all-to-all-start) | async-done | bytes 262176 | tf_op jit(solution)/shard_map/all_to_all | solution.py:268
  19.6 0.4 fusion.48
  20.1 0.1 add_divide_fusion.eps
  20.3 0.1 copy.11
  20.4 0.6 broadcast_in_dim.5.kq
  21.0 2.1 %shard_map.76 = f32[32,1024]{1,0:T(8,128)S(1)} custom-call(f32[128,32,128]{2,1,0:T(8,128)S(1)} %broadcast_in_dim.5.kq, f32[128,1024]{1,0:T(8,128)S(1)} %add_divide_fusion.eps, bf16[128,1024]{1,0:T(8,128)(2,1)S(1)} %copy-done), custom_call_target="tpu_custom_call" | custom-call | flops 8388608 | bytes 1024 | tf_op jit(solution)/shard_map/pallas_call | solution.py:213
  23.1 1.3 collective-permute-start.3
  24.4 1.3 collective-permute-start.2
  25.7 1.3 collective-permute-start.1
  27.0 5.1 %collective-permute-done.6 = bf16[128,512]{1,0:T(8,128)(2,1)} collective-permute-done((bf16[128,512]{1,0:T(8,128)(2,1)S(1)}, bf16[128,512]{1,0:T(8,128)(2,1)}, u32[]{:S(2)}, u32[]{:S(2)}) %collective-permute-start.6) | collective-permute-done | bytes 131104 | tf_op jit(solution)/shard_map/ppermute | solution.py:334
  32.1 1.7 %pad_maximum_fusion.5 = bf16[384,512]{1,0:T(8,128)(2,1)} fusion(bf16[128,512]{1,0:T(8,128)(2,1)} %collective-permute-done.6, bf16[128,512]{1,0:T(8,128)(2,1)} %collective-permute-done.5, bf16[128,512]{1,0:T(8,128)(2,1)S(1)} %collective-permute-done.4), kind=kLoop, calls=%fused_computation.22 | loop fusion | flops 1179648 | bytes 786432 | tf_op jit(solution)/shard_map/concatenate | solution.py:325
  33.9 8.9 %collective-permute-done.1 = bf16[32,1024]{1,0:T(8,128)(2,1)S(1)} collective-permute-done((bf16[32,1024]{1,0:T(8,128)(2,1)S(1)}, bf16[32,1024]{1,0:T(8,128)(2,1)S(1)}, u32[]{:S(2)}, u32[]{:S(2)}) %collective-permute-start.1) | collective-permute-done | bytes 65568 | tf_op jit(solution)/shard_map/ppermute | solution.py:232
  42.8 0.7 fusion.28
  43.5 1.6 %fusion.18 = f32[128,1024]{1,0:T(8,128)S(1)} fusion(bf16[512,1024]{1,0:T(8,128)(2,1)} %param.6, bf16[128,4096]{1,0:T(8,128)(2,1)} %param.5, s32[]{:T(128)S(6)} %select_n.109), kind=kOutput, calls=%fused_computation.36 | convolution fusion | flops 134217728 | bytes 1703940 | tf_op jit(solution)/shard_map/dot_general | solution.py:345
  45.1 1.4 collective-permute-start.9
  46.5 1.2 broadcast_select_fusion.3
  47.7 1.7 %fusion.11 = f32[256,1024]{1,0:T(8,128)S(1)} fusion(bf16[512,1024]{1,0:T(8,128)(2,1)} %collective-permute-done, bf16[384,512]{1,0:T(8,128)(2,1)S(1)} %get-tuple-element.43), kind=kOutput, calls=%fused_computation.26 | convolution fusion | flops 268435456 | bytes 2359296 | tf_op jit(solution)/shard_map/dot_general | solution.py:345
  49.4 0.4 fusion.2
  49.9 1.8 %collective-permute-start.8 = (bf16[256,1024]{1,0:T(8,128)(2,1)S(1)}, bf16[256,1024]{1,0:T(8,128)(2,1)S(1)}, u32[]{:S(2)}, u32[]{:S(2)}) collective-permute-start(bf16[256,1024]{1,0:T(8,128)(2,1)S(1)} %fusion.2), channel_id=1, source_target_pairs={{0,8},{4,12},{8,0},{12,4},{16,24},{20,28},{24,16},{28,20},{1,9},{5... | collective-permute-start | bytes 1572872 | tf_op jit(solution)/shard_map/ppermute | solution.py:334
  51.7 1.4 collective-permute-start.14
  53.1 0.5 collective-permute-start.13
  53.7 5.4 %shard_map.77 = (f32[128,16,1024]{2,1,0:T(8,128)}, bf16[128,1024]{1,0:T(8,128)(2,1)S(1)}) custom-call(f32[128,32,128]{2,1,0:T(8,128)S(1)} %broadcast_in_dim.5.kq, f32[128,1024]{1,0:T(8,128)S(1)} %add_divide_fusion.eps, bf16[128,1024]{1,0:T(8,128)(2,1)S(1)} %copy-done, f32[16,1024]{1,0:T(8,128)S(1)} %fusion.25.start), custom_call_target="tpu_custom_call" | custom-call | flops 20971520 | bytes 1024 | tf_op jit(solution)/shard_map/pallas_call | solution.py:213
  59.1 3.4 %collective-permute-start.10 = (bf16[128,1024]{1,0:T(8,128)(2,1)S(1)}, bf16[128,1024]{1,0:T(8,128)(2,1)S(1)}, u32[]{:S(2)}, u32[]{:S(2)}) collective-permute-start(bf16[128,1024]{1,0:T(8,128)(2,1)S(1)} %get-tuple-element.20), channel_id=1, source_target_pairs={{0,16},{4,20},{8,24},{12,28},{16,0},{20,4},{24,8},{28,12},{1,17},{... | collective-permute-start | bytes 786440 | tf_op jit(solution)/shard_map/ppermute | solution.py:334
  62.5 1.5 %fusion.14 = f32[128,1024]{1,0:T(8,128)S(1)} fusion(bf16[512,1024]{1,0:T(8,128)(2,1)} %collective-permute-done, bf16[384,512]{1,0:T(8,128)(2,1)S(1)} %get-tuple-element.43), kind=kOutput, calls=%fused_computation.32 | convolution fusion | flops 134217728 | bytes 1703936 | tf_op jit(solution)/shard_map/dot_general | solution.py:345
  64.0 2.7 %collective-permute-done.8 = bf16[256,1024]{1,0:T(8,128)(2,1)S(1)} collective-permute-done((bf16[256,1024]{1,0:T(8,128)(2,1)S(1)}, bf16[256,1024]{1,0:T(8,128)(2,1)S(1)}, u32[]{:S(2)}, u32[]{:S(2)}) %collective-permute-start.8) | collective-permute-done | bytes 524320 | tf_op jit(solution)/shard_map/ppermute | solution.py:334
  66.7 0.3 fusion.6
  67.0 7.6 %collective-permute-done.10 = bf16[128,1024]{1,0:T(8,128)(2,1)S(1)} collective-permute-done((bf16[128,1024]{1,0:T(8,128)(2,1)S(1)}, bf16[128,1024]{1,0:T(8,128)(2,1)S(1)}, u32[]{:S(2)}, u32[]{:S(2)}) %collective-permute-start.10) | collective-permute-done | bytes 262176 | tf_op jit(solution)/shard_map/ppermute | solution.py:334
  74.6 0.7 pad_maximum_fusion.6
  75.4 3.6 %collective-permute-start.18 = (bf16[256,1024]{1,0:T(8,128)(2,1)S(1)}, bf16[256,1024]{1,0:T(8,128)(2,1)S(1)}, u32[]{:S(2)}, u32[]{:S(2)}) collective-permute-start(bf16[256,1024]{1,0:T(8,128)(2,1)S(1)} %constant_dynamic-update-slice_fusion), channel_id=1, source_target_pairs={{0,8},{4,12},{8,0},{12,4},{16,24},{20,28},{24,16},{28,20},{1,9},{5... | collective-permute-start | bytes 1572872 | tf_op jit(solution)/shard_map/ppermute | solution.py:334
  79.0 11.0 %collective-permute-done.11 = bf16[128,1024]{1,0:T(8,128)(2,1)S(1)} collective-permute-done((bf16[128,1024]{1,0:T(8,128)(2,1)S(1)}, bf16[128,1024]{1,0:T(8,128)(2,1)S(1)}, u32[]{:S(2)}, u32[]{:S(2)}) %collective-permute-start.11) | collective-permute-done | bytes 262176 | tf_op jit(solution)/shard_map/ppermute | solution.py:334
  90.0 1.6 %fusion.4.inner = f32[128,1024]{1,0:T(8,128)S(1)} fusion(f32[128,1024]{1,0:T(8,128)S(1)} %fusion.18, bf16[512,1024]{1,0:T(8,128)(2,1)} %collective-permute-done, bf16[128,1024]{1,0:T(8,128)(2,1)S(1)} %collective-permute-done.11, bf16[256,1024]{1,0:T(8,128)(2,1)S(1)} %collective-permute-done.8, bf16[128,4096]{1,0:T(8,128)(2,1)} %param.5, s32[]{:T(128)S(6)} %select_n.110), kind=kOutput, calls=%fused_computation.10 | convolution fusion | flops 134873088 | bytes 2752516 | tf_op jit(solution)/shard_map/dot_general | solution.py:345
  91.6 1.9 %shard_map.78 = f32[16,1024]{1,0:T(8,128)S(1)} custom-call(f32[128,32,128]{2,1,0:T(8,128)S(1)} %broadcast_in_dim.5.kq, f32[128,1024]{1,0:T(8,128)S(1)} %add_divide_fusion.eps, f32[128,1024]{1,0:T(8,128)S(1)} %fusion.4.inner), custom_call_target="tpu_custom_call" | custom-call | flops 8388608 | bytes 1024 | tf_op jit(solution)/shard_map/pallas_call | solution.py:213
  93.5 1.3 collective-permute-start.17
  94.8 1.5 %collective-permute-start.16 = (bf16[32,1024]{1,0:T(8,128)(2,1)S(1)}, bf16[32,1024]{1,0:T(8,128)(2,1)S(1)}, u32[]{:S(2)}, u32[]{:S(2)}) collective-permute-start(bf16[32,1024]{1,0:T(8,128)(2,1)S(1)} %pad_maximum_fusion.7), channel_id=1, source_target_pairs={{0,8},{4,12},{8,16},{12,20},{16,24},{20,28},{1,9},{5,13},{9,17},{1... | collective-permute-start | bytes 196616 | tf_op jit(solution)/shard_map/ppermute | solution.py:232
  96.4 6.1 %collective-permute-start.15 = (bf16[32,1024]{1,0:T(8,128)(2,1)S(1)}, bf16[32,1024]{1,0:T(8,128)(2,1)S(1)}, u32[]{:S(2)}, u32[]{:S(2)}) collective-permute-start(bf16[32,1024]{1,0:T(8,128)(2,1)S(1)} %pad_maximum_fusion.7), channel_id=1, source_target_pairs={{0,4},{4,8},{8,12},{12,16},{16,20},{20,24},{24,28},{1,5},{5,9},{9,... | collective-permute-start | bytes 196616 | tf_op jit(solution)/shard_map/ppermute | solution.py:232
  102.5 1.4 broadcast_select_fusion.1
  104.0 0.4 collective-permute-done.15
  104.4 0.9 add_convert_fusion.1
  105.3 1.8 %fusion = f32[256,1024]{1,0:T(8,128)} fusion(bf16[512,1024]{1,0:T(8,128)(2,1)S(1)} %get-tuple-element.38, bf16[512,1024]{1,0:T(8,128)(2,1)S(1)} %get-tuple-element.37, bf16[256,1024]{1,0:T(8,128)(2,1)S(1)} %collective-permute-done.18, bf16[256,1024]{1,0:T(8,128)(2,1)S(1)} %constant_dynamic-update-slice_fusion, pred[]{:T(512)S(6)} %eq.14), kind=kOutput, calls=%fused_computation.4 | convolution fusion | flops 541327360 | bytes 4194305 | tf_op jit(solution)/shard_map/dot_general | solution.py:388
  107.1 0.1 collective-permute-start.19
  107.2 2.9 %collective-permute-start.20 = (bf16[16,1024]{1,0:T(8,128)(2,1)}, bf16[16,1024]{1,0:T(8,128)(2,1)S(1)}, u32[]{:S(2)}, u32[]{:S(2)}) collective-permute-start(bf16[16,1024]{1,0:T(8,128)(2,1)} %get-tuple-element.27), channel_id=1, source_target_pairs={{0,16},{4,20},{8,24},{12,28},{1,17},{5,21},{9,25},{13,29},{2,18},{... | collective-permute-start | bytes 98312 | tf_op jit(solution)/shard_map/ppermute | solution.py:232
  110.2 1.9 %collective-permute-done.20 = bf16[16,1024]{1,0:T(8,128)(2,1)S(1)} collective-permute-done((bf16[16,1024]{1,0:T(8,128)(2,1)}, bf16[16,1024]{1,0:T(8,128)(2,1)S(1)}, u32[]{:S(2)}, u32[]{:S(2)}) %collective-permute-start.20) | collective-permute-done | bytes 32800 | tf_op jit(solution)/shard_map/ppermute | solution.py:232
  112.0 0.9 fusion.21.start
  113.0 2.8 %fusion.1 = bf16[256,1024]{1,0:T(8,128)(2,1)S(1)} fusion(f32[256,1024]{1,0:T(8,128)} %collective-permute-done.19, bf16[512,1024]{1,0:T(8,128)(2,1)} %copy-done.5, bf16[512,1024]{1,0:T(8,128)(2,1)} %copy-done.4, bf16[256,1024]{1,0:T(8,128)(2,1)} %copy-done.14, bf16[256,1024]{1,0:T(8,128)(2,1)} %copy-done.16, pred[]{:T(512)S(6)} %eq.14), kind=kOutput, calls=%fused_computation.5 | convolution fusion | flops 541851648 | bytes 4718593 | tf_op jit(solution)/shard_map/dot_general | solution.py:388
  115.8 0.8 dynamic-slice_bitcast_fusion.1
  116.6 3.6 %collective-permute-start.21 = (bf16[128,1024]{1,0:T(8,128)(2,1)}, bf16[128,1024]{1,0:T(8,128)(2,1)}, u32[]{:S(2)}, u32[]{:S(2)}) collective-permute-start(bf16[128,1024]{1,0:T(8,128)(2,1)} %get-tuple-element.44), channel_id=1, source_target_pairs={{0,0},{1,8},{2,16},{3,24},{4,4},{5,12},{6,20},{7,28},{8,9},{9,1},{... | collective-permute-start | bytes 786440 | tf_op jit(solution)/shard_map/ppermute | solution.py:382
  120.2 4.9 %collective-permute-start.22 = (bf16[128,1024]{1,0:T(8,128)(2,1)}, bf16[128,1024]{1,0:T(8,128)(2,1)}, u32[]{:S(2)}, u32[]{:S(2)}) collective-permute-start(bf16[128,1024]{1,0:T(8,128)(2,1)} %get-tuple-element.45), channel_id=1, source_target_pairs={{0,16},{1,24},{2,0},{3,8},{4,20},{5,28},{6,4},{7,12},{8,25},{9,17}... | collective-permute-start | bytes 786440 | tf_op jit(solution)/shard_map/ppermute | solution.py:382
  125.1 11.9 %shard_map.79 = (bf16[128,1024]{1,0:T(8,128)(2,1)}, f32[128,128]{1,0:T(8,128)S(1)}) custom-call(f32[128,32,128]{2,1,0:T(8,128)S(1)} %broadcast_in_dim.5.kq, f32[128,1024]{1,0:T(8,128)S(1)} %add_divide_fusion.eps, f32[128,1024]{1,0:T(8,128)S(1)} %fusion.4.inner, bf16[128,1024]{1,0:T(8,128)(2,1)S(1)} %copy-done, f32[128,16,1024]{2,1,0:T(8,128)} %get-tuple-element.24.adj_in, ...), custom_call_target="tpu_custom_call" | custom-call | flops 46137344 | bytes 1024 | tf_op jit(solution)/shard_map/pallas_call | solution.py:213
  136.9 0.3 convolution_convert_fusion
  137.2 0.7 copy.16
  138.0 3.6 %all-to-all-start.1 = ((bf16[8,32,512]{2,1,0:T(8,128)(2,1)}), bf16[8,32,512]{2,1,0:T(8,128)(2,1)S(1)}, u32[]{:S(2)}, u32[]{:S(2)}) async-start(bf16[8,32,512]{2,1,0:T(8,128)(2,1)} %bitcast.30), calls=%async_computation.1 | async-start | bytes 524288 | tf_op jit(solution)/shard_map/all_to_all | solution.py:456
  141.7 1.5 %collective-permute-start.24 = (bf16[128,32]{1,0:T(8,128)(2,1)S(1)}, bf16[128,32]{1,0:T(8,128)(2,1)S(1)}, u32[]{:S(2)}, u32[]{:S(2)}) collective-permute-start(bf16[128,32]{1,0:T(8,128)(2,1)S(1)} %slice.180), channel_id=1, source_target_pairs={{0,2},{1,3},{2,0},{3,1},{4,6},{5,7},{6,4},{7,5},{8,10},{9,11},{10,... | collective-permute-start | bytes 24584 | tf_op jit(solution)/shard_map/ppermute | solution.py:263
  143.2 0.1 collective-permute-done.25
  143.3 2.5 %collective-permute-done.24 = bf16[128,32]{1,0:T(8,128)(2,1)S(1)} collective-permute-done((bf16[128,32]{1,0:T(8,128)(2,1)S(1)}, bf16[128,32]{1,0:T(8,128)(2,1)S(1)}, u32[]{:S(2)}, u32[]{:S(2)}) %collective-permute-start.24) | collective-permute-done | bytes 8224 | tf_op jit(solution)/shard_map/ppermute | solution.py:263
  145.8 0.7 collective-permute-done.23
  146.6 2.0 %add_convert_fusion = bf16[128,1024]{1,0:T(8,128)(2,1)} fusion(bf16[128,1024]{1,0:T(8,128)(2,1)} %collective-permute-done.22, bf16[128,1024]{1,0:T(8,128)(2,1)} %collective-permute-done.21, bf16[128,1024]{1,0:T(8,128)(2,1)S(1)} %copy-done.6, bf16[128,32]{1,0:T(8,128)(2,1)S(1)} %collective-permute-done.25, bf16[128,32]{1,0:T(8,128)(2,1)S(1)} %collective-permute-done.24, ...), kind=kOutput, calls=%fused_computation.16 | convolution fusion | flops 34340864 | bytes 1081344 | tf_op jit(solution)/shard_map/dot_general | solution.py:450
  148.6 2.3 %all-to-all-done.1 = bf16[8,32,512]{2,1,0:T(8,128)(2,1)S(1)} async-done(((bf16[8,32,512]{2,1,0:T(8,128)(2,1)}), bf16[8,32,512]{2,1,0:T(8,128)(2,1)S(1)}, u32[]{:S(2)}, u32[]{:S(2)}) %all-to-all-start.1) | async-done | bytes 262176 | tf_op jit(solution)/shard_map/all_to_all | solution.py:456
  150.9 0.7 convert_reduce_fusion
  (73 shorter events, 0.4 us)
Async XLA Ops:
  0.6 19.0 %copy-start.2 = (bf16[128,4096]{1,0:T(8,128)(2,1)S(1)}, bf16[128,4096]{1,0:T(8,128)(2,1)}, u32[]{:S(2)}) copy-start(bf16[128,4096]{1,0:T(8,128)(2,1)} %param.5) | copy-start | bytes 3145732
  0.6 19.5 %copy-start.15 = (f32[1024]{0:T(1024)S(1)}, f32[1024]{0:T(1024)}, u32[]{:S(2)}) copy-start(f32[1024]{0:T(1024)} %param.8) | copy-start | bytes 12292
  2.2 17.3 %all-to-all-start = ((bf16[8,32,512]{2,1,0:T(8,128)(2,1)}), bf16[8,32,512]{2,1,0:T(8,128)(2,1)S(1)}, u32[]{:S(2)}, u32[]{:S(2)}) async-start(bf16[8,32,512]{2,1,0:T(8,128)(2,1)} %broadcast_in_dim.4), calls=%async_computation | async-start | bytes 524288 | tf_op jit(solution)/shard_map/all_to_all | solution.py:268
  11.2 13.1 %collective-permute-start.4 = (bf16[128,512]{1,0:T(8,128)(2,1)}, bf16[128,512]{1,0:T(8,128)(2,1)S(1)}, u32[]{:S(2)}, u32[]{:S(2)}) collective-permute-start(bf16[128,512]{1,0:T(8,128)(2,1)} %get-tuple-element.39), channel_id=1, source_target_pairs={{0,8},{4,12},{8,0},{12,4},{16,24},{20,28},{24,16},{28,20},{1,9},{5... | collective-permute-start | bytes 393224 | tf_op jit(solution)/shard_map/ppermute | solution.py:334
  13.2 12.4 %collective-permute-start.5 = (bf16[128,512]{1,0:T(8,128)(2,1)}, bf16[128,512]{1,0:T(8,128)(2,1)}, u32[]{:S(2)}, u32[]{:S(2)}) collective-permute-start(bf16[128,512]{1,0:T(8,128)(2,1)} %get-tuple-element.40), channel_id=1, source_target_pairs={{0,24},{4,28},{8,16},{12,20},{16,8},{20,12},{24,0},{28,4},{1,25},{... | collective-permute-start | bytes 393224 | tf_op jit(solution)/shard_map/ppermute | solution.py:334
  15.6 16.5 %collective-permute-start.6 = (bf16[128,512]{1,0:T(8,128)(2,1)S(1)}, bf16[128,512]{1,0:T(8,128)(2,1)}, u32[]{:S(2)}, u32[]{:S(2)}) collective-permute-start(bf16[128,512]{1,0:T(8,128)(2,1)S(1)} %get-tuple-element.41), channel_id=1, source_target_pairs={{0,16},{4,20},{8,24},{12,28},{16,0},{20,4},{24,8},{28,12},{1,17},{... | collective-permute-start | bytes 393224 | tf_op jit(solution)/shard_map/ppermute | solution.py:334
  15.6 32.1 %collective-permute-start = (bf16[512,1024]{1,0:T(8,128)(2,1)}, bf16[512,1024]{1,0:T(8,128)(2,1)}, u32[]{:S(2)}, u32[]{:S(2)}) collective-permute-start(bf16[512,1024]{1,0:T(8,128)(2,1)} %param.6), channel_id=1, source_target_pairs={{0,4},{4,0},{8,12},{12,8},{16,20},{20,16},{24,28},{28,24},{1,5},{5... | collective-permute-start | bytes 3145736 | tf_op jit(solution)/shard_map/ppermute | solution.py:334
  19.6 1.4 copy-start
  23.1 10.8 %collective-permute-start.3 = (bf16[32,1024]{1,0:T(8,128)(2,1)S(1)}, bf16[32,1024]{1,0:T(8,128)(2,1)S(1)}, u32[]{:S(2)}, u32[]{:S(2)}) collective-permute-start(bf16[32,1024]{1,0:T(8,128)(2,1)S(1)} %convert_element_type.68), channel_id=1, source_target_pairs={{12,0},{16,4},{20,8},{24,12},{28,16},{13,1},{17,5},{21,9},{25,13},... | collective-permute-start | bytes 196616 | tf_op jit(solution)/shard_map/ppermute | solution.py:232
  24.4 9.5 %collective-permute-start.2 = (bf16[32,1024]{1,0:T(8,128)(2,1)S(1)}, bf16[32,1024]{1,0:T(8,128)(2,1)S(1)}, u32[]{:S(2)}, u32[]{:S(2)}) collective-permute-start(bf16[32,1024]{1,0:T(8,128)(2,1)S(1)} %convert_element_type.68), channel_id=1, source_target_pairs={{8,0},{12,4},{16,8},{20,12},{24,16},{28,20},{9,1},{13,5},{17,9},{2... | collective-permute-start | bytes 196616 | tf_op jit(solution)/shard_map/ppermute | solution.py:232
  25.7 17.1 %collective-permute-start.1 = (bf16[32,1024]{1,0:T(8,128)(2,1)S(1)}, bf16[32,1024]{1,0:T(8,128)(2,1)S(1)}, u32[]{:S(2)}, u32[]{:S(2)}) collective-permute-start(bf16[32,1024]{1,0:T(8,128)(2,1)S(1)} %convert_element_type.68), channel_id=1, source_target_pairs={{4,0},{8,4},{12,8},{16,12},{20,16},{24,20},{28,24},{5,1},{9,5},{13... | collective-permute-start | bytes 196616 | tf_op jit(solution)/shard_map/ppermute | solution.py:232
  33.8 9.0 %copy-start.9 = (f32[32,1024]{1,0:T(8,128)}, f32[32,1024]{1,0:T(8,128)S(1)}, u32[]{:S(2)}) copy-start(f32[32,1024]{1,0:T(8,128)S(1)} %convert_element_type.71) | copy-start | bytes 393220
  43.5 3.1 %collective-permute-start.7 = (bf16[384,512]{1,0:T(8,128)(2,1)}, bf16[384,512]{1,0:T(8,128)(2,1)}, u32[]{:S(2)}, u32[]{:S(2)}) collective-permute-start(bf16[384,512]{1,0:T(8,128)(2,1)} %pad_maximum_fusion.5), channel_id=1, source_target_pairs={{0,1},{1,0},{2,3},{3,2},{4,5},{5,4},{6,7},{7,6},{8,9},{9,8},{10,11... | collective-permute-start | bytes 1179656 | tf_op jit(solution)/shard_map/ppermute | solution.py:334
  45.1 4.3 %copy-start.1 = (bf16[512,1024]{1,0:T(8,128)(2,1)S(1)}, bf16[512,1024]{1,0:T(8,128)(2,1)}, u32[]{:S(2)}) copy-start(bf16[512,1024]{1,0:T(8,128)(2,1)} %param.6) | copy-start | bytes 3145732
  45.1 8.5 %collective-permute-start.9 = (bf16[16,1024]{1,0:T(8,128)(2,1)}, bf16[16,1024]{1,0:T(8,128)(2,1)S(1)}, u32[]{:S(2)}, u32[]{:S(2)}) collective-permute-start(bf16[16,1024]{1,0:T(8,128)(2,1)} %get-tuple-element.19), channel_id=1, source_target_pairs={{16,0},{20,4},{24,8},{28,12},{17,1},{21,5},{25,9},{29,13},{18,2},{... | collective-permute-start | bytes 98312 | tf_op jit(solution)/shard_map/ppermute | solution.py:232
  49.4 4.2 %copy-start.10 = (f32[32,1024]{1,0:T(8,128)S(1)}, f32[32,1024]{1,0:T(8,128)}, u32[]{:S(2)}) copy-start(f32[32,1024]{1,0:T(8,128)} %copy-done.9) | copy-start | bytes 393220
  49.4 4.2 %copy-start.12 = (f32[16,1024]{1,0:T(8,128)S(1)}, f32[16,1024]{1,0:T(8,128)}, u32[]{:S(2)}) copy-start(f32[16,1024]{1,0:T(8,128)} %get-tuple-element.36) | copy-start | bytes 196612
  49.9 16.8 %collective-permute-start.8 = (bf16[256,1024]{1,0:T(8,128)(2,1)S(1)}, bf16[256,1024]{1,0:T(8,128)(2,1)S(1)}, u32[]{:S(2)}, u32[]{:S(2)}) collective-permute-start(bf16[256,1024]{1,0:T(8,128)(2,1)S(1)} %fusion.2), channel_id=1, source_target_pairs={{0,8},{4,12},{8,0},{12,4},{16,24},{20,28},{24,16},{28,20},{1,9},{5... | collective-permute-start | bytes 1572872 | tf_op jit(solution)/shard_map/ppermute | solution.py:334
  51.7 22.9 %collective-permute-start.14 = (bf16[32,1024]{1,0:T(8,128)(2,1)S(1)}, bf16[32,1024]{1,0:T(8,128)(2,1)S(1)}, u32[]{:S(2)}, u32[]{:S(2)}) collective-permute-start(bf16[32,1024]{1,0:T(8,128)(2,1)S(1)} %get-tuple-element.47), channel_id=1, source_target_pairs={{0,3},{1,0},{2,1},{3,2},{4,7},{5,4},{6,5},{7,6},{8,11},{9,8},{10,9... | collective-permute-start | bytes 196616 | tf_op jit(solution)/shard_map/ppermute | solution.py:263
  53.1 21.5 %collective-permute-start.13 = (bf16[32,1024]{1,0:T(8,128)(2,1)S(1)}, bf16[32,1024]{1,0:T(8,128)(2,1)S(1)}, u32[]{:S(2)}, u32[]{:S(2)}) collective-permute-start(bf16[32,1024]{1,0:T(8,128)(2,1)S(1)} %get-tuple-element.48), channel_id=1, source_target_pairs={{0,2},{1,3},{2,0},{3,1},{4,6},{5,7},{6,4},{7,5},{8,10},{9,11},{10,... | collective-permute-start | bytes 196616 | tf_op jit(solution)/shard_map/ppermute | solution.py:263
  53.6 21.0 %collective-permute-start.12 = (bf16[32,1024]{1,0:T(8,128)(2,1)S(1)}, bf16[32,1024]{1,0:T(8,128)(2,1)S(1)}, u32[]{:S(2)}, u32[]{:S(2)}) collective-permute-start(bf16[32,1024]{1,0:T(8,128)(2,1)S(1)} %get-tuple-element.49), channel_id=1, source_target_pairs={{0,1},{1,2},{2,3},{3,0},{4,5},{5,6},{6,7},{7,4},{8,9},{9,10},{10,1... | collective-permute-start | bytes 196616 | tf_op jit(solution)/shard_map/ppermute | solution.py:263
  59.1 15.5 %collective-permute-start.10 = (bf16[128,1024]{1,0:T(8,128)(2,1)S(1)}, bf16[128,1024]{1,0:T(8,128)(2,1)S(1)}, u32[]{:S(2)}, u32[]{:S(2)}) collective-permute-start(bf16[128,1024]{1,0:T(8,128)(2,1)S(1)} %get-tuple-element.20), channel_id=1, source_target_pairs={{0,16},{4,20},{8,24},{12,28},{16,0},{20,4},{24,8},{28,12},{1,17},{... | collective-permute-start | bytes 786440 | tf_op jit(solution)/shard_map/ppermute | solution.py:334
  74.6 15.4 %collective-permute-start.11 = (bf16[128,1024]{1,0:T(8,128)(2,1)S(1)}, bf16[128,1024]{1,0:T(8,128)(2,1)S(1)}, u32[]{:S(2)}, u32[]{:S(2)}) collective-permute-start(bf16[128,1024]{1,0:T(8,128)(2,1)S(1)} %fusion.6), channel_id=1, source_target_pairs={{0,16},{4,20},{8,24},{12,28},{16,0},{20,4},{24,8},{28,12},{1,17},{... | collective-permute-start | bytes 786440 | tf_op jit(solution)/shard_map/ppermute | solution.py:334
  75.4 29.9 %copy-start.14 = (bf16[256,1024]{1,0:T(8,128)(2,1)}, bf16[256,1024]{1,0:T(8,128)(2,1)S(1)}, u32[]{:S(2)}) copy-start(bf16[256,1024]{1,0:T(8,128)(2,1)S(1)} %constant_dynamic-update-slice_fusion) | copy-start | bytes 1572868
  75.4 29.9 %collective-permute-start.18 = (bf16[256,1024]{1,0:T(8,128)(2,1)S(1)}, bf16[256,1024]{1,0:T(8,128)(2,1)S(1)}, u32[]{:S(2)}, u32[]{:S(2)}) collective-permute-start(bf16[256,1024]{1,0:T(8,128)(2,1)S(1)} %constant_dynamic-update-slice_fusion), channel_id=1, source_target_pairs={{0,8},{4,12},{8,0},{12,4},{16,24},{20,28},{24,16},{28,20},{1,9},{5... | collective-permute-start | bytes 1572872 | tf_op jit(solution)/shard_map/ppermute | solution.py:334
  93.5 10.3 %collective-permute-start.17 = (bf16[32,1024]{1,0:T(8,128)(2,1)S(1)}, bf16[32,1024]{1,0:T(8,128)(2,1)S(1)}, u32[]{:S(2)}, u32[]{:S(2)}) collective-permute-start(bf16[32,1024]{1,0:T(8,128)(2,1)S(1)} %pad_maximum_fusion.7), channel_id=1, source_target_pairs={{0,12},{4,16},{8,20},{12,24},{16,28},{1,13},{5,17},{9,21},{13,25},... | collective-permute-start | bytes 196616 | tf_op jit(solution)/shard_map/ppermute | solution.py:232
  94.8 9.1 %collective-permute-start.16 = (bf16[32,1024]{1,0:T(8,128)(2,1)S(1)}, bf16[32,1024]{1,0:T(8,128)(2,1)S(1)}, u32[]{:S(2)}, u32[]{:S(2)}) collective-permute-start(bf16[32,1024]{1,0:T(8,128)(2,1)S(1)} %pad_maximum_fusion.7), channel_id=1, source_target_pairs={{0,8},{4,12},{8,16},{12,20},{16,24},{20,28},{1,9},{5,13},{9,17},{1... | collective-permute-start | bytes 196616 | tf_op jit(solution)/shard_map/ppermute | solution.py:232
  96.4 8.0 %collective-permute-start.15 = (bf16[32,1024]{1,0:T(8,128)(2,1)S(1)}, bf16[32,1024]{1,0:T(8,128)(2,1)S(1)}, u32[]{:S(2)}, u32[]{:S(2)}) collective-permute-start(bf16[32,1024]{1,0:T(8,128)(2,1)S(1)} %pad_maximum_fusion.7), channel_id=1, source_target_pairs={{0,4},{4,8},{8,12},{12,16},{16,20},{20,24},{24,28},{1,5},{5,9},{9,... | collective-permute-start | bytes 196616 | tf_op jit(solution)/shard_map/ppermute | solution.py:232
  103.8 3.3 %copy-start.4 = (bf16[512,1024]{1,0:T(8,128)(2,1)}, bf16[512,1024]{1,0:T(8,128)(2,1)S(1)}, u32[]{:S(2)}) copy-start(bf16[512,1024]{1,0:T(8,128)(2,1)S(1)} %get-tuple-element.37) | copy-start | bytes 3145732
  103.9 3.3 %copy-start.5 = (bf16[512,1024]{1,0:T(8,128)(2,1)}, bf16[512,1024]{1,0:T(8,128)(2,1)S(1)}, u32[]{:S(2)}) copy-start(bf16[512,1024]{1,0:T(8,128)(2,1)S(1)} %get-tuple-element.38) | copy-start | bytes 3145732
  103.9 3.2 %copy-start.11 = (f32[32,1024]{1,0:T(8,128)}, f32[32,1024]{1,0:T(8,128)S(1)}, u32[]{:S(2)}) copy-start(f32[32,1024]{1,0:T(8,128)S(1)} %convert_element_type.81) | copy-start | bytes 393220
  103.9 3.2 %copy-start.7 = (f32[32,1024]{1,0:T(8,128)}, f32[32,1024]{1,0:T(8,128)S(1)}, u32[]{:S(2)}) copy-start(f32[32,1024]{1,0:T(8,128)S(1)} %convert_element_type.80) | copy-start | bytes 393220
  104.4 2.8 %copy-start.8 = (f32[32,1024]{1,0:T(8,128)}, f32[32,1024]{1,0:T(8,128)S(1)}, u32[]{:S(2)}) copy-start(f32[32,1024]{1,0:T(8,128)S(1)} %convert_element_type.79) | copy-start | bytes 393220
  105.3 1.8 %copy-start.16 = (bf16[256,1024]{1,0:T(8,128)(2,1)}, bf16[256,1024]{1,0:T(8,128)(2,1)S(1)}, u32[]{:S(2)}) copy-start(bf16[256,1024]{1,0:T(8,128)(2,1)S(1)} %collective-permute-done.18) | copy-start | bytes 1572868
  105.3 6.7 %copy-start.13 = (f32[16,1024]{1,0:T(8,128)S(1)}, f32[16,1024]{1,0:T(8,128)}, u32[]{:S(2)}) copy-start(f32[16,1024]{1,0:T(8,128)} %get-tuple-element.34) | copy-start | bytes 196612
  107.1 5.8 %collective-permute-start.19 = (f32[256,1024]{1,0:T(8,128)}, f32[256,1024]{1,0:T(8,128)}, u32[]{:S(2)}, u32[]{:S(2)}) collective-permute-start(f32[256,1024]{1,0:T(8,128)} %fusion), channel_id=1, source_target_pairs={{0,1},{1,0},{2,3},{3,2},{4,5},{5,4},{6,7},{7,6},{8,9},{9,8},{10,11... | collective-permute-start | bytes 3145736 | tf_op jit(solution)/shard_map/ppermute | solution.py:334
  107.2 4.8 %collective-permute-start.20 = (bf16[16,1024]{1,0:T(8,128)(2,1)}, bf16[16,1024]{1,0:T(8,128)(2,1)S(1)}, u32[]{:S(2)}, u32[]{:S(2)}) collective-permute-start(bf16[16,1024]{1,0:T(8,128)(2,1)} %get-tuple-element.27), channel_id=1, source_target_pairs={{0,16},{4,20},{8,24},{12,28},{1,17},{5,21},{9,25},{13,29},{2,18},{... | collective-permute-start | bytes 98312 | tf_op jit(solution)/shard_map/ppermute | solution.py:232
  116.6 30.0 %collective-permute-start.21 = (bf16[128,1024]{1,0:T(8,128)(2,1)}, bf16[128,1024]{1,0:T(8,128)(2,1)}, u32[]{:S(2)}, u32[]{:S(2)}) collective-permute-start(bf16[128,1024]{1,0:T(8,128)(2,1)} %get-tuple-element.44), channel_id=1, source_target_pairs={{0,0},{1,8},{2,16},{3,24},{4,4},{5,12},{6,20},{7,28},{8,9},{9,1},{... | collective-permute-start | bytes 786440 | tf_op jit(solution)/shard_map/ppermute | solution.py:382
  120.2 26.4 %collective-permute-start.22 = (bf16[128,1024]{1,0:T(8,128)(2,1)}, bf16[128,1024]{1,0:T(8,128)(2,1)}, u32[]{:S(2)}, u32[]{:S(2)}) collective-permute-start(bf16[128,1024]{1,0:T(8,128)(2,1)} %get-tuple-element.45), channel_id=1, source_target_pairs={{0,16},{1,24},{2,0},{3,8},{4,20},{5,28},{6,4},{7,12},{8,25},{9,17}... | collective-permute-start | bytes 786440 | tf_op jit(solution)/shard_map/ppermute | solution.py:382
  125.1 11.9 %copy-start.3 = (bf16[128,4096]{1,0:T(8,128)(2,1)S(1)}, bf16[128,4096]{1,0:T(8,128)(2,1)}, u32[]{:S(2)}) copy-start(bf16[128,4096]{1,0:T(8,128)(2,1)} %param.5) | copy-start | bytes 3145732
  136.9 9.6 %copy-start.6 = (bf16[128,1024]{1,0:T(8,128)(2,1)S(1)}, bf16[128,1024]{1,0:T(8,128)(2,1)}, u32[]{:S(2)}) copy-start(bf16[128,1024]{1,0:T(8,128)(2,1)} %pad_maximum_fusion.6) | copy-start | bytes 786436
  138.0 12.9 %all-to-all-start.1 = ((bf16[8,32,512]{2,1,0:T(8,128)(2,1)}), bf16[8,32,512]{2,1,0:T(8,128)(2,1)S(1)}, u32[]{:S(2)}, u32[]{:S(2)}) async-start(bf16[8,32,512]{2,1,0:T(8,128)(2,1)} %bitcast.30), calls=%async_computation.1 | async-start | bytes 524288 | tf_op jit(solution)/shard_map/all_to_all | solution.py:456
  141.6 1.7 %collective-permute-start.25 = (bf16[128,32]{1,0:T(8,128)(2,1)S(1)}, bf16[128,32]{1,0:T(8,128)(2,1)S(1)}, u32[]{:S(2)}, u32[]{:S(2)}) collective-permute-start(bf16[128,32]{1,0:T(8,128)(2,1)S(1)} %slice.180), channel_id=1, source_target_pairs={{0,3},{1,0},{2,1},{3,2},{4,7},{5,4},{6,5},{7,6},{8,11},{9,8},{10,9... | collective-permute-start | bytes 24584 | tf_op jit(solution)/shard_map/ppermute | solution.py:263
  141.7 4.1 %collective-permute-start.24 = (bf16[128,32]{1,0:T(8,128)(2,1)S(1)}, bf16[128,32]{1,0:T(8,128)(2,1)S(1)}, u32[]{:S(2)}, u32[]{:S(2)}) collective-permute-start(bf16[128,32]{1,0:T(8,128)(2,1)S(1)} %slice.180), channel_id=1, source_target_pairs={{0,2},{1,3},{2,0},{3,1},{4,6},{5,7},{6,4},{7,5},{8,10},{9,11},{10,... | collective-permute-start | bytes 24584 | tf_op jit(solution)/shard_map/ppermute | solution.py:263
  143.2 3.3 %collective-permute-start.23 = (bf16[128,32]{1,0:T(8,128)(2,1)S(1)}, bf16[128,32]{1,0:T(8,128)(2,1)S(1)}, u32[]{:S(2)}, u32[]{:S(2)}) collective-permute-start(bf16[128,32]{1,0:T(8,128)(2,1)S(1)} %slice.180), channel_id=1, source_target_pairs={{0,1},{1,2},{2,3},{3,0},{4,5},{5,6},{6,7},{7,4},{8,9},{9,10},{10,1... | collective-permute-start | bytes 24584 | tf_op jit(solution)/shard_map/ppermute | solution.py:263

commit v5 on v4

--- a/solution.py
+++ b/solution.py
@@ -64,7 +64,7 @@
         pair_out[NS:, cols] = total
 
 
-def adjoint_kernel(kq, eps, cot, start, adj_out, grad_out, cot_f, grad_f):
+def inner_grad_kernel(kq, eps, cot, start, grad_out, cot_f, grad_f):
     tokens, width = eps.shape
     groups = lane_groups(width)
     to_float(cot, cot_f)
@@ -82,7 +82,6 @@
             new_lams = []
             for n, cols in enumerate(groups):
                 adj = queries * cots[n][j : j + 1] + lams[n]
-                adj_out[t, :, cols] = adj
                 grads[n] = place(grads[n], j, jnp.sum(adj * keys, axis=0, keepdims=True))
                 new_lams.append((1.0 - steps[n][j : j + 1] * square) * adj)
             lams = new_lams
@@ -92,6 +91,31 @@
 
     lax.fori_loop(0, tokens // UNROLL, block, tuple(start[:, cols] for cols in groups))
     grad_out[...] = grad_f[...].astype(BF16)
+
+
+def adjoint_kernel(kq, eps, cot, start, adj_out, cot_f):
+    tokens, width = eps.shape
+    groups = lane_groups(width)
+    to_float(cot, cot_f)
+
+    def block(i, lams):
+        first = pl.multiple_of(tokens - (i + 1) * UNROLL, UNROLL)
+        steps = [tile(eps, first, cols) for cols in groups]
+        cots = [tile(cot_f, first, cols) for cols in groups]
+        for j in reversed(range(UNROLL)):
+            t = first + j
+            keys = kq[t, :NS, :]
+            queries = kq[t, NS:, :]
+            square = keys * keys
+            new_lams = []
+            for n, cols in enumerate(groups):
+                adj = queries * cots[n][j : j + 1] + lams[n]
+                adj_out[t, :, cols] = adj
+                new_lams.append((1.0 - steps[n][j : j + 1] * square) * adj)
+            lams = new_lams
+        return tuple(lams)
+
+    lax.fori_loop(0, tokens // UNROLL, block, tuple(start[:, cols] for cols in groups))
 
 
 def state_total_kernel(kq, eps, inner, state_out):
@@ -118,7 +142,7 @@
         state_out[:, cols] = state
 
 
-def mixer_kernel(kq, eps, inner, cot, adj_in, start, mixed_out, gkq_out, cot_f, mixed_f, key_acc, query_acc):
+def kq_grad_kernel(kq, eps, inner, cot, adj_in, start, gkq_out, cot_f, key_acc, query_acc):
     tokens, width = eps.shape
     groups = lane_groups(width)
     to_float(cot, cot_f)
@@ -135,11 +159,9 @@
         pushes = [step * x for step, x in zip(steps, inners)]
         squares = [step * step for step in steps]
         cots = [tile(cot_f, first, cols) for cols in groups]
-        outs = [jnp.zeros((UNROLL, LANES), F32) for _ in groups]
         for j in range(UNROLL):
             t = first + j
             keys = kq[t, :NS, :]
-            queries = kq[t, NS:, :]
             square = keys * keys
             new_states = []
             key_sum = jnp.zeros((NS, LANES), F32)
@@ -154,18 +176,14 @@
                 step_sum = step_sum + squares[n][j : j + 1] * through_both
                 state = (1.0 - step * square) * states[n] + pushes[n][j : j + 1] * keys
                 query_sum = query_sum + state * cots[n][j : j + 1]
-                outs[n] = place(outs[n], j, jnp.sum(state * queries, axis=0, keepdims=True))
                 new_states.append(state)
             states = new_states
             through_step = jnp.sum(keys * step_sum, axis=0, keepdims=True)
             key_acc[t] += key_sum - 2.0 * keys * through_step
             query_acc[t] += query_sum
-        for n, cols in enumerate(groups):
-            mixed_f[pl.ds(first, UNROLL), cols] = outs[n]
         return tuple(states)
 
     lax.fori_loop(0, tokens // UNROLL, block, tuple(start[:, cols] for cols in groups))
-    mixed_out[...] = mixed_f[...].astype(BF16)
 
     @pl.when(pl.program_id(0) == pl.num_programs(0) - 1)
     def _():
@@ -186,6 +204,36 @@
             return jnp.sum(placed, axis=1)
 
         gkq_out[...] = spread(key_acc, 0) + spread(query_acc, NS)
+
+
+def mixer_kernel(kq, eps, inner, start, mixed_out, mixed_f):
+    tokens, width = eps.shape
+    groups = lane_groups(width)
+
+    def block(i, states):
+        first = pl.multiple_of(i * UNROLL, UNROLL)
+        steps = [tile(eps, first, cols) for cols in groups]
+        pushes = [tile(inner, first, cols) * step for cols, step in zip(groups, steps)]
+        outs = [jnp.zeros((UNROLL, LANES), F32) for _ in groups]
+        for j in range(UNROLL):
+            t = first + j
+            keys = kq[t, :NS, :]
+            queries = kq[t, NS:, :]
+            square = keys * keys
+            states = [
+                (1.0 - step[j : j + 1] * square) * state + push[j : j + 1] * keys
+                for state, step, push in zip(states, steps, pushes)
+            ]
+            outs = [
+                place(out, j, jnp.sum(state * queries, axis=0, keepdims=True))
+                for out, state in zip(outs, states)
+            ]
+        for out, cols in zip(outs, groups):
+            mixed_f[pl.ds(first, UNROLL), cols] = out
+        return tuple(states)
+
+    lax.fori_loop(0, tokens // UNROLL, block, tuple(start[:, cols] for cols in groups))
+    mixed_out[...] = mixed_f[...].astype(BF16)
 
 
 def call(kernel, tokens, width, block, ins, outs, scratch, args, work):
@@ -421,14 +469,22 @@
     end_adjoint, plan.came = carried(pair, -1, plan.came)
     beside, rest = plan.partials()
     near, far, beside = plan.spread(beside, rest)
-    adjoints, inner_grad = run(
+    (inner_grad,) = run(
+        inner_grad_kernel,
+        ins=["kq", "rows", "rows16", "state"], outs=["rows16"], scratch=[rows_f, rows_f],
+        args=(spread, eps, grad_out, end_adjoint), work=8,
+    )
+    (adjoints,) = run(
         adjoint_kernel,
-        ins=["kq", "rows", "rows16", "state"], outs=["states", "rows16"], scratch=[rows_f, rows_f],
-        args=(spread, eps, grad_out, end_adjoint), work=10,
+        ins=["kq", "rows", "rows16", "state"], outs=["states"], scratch=[rows_f],
+        args=(spread, eps, grad_out, lax.optimization_barrier((end_adjoint, inner_grad))[0]),
+        work=10,
     )
     beside, _ = lax.optimization_barrier((beside, inner_grad))
     inner, even, odd = plan.inner(near, far, beside, inner_grad)
-    inner, kq_rows = lax.optimization_barrier((inner, jnp.concatenate(kq_rows, axis=0)))
+    inner, kq_rows, adjoints = lax.optimization_barrier(
+        (inner, jnp.concatenate(kq_rows, axis=0), adjoints)
+    )
     (alone_end,) = run(
         state_total_kernel,
         ins=["kq", "rows", "rows"], outs=["state"], scratch=[],
@@ -437,11 +493,17 @@
     start_state, odd = carried(jnp.concatenate([alone_end, pair[NS:]], axis=0), 1, odd)
     tokens_sum, start_state = plan.grad_tokens(even, odd, start_state)
     acc = pltpu.VMEM((count, NS, LANES), F32)
-    mixed, kq_grad = run(
+    (kq_grad,) = run(
+        kq_grad_kernel,
+        ins=["kq", "rows", "rows", "rows16", "states", "state"], outs=["gkq"],
+        scratch=[rows_f, acc, acc],
+        args=(spread, eps, inner, grad_out, adjoints, start_state), work=22,
+    )
+    (mixed,) = run(
         mixer_kernel,
-        ins=["kq", "rows", "rows", "rows16", "states", "state"], outs=["rows16", "gkq"],
-        scratch=[rows_f, rows_f, acc, acc],
-        args=(spread, eps, inner, grad_out, adjoints, start_state), work=22,
+        ins=["kq", "rows", "rows", "state"], outs=["rows16"], scratch=[rows_f],
+        args=(spread, eps, inner, lax.optimization_barrier((start_state, kq_grad))[0]),
+        work=8,
     )
     kq_grad = kq_grad[:, :kq_cols].astype(BF16)
 

time: 153 us -> 149 us (0.974)
  waiting for transfers between devices: 45.7 us -> 34.4 us
  Pallas kernels: 21.2 us -> 25.4 us
  local copies, waits for them, and re-layouts: 5.77 us -> 8.4 us
    ppermute x10, waiting for transfers between devices: 26.3 us -> 19.2 us  [trade(): return lax.ppermute(value, axis, pairs)]
    pallas_call x4 -> x6, Pallas kernels: 21.2 us -> 25.4 us  [call(): pl.pallas_call(kernel, grid=(width // block,), in_specs=[spec(kind) for k...]
    ppermute x6, waiting for transfers between devices: 3.34 us -> 0.02 us  [along_chan(): lax.ppermute(value, 'chan', [(i, (i + by) % count) for i in range(count)])]
    unnamed x35 -> x54, local copies, waits for them, and re-layouts: 0.11 us -> 2.07 us
  transfers between devices with their start and end apart: 28 -> 28, of which waited for: 12 -> 10; matrix products, arithmetic and copies ran while one was open for 14% -> 16% of each run, Pallas kernels for 14% -> 17%
where the time goes in v5:
time: 149 us; the launch traced here: 148 us
  starting transfers between devices  53.9 us (36%)
  waiting for transfers between devices  34.4 us (23%)
  Pallas kernels  25.4 us (17%)
  matrix products  15.6 us (10%)
  other arithmetic  8.81 us (6%)
  local copies, waits for them, and re-layouts  8.4 us (6%)
    pallas_call x6, Pallas kernels, call(): pl.pallas_call(kernel, grid=(width // block,), in_specs=[spec(kind) for k...  25.4 us
    ppermute x10, waiting for transfers between devices, trade(): return lax.ppermute(value, axis, pairs)  19.2 us
    ppermute x8, starting transfers between devices, shifted(): return lax.ppermute(value, axis, pairs)  17.3 us
    ppermute x10, starting transfers between devices, trade(): return lax.ppermute(value, axis, pairs)  13.8 us
    ppermute x8, waiting for transfers between devices, shifted(): return lax.ppermute(value, axis, pairs)  11.2 us
    ppermute x2, starting transfers between devices, grad_tokens(): piece = lax.ppermute(piece, ('seq', 'chan'), route).astype(F32)  8.53 us
    all_to_all x1, starting transfers between devices, gathered(): return lax.all_to_all(copies, axis, 0, 0, tiled=True)  7.25 us
    dot_general x3, matrix products, dot_t(): lax.dot_general(left, right, (((1,), (1,)), ((), ())), preferred_element_...  5.02 us
  transfers between devices with their start and end apart: 28, of which 10 were waited for; matrix products, arithmetic and copies ran while one was open for 16% of the time, Pallas kernels for 17%

profile of v5, /device:TPU:0, one launch (start us, length us, event | category | flops | bytes accessed | tf_op | source)
XLA Modules:
  0.0 148.0 jit_solution(12437758258797244585)
XLA Ops:
  0.7 1.6 %broadcast_in_dim.4 = bf16[8,32,512]{2,1,0:T(8,128)(2,1)} broadcast(bf16[32,512]{1,0:T(8,128)(2,1)} %bitcast.38), dimensions={1,2} | broadcast | bytes 294912 | tf_op jit(solution)/shard_map/broadcast_in_dim | solution.py:315
  2.2 7.3 %all-to-all-start = ((bf16[8,32,512]{2,1,0:T(8,128)(2,1)}), bf16[8,32,512]{2,1,0:T(8,128)(2,1)S(1)}, u32[]{:S(2)}, u32[]{:S(2)}) async-start(bf16[8,32,512]{2,1,0:T(8,128)(2,1)} %broadcast_in_dim.4), calls=%async_computation | async-start | bytes 524288 | tf_op jit(solution)/shard_map/all_to_all | solution.py:316
  9.5 1.8 %constant_dynamic-slice_fusion.6 = (bf16[128,512]{1,0:T(8,128)(2,1)}, bf16[128,512]{1,0:T(8,128)(2,1)}, bf16[128,512]{1,0:T(8,128)(2,1)S(1)}) fusion(bf16[128,4096]{1,0:T(8,128)(2,1)} %param.5, s32[]{:T(128)S(6)} %select_n.114, s32[]{:T(128)S(6)} %select_n.115, s32[]{:T(128)S(6)} %select_n.116), kind=kLoop, calls=%fused_computation.77 | loop fusion | bytes 786444 | tf_op jit(solution)/shard_map/dynamic_slice | solution.py:378
  11.2 2.0 %collective-permute-start.4 = (bf16[128,512]{1,0:T(8,128)(2,1)}, bf16[128,512]{1,0:T(8,128)(2,1)S(1)}, u32[]{:S(2)}, u32[]{:S(2)}) collective-permute-start(bf16[128,512]{1,0:T(8,128)(2,1)} %get-tuple-element.37), channel_id=1, source_target_pairs={{0,8},{4,12},{8,0},{12,4},{16,24},{20,28},{24,16},{28,20},{1,9},{5... | collective-permute-start | bytes 393224 | tf_op jit(solution)/shard_map/ppermute | solution.py:382
  13.3 2.4 %collective-permute-start.5 = (bf16[128,512]{1,0:T(8,128)(2,1)}, bf16[128,512]{1,0:T(8,128)(2,1)}, u32[]{:S(2)}, u32[]{:S(2)}) collective-permute-start(bf16[128,512]{1,0:T(8,128)(2,1)} %get-tuple-element.38), channel_id=1, source_target_pairs={{0,24},{4,28},{8,16},{12,20},{16,8},{20,12},{24,0},{28,4},{1,25},{... | collective-permute-start | bytes 393224 | tf_op jit(solution)/shard_map/ppermute | solution.py:382
  15.6 1.5 collective-permute-start
  17.1 2.5 %all-to-all-done = bf16[8,32,512]{2,1,0:T(8,128)(2,1)S(1)} async-done(((bf16[8,32,512]{2,1,0:T(8,128)(2,1)}), bf16[8,32,512]{2,1,0:T(8,128)(2,1)S(1)}, u32[]{:S(2)}, u32[]{:S(2)}) %all-to-all-start) | async-done | bytes 262176 | tf_op jit(solution)/shard_map/all_to_all | solution.py:316
  19.6 0.4 fusion.48
  20.4 0.6 broadcast_in_dim.5.kq
  21.0 2.1 %shard_map.76 = f32[32,1024]{1,0:T(8,128)S(1)} custom-call(f32[128,32,128]{2,1,0:T(8,128)S(1)} %broadcast_in_dim.5.kq, f32[128,1024]{1,0:T(8,128)S(1)} %add_divide_fusion.eps, bf16[128,1024]{1,0:T(8,128)(2,1)S(1)} %copy-done), custom_call_target="tpu_custom_call" | custom-call | flops 8388608 | bytes 1024 | tf_op jit(solution)/shard_map/pallas_call | solution.py:261
  23.1 1.3 collective-permute-start.3
  24.4 1.3 collective-permute-start.2
  25.7 1.3 collective-permute-start.1
  27.0 5.1 %collective-permute-done.6 = bf16[128,512]{1,0:T(8,128)(2,1)} collective-permute-done((bf16[128,512]{1,0:T(8,128)(2,1)S(1)}, bf16[128,512]{1,0:T(8,128)(2,1)}, u32[]{:S(2)}, u32[]{:S(2)}) %collective-permute-start.6) | collective-permute-done | bytes 131104 | tf_op jit(solution)/shard_map/ppermute | solution.py:382
  32.1 1.8 %pad_maximum_fusion.6 = bf16[384,512]{1,0:T(8,128)(2,1)} fusion(bf16[128,512]{1,0:T(8,128)(2,1)} %collective-permute-done.6, bf16[128,512]{1,0:T(8,128)(2,1)} %collective-permute-done.5, bf16[128,512]{1,0:T(8,128)(2,1)S(1)} %collective-permute-done.4), kind=kLoop, calls=%fused_computation.23 | loop fusion | flops 1179648 | bytes 786432 | tf_op jit(solution)/shard_map/concatenate | solution.py:373
  33.9 8.9 %collective-permute-done.1 = bf16[32,1024]{1,0:T(8,128)(2,1)S(1)} collective-permute-done((bf16[32,1024]{1,0:T(8,128)(2,1)S(1)}, bf16[32,1024]{1,0:T(8,128)(2,1)S(1)}, u32[]{:S(2)}, u32[]{:S(2)}) %collective-permute-start.1) | collective-permute-done | bytes 65568 | tf_op jit(solution)/shard_map/ppermute | solution.py:280
  42.8 0.6 copy-done.11
  43.7 1.4 collective-permute-start.9
  45.1 0.5 collective-permute-done.7
  45.6 1.2 broadcast_select_fusion.3
  46.8 1.7 %fusion.11 = f32[256,1024]{1,0:T(8,128)S(1)} fusion(bf16[512,1024]{1,0:T(8,128)(2,1)} %collective-permute-done, bf16[384,512]{1,0:T(8,128)(2,1)S(1)} %get-tuple-element.41), kind=kOutput, calls=%fused_computation.27 | convolution fusion | flops 268435456 | bytes 2359296 | tf_op jit(solution)/shard_map/dot_general | solution.py:393
  48.5 0.4 fusion.2
  49.0 1.8 %collective-permute-start.8 = (bf16[256,1024]{1,0:T(8,128)(2,1)S(1)}, bf16[256,1024]{1,0:T(8,128)(2,1)S(1)}, u32[]{:S(2)}, u32[]{:S(2)}) collective-permute-start(bf16[256,1024]{1,0:T(8,128)(2,1)S(1)} %fusion.2), channel_id=1, source_target_pairs={{0,8},{4,12},{8,0},{12,4},{16,24},{20,28},{24,16},{28,20},{1,9},{5... | collective-permute-start | bytes 1572872 | tf_op jit(solution)/shard_map/ppermute | solution.py:382
  50.7 0.7 constant_dynamic-slice_fusion.3
  51.5 1.0 collective-permute-start.14
  52.4 0.5 collective-permute-start.13
  53.2 3.4 %shard_map.77 = bf16[128,1024]{1,0:T(8,128)(2,1)S(1)} custom-call(f32[128,32,128]{2,1,0:T(8,128)S(1)} %broadcast_in_dim.5.kq, f32[128,1024]{1,0:T(8,128)S(1)} %add_divide_fusion.eps, bf16[128,1024]{1,0:T(8,128)(2,1)S(1)} %copy-done, f32[16,1024]{1,0:T(8,128)S(1)} %fusion.25.start), custom_call_target="tpu_custom_call" | custom-call | flops 16777216 | bytes 1024 | tf_op jit(solution)/shard_map/pallas_call | solution.py:261
  56.6 3.1 %collective-permute-start.10 = (bf16[128,1024]{1,0:T(8,128)(2,1)S(1)}, bf16[128,1024]{1,0:T(8,128)(2,1)S(1)}, u32[]{:S(2)}, u32[]{:S(2)}) collective-permute-start(bf16[128,1024]{1,0:T(8,128)(2,1)S(1)} %shard_map.77), channel_id=1, source_target_pairs={{0,16},{4,20},{8,24},{12,28},{16,0},{20,4},{24,8},{28,12},{1,17},{... | collective-permute-start | bytes 786440 | tf_op jit(solution)/shard_map/ppermute | solution.py:382
  59.7 1.5 %fusion.14 = f32[128,1024]{1,0:T(8,128)S(1)} fusion(bf16[512,1024]{1,0:T(8,128)(2,1)} %collective-permute-done, bf16[384,512]{1,0:T(8,128)(2,1)S(1)} %get-tuple-element.41), kind=kOutput, calls=%fused_computation.33 | convolution fusion | flops 134217728 | bytes 1703936 | tf_op jit(solution)/shard_map/dot_general | solution.py:393
  61.3 6.0 %collective-permute-done.8 = bf16[256,1024]{1,0:T(8,128)(2,1)S(1)} collective-permute-done((bf16[256,1024]{1,0:T(8,128)(2,1)S(1)}, bf16[256,1024]{1,0:T(8,128)(2,1)S(1)}, u32[]{:S(2)}, u32[]{:S(2)}) %collective-permute-start.8) | collective-permute-done | bytes 524320 | tf_op jit(solution)/shard_map/ppermute | solution.py:382
  67.3 1.0 fusion.6
  68.3 3.6 %collective-permute-done.10 = bf16[128,1024]{1,0:T(8,128)(2,1)S(1)} collective-permute-done((bf16[128,1024]{1,0:T(8,128)(2,1)S(1)}, bf16[128,1024]{1,0:T(8,128)(2,1)S(1)}, u32[]{:S(2)}, u32[]{:S(2)}) %collective-permute-start.10) | collective-permute-done | bytes 262176 | tf_op jit(solution)/shard_map/ppermute | solution.py:382
  71.9 0.7 copy-done.21
  72.6 2.0 %fusion.18 = f32[128,1024]{1,0:T(8,128)} fusion(bf16[512,1024]{1,0:T(8,128)(2,1)S(1)} %copy-done.3, bf16[128,4096]{1,0:T(8,128)(2,1)} %param.5, s32[]{:T(128)S(6)} %select_n.109), kind=kOutput, calls=%fused_computation.37 | convolution fusion | flops 134217728 | bytes 1703940 | tf_op jit(solution)/shard_map/dot_general | solution.py:393
  74.7 1.6 %pad_maximum_fusion.7 = bf16[128,1024]{1,0:T(8,128)(2,1)} fusion(bf16[32,1024]{1,0:T(8,128)(2,1)} %collective-permute-done.14, bf16[32,1024]{1,0:T(8,128)(2,1)} %collective-permute-done.13, bf16[32,1024]{1,0:T(8,128)(2,1)} %collective-permute-done.12, bf16[32,1024]{1,0:T(8,128)(2,1)S(1)} %copy-done.23), kind=kLoop, calls=%fused_computation.30 | loop fusion | flops 1048576 | bytes 524288 | tf_op jit(solution)/shard_map/concatenate | solution.py:486
  76.3 4.3 %shard_map.78.adj_in = f32[128,16,1024]{2,1,0:T(8,128)} custom-call(f32[128,32,128]{2,1,0:T(8,128)S(1)} %broadcast_in_dim.5.kq, f32[128,1024]{1,0:T(8,128)S(1)} %add_divide_fusion.eps, bf16[128,1024]{1,0:T(8,128)(2,1)S(1)} %copy-done, f32[16,1024]{1,0:T(8,128)S(1)} %fusion.25.start), custom_call_target="tpu_custom_call" | custom-call | flops 20971520 | bytes 1024 | tf_op jit(solution)/shard_map/pallas_call | solution.py:261
  80.6 2.9 %collective-permute-start.18 = (bf16[256,1024]{1,0:T(8,128)(2,1)S(1)}, bf16[256,1024]{1,0:T(8,128)(2,1)S(1)}, u32[]{:S(2)}, u32[]{:S(2)}) collective-permute-start(bf16[256,1024]{1,0:T(8,128)(2,1)S(1)} %pad_maximum_fusion.5), channel_id=1, source_target_pairs={{0,8},{4,12},{8,0},{12,4},{16,24},{20,28},{24,16},{28,20},{1,9},{5... | collective-permute-start | bytes 1572872 | tf_op jit(solution)/shard_map/ppermute | solution.py:382
  83.5 4.0 %collective-permute-done.11 = bf16[128,1024]{1,0:T(8,128)(2,1)} collective-permute-done((bf16[128,1024]{1,0:T(8,128)(2,1)}, bf16[128,1024]{1,0:T(8,128)(2,1)}, u32[]{:S(2)}, u32[]{:S(2)}) %collective-permute-start.11) | collective-permute-done | bytes 262176 | tf_op jit(solution)/shard_map/ppermute | solution.py:382
  87.5 1.6 %fusion.4.inner = f32[128,1024]{1,0:T(8,128)S(1)} fusion(f32[128,1024]{1,0:T(8,128)S(1)} %copy-done.7, bf16[512,1024]{1,0:T(8,128)(2,1)} %collective-permute-done, bf16[128,1024]{1,0:T(8,128)(2,1)} %collective-permute-done.11, bf16[256,1024]{1,0:T(8,128)(2,1)S(1)} %copy-done.16, bf16[128,4096]{1,0:T(8,128)(2,1)} %param.5, s32[]{:T(128)S(6)} %select_n.110), kind=kOutput, calls=%fused_computation.10 | convolution fusion | flops 134873088 | bytes 2752516 | tf_op jit(solution)/shard_map/dot_general | solution.py:393
  89.2 1.9 %shard_map.79 = f32[16,1024]{1,0:T(8,128)S(1)} custom-call(f32[128,32,128]{2,1,0:T(8,128)S(1)} %broadcast_in_dim.5.kq, f32[128,1024]{1,0:T(8,128)S(1)} %add_divide_fusion.eps, f32[128,1024]{1,0:T(8,128)S(1)} %fusion.4.inner), custom_call_target="tpu_custom_call" | custom-call | flops 8388608 | bytes 1024 | tf_op jit(solution)/shard_map/pallas_call | solution.py:261
  91.1 1.4 collective-permute-start.17
  92.5 1.6 %collective-permute-start.16 = (bf16[32,1024]{1,0:T(8,128)(2,1)S(1)}, bf16[32,1024]{1,0:T(8,128)(2,1)S(1)}, u32[]{:S(2)}, u32[]{:S(2)}) collective-permute-start(bf16[32,1024]{1,0:T(8,128)(2,1)S(1)} %pad_maximum_fusion.8), channel_id=1, source_target_pairs={{0,8},{4,12},{8,16},{12,20},{16,24},{20,28},{1,9},{5,13},{9,17},{1... | collective-permute-start | bytes 196616 | tf_op jit(solution)/shard_map/ppermute | solution.py:280
  94.1 6.1 %collective-permute-start.15 = (bf16[32,1024]{1,0:T(8,128)(2,1)S(1)}, bf16[32,1024]{1,0:T(8,128)(2,1)S(1)}, u32[]{:S(2)}, u32[]{:S(2)}) collective-permute-start(bf16[32,1024]{1,0:T(8,128)(2,1)S(1)} %pad_maximum_fusion.8), channel_id=1, source_target_pairs={{0,4},{4,8},{8,12},{12,16},{16,20},{20,24},{24,28},{1,5},{5,9},{9,... | collective-permute-start | bytes 196616 | tf_op jit(solution)/shard_map/ppermute | solution.py:280
  100.2 1.4 broadcast_select_fusion.1
  101.7 0.4 collective-permute-done.15
  102.1 0.9 add_convert_fusion.1
  103.1 1.8 %fusion = f32[256,1024]{1,0:T(8,128)} fusion(bf16[512,1024]{1,0:T(8,128)(2,1)S(1)} %get-tuple-element.36, bf16[512,1024]{1,0:T(8,128)(2,1)S(1)} %get-tuple-element.35, bf16[256,1024]{1,0:T(8,128)(2,1)S(1)} %collective-permute-done.18, pred[]{:T(512)S(6)} %eq.14, bf16[128,1024]{1,0:T(8,128)(2,1)S(1)} %copy-done.22, bf16[128,1024]{1,0:T(8,128)(2,1)S(1)} %copy-done.2), kind=kOutput, calls=%fused_computation.4 | convolution fusion | flops 542375936 | bytes 4194305 | tf_op jit(solution)/shard_map/dot_general | solution.py:436
  104.9 2.9 %collective-permute-start.20 = (bf16[16,1024]{1,0:T(8,128)(2,1)}, bf16[16,1024]{1,0:T(8,128)(2,1)S(1)}, u32[]{:S(2)}, u32[]{:S(2)}) collective-permute-start(bf16[16,1024]{1,0:T(8,128)(2,1)} %get-tuple-element.25), channel_id=1, source_target_pairs={{0,16},{4,20},{8,24},{12,28},{1,17},{5,21},{9,25},{13,29},{2,18},{... | collective-permute-start | bytes 98312 | tf_op jit(solution)/shard_map/ppermute | solution.py:280
  107.9 1.9 %collective-permute-done.20 = bf16[16,1024]{1,0:T(8,128)(2,1)S(1)} collective-permute-done((bf16[16,1024]{1,0:T(8,128)(2,1)}, bf16[16,1024]{1,0:T(8,128)(2,1)S(1)}, u32[]{:S(2)}, u32[]{:S(2)}) %collective-permute-start.20) | collective-permute-done | bytes 32800 | tf_op jit(solution)/shard_map/ppermute | solution.py:280
  109.8 0.6 copy-done.24
  110.4 0.9 fusion.21.start
  111.3 2.8 %fusion.1 = bf16[256,1024]{1,0:T(8,128)(2,1)S(1)} fusion(f32[256,1024]{1,0:T(8,128)} %collective-permute-done.19, bf16[512,1024]{1,0:T(8,128)(2,1)} %copy-done.9, bf16[512,1024]{1,0:T(8,128)(2,1)} %copy-done.8, bf16[256,1024]{1,0:T(8,128)(2,1)} %copy-done.26, pred[]{:T(512)S(6)} %eq.14, bf16[128,1024]{1,0:T(8,128)(2,1)} %copy-done.21, ...), kind=kOutput, calls=%fused_computation.5 | convolution fusion | flops 542900224 | bytes 4718593 | tf_op jit(solution)/shard_map/dot_general | solution.py:436
  114.1 0.8 dynamic-slice_bitcast_fusion.1
  114.9 3.6 %collective-permute-start.21 = (bf16[128,1024]{1,0:T(8,128)(2,1)}, bf16[128,1024]{1,0:T(8,128)(2,1)}, u32[]{:S(2)}, u32[]{:S(2)}) collective-permute-start(bf16[128,1024]{1,0:T(8,128)(2,1)} %get-tuple-element.42), channel_id=1, source_target_pairs={{0,0},{1,8},{2,16},{3,24},{4,4},{5,12},{6,20},{7,28},{8,9},{9,1},{... | collective-permute-start | bytes 786440 | tf_op jit(solution)/shard_map/ppermute | solution.py:430
  118.5 4.9 %collective-permute-start.22 = (bf16[128,1024]{1,0:T(8,128)(2,1)}, bf16[128,1024]{1,0:T(8,128)(2,1)}, u32[]{:S(2)}, u32[]{:S(2)}) collective-permute-start(bf16[128,1024]{1,0:T(8,128)(2,1)} %get-tuple-element.43), channel_id=1, source_target_pairs={{0,16},{1,24},{2,0},{3,8},{4,20},{5,28},{6,4},{7,12},{8,25},{9,17}... | collective-permute-start | bytes 786440 | tf_op jit(solution)/shard_map/ppermute | solution.py:430
  123.5 9.7 %shard_map.80 = f32[128,128]{1,0:T(8,128)S(1)} custom-call(f32[128,32,128]{2,1,0:T(8,128)S(1)} %broadcast_in_dim.5.kq, f32[128,1024]{1,0:T(8,128)S(1)} %add_divide_fusion.eps, f32[128,1024]{1,0:T(8,128)S(1)} %fusion.4.inner, bf16[128,1024]{1,0:T(8,128)(2,1)S(1)} %copy-done, f32[128,16,1024]{2,1,0:T(8,128)} %shard_map.78.adj_in, f32[16,1024]{1,0:T(8,128)S(1)} %fusion.21.start), custom_call_target="tpu_custom_call" | custom-call | flops 46137344 | bytes 1024 | tf_op jit(solution)/shard_map/pallas_call | solution.py:261
  133.2 0.3 convolution_convert_fusion
  133.5 0.7 copy.16
  134.2 3.7 %all-to-all-start.1 = ((bf16[8,32,512]{2,1,0:T(8,128)(2,1)}), bf16[8,32,512]{2,1,0:T(8,128)(2,1)S(1)}, u32[]{:S(2)}, u32[]{:S(2)}) async-start(bf16[8,32,512]{2,1,0:T(8,128)(2,1)} %bitcast.34), calls=%async_computation.1 | async-start | bytes 524288 | tf_op jit(solution)/shard_map/all_to_all | solution.py:518
  138.0 1.6 %collective-permute-start.24 = (bf16[128,32]{1,0:T(8,128)(2,1)S(1)}, bf16[128,32]{1,0:T(8,128)(2,1)S(1)}, u32[]{:S(2)}, u32[]{:S(2)}) collective-permute-start(bf16[128,32]{1,0:T(8,128)(2,1)S(1)} %slice.180), channel_id=1, source_target_pairs={{0,2},{1,3},{2,0},{3,1},{4,6},{5,7},{6,4},{7,5},{8,10},{9,11},{10,... | collective-permute-start | bytes 24584 | tf_op jit(solution)/shard_map/ppermute | solution.py:311
  139.6 4.1 %shard_map.81 = bf16[128,1024]{1,0:T(8,128)(2,1)} custom-call(f32[128,32,128]{2,1,0:T(8,128)S(1)} %broadcast_in_dim.5.kq, f32[128,1024]{1,0:T(8,128)S(1)} %add_divide_fusion.eps, f32[128,1024]{1,0:T(8,128)S(1)} %fusion.4.inner, f32[16,1024]{1,0:T(8,128)S(1)} %fusion.21.start), custom_call_target="tpu_custom_call" | custom-call | flops 16777216 | bytes 1024 | tf_op jit(solution)/shard_map/pallas_call | solution.py:261
  143.8 2.0 %add_convert_fusion = bf16[128,1024]{1,0:T(8,128)(2,1)} fusion(bf16[128,1024]{1,0:T(8,128)(2,1)} %collective-permute-done.22, bf16[128,1024]{1,0:T(8,128)(2,1)} %collective-permute-done.21, bf16[128,1024]{1,0:T(8,128)(2,1)S(1)} %copy-done.10, bf16[128,32]{1,0:T(8,128)(2,1)S(1)} %collective-permute-done.25, bf16[128,32]{1,0:T(8,128)(2,1)S(1)} %collective-permute-done.24, ...), kind=kOutput, calls=%fused_computation.17 | convolution fusion | flops 34340864 | bytes 1081344 | tf_op jit(solution)/shard_map/dot_general | solution.py:512
  145.8 1.5 %all-to-all-done.1 = bf16[8,32,512]{2,1,0:T(8,128)(2,1)S(1)} async-done(((bf16[8,32,512]{2,1,0:T(8,128)(2,1)}), bf16[8,32,512]{2,1,0:T(8,128)(2,1)S(1)}, u32[]{:S(2)}, u32[]{:S(2)}) %all-to-all-start.1) | async-done | bytes 262176 | tf_op jit(solution)/shard_map/all_to_all | solution.py:518
  147.3 0.7 convert_reduce_fusion
  (94 shorter events, 1.1 us)
Async XLA Ops:
  0.6 19.0 %copy-start.5 = (bf16[128,4096]{1,0:T(8,128)(2,1)S(1)}, bf16[128,4096]{1,0:T(8,128)(2,1)}, u32[]{:S(2)}) copy-start(bf16[128,4096]{1,0:T(8,128)(2,1)} %param.5) | copy-start | bytes 3145732
  0.6 19.5 %copy-start.25 = (f32[1024]{0:T(1024)S(1)}, f32[1024]{0:T(1024)}, u32[]{:S(2)}) copy-start(f32[1024]{0:T(1024)} %param.8) | copy-start | bytes 12292
  2.2 17.3 %all-to-all-start = ((bf16[8,32,512]{2,1,0:T(8,128)(2,1)}), bf16[8,32,512]{2,1,0:T(8,128)(2,1)S(1)}, u32[]{:S(2)}, u32[]{:S(2)}) async-start(bf16[8,32,512]{2,1,0:T(8,128)(2,1)} %broadcast_in_dim.4), calls=%async_computation | async-start | bytes 524288 | tf_op jit(solution)/shard_map/all_to_all | solution.py:316
  11.2 13.1 %collective-permute-start.4 = (bf16[128,512]{1,0:T(8,128)(2,1)}, bf16[128,512]{1,0:T(8,128)(2,1)S(1)}, u32[]{:S(2)}, u32[]{:S(2)}) collective-permute-start(bf16[128,512]{1,0:T(8,128)(2,1)} %get-tuple-element.37), channel_id=1, source_target_pairs={{0,8},{4,12},{8,0},{12,4},{16,24},{20,28},{24,16},{28,20},{1,9},{5... | collective-permute-start | bytes 393224 | tf_op jit(solution)/shard_map/ppermute | solution.py:382
  13.3 12.4 %collective-permute-start.5 = (bf16[128,512]{1,0:T(8,128)(2,1)}, bf16[128,512]{1,0:T(8,128)(2,1)}, u32[]{:S(2)}, u32[]{:S(2)}) collective-permute-start(bf16[128,512]{1,0:T(8,128)(2,1)} %get-tuple-element.38), channel_id=1, source_target_pairs={{0,24},{4,28},{8,16},{12,20},{16,8},{20,12},{24,0},{28,4},{1,25},{... | collective-permute-start | bytes 393224 | tf_op jit(solution)/shard_map/ppermute | solution.py:382
  15.6 16.5 %collective-permute-start.6 = (bf16[128,512]{1,0:T(8,128)(2,1)S(1)}, bf16[128,512]{1,0:T(8,128)(2,1)}, u32[]{:S(2)}, u32[]{:S(2)}) collective-permute-start(bf16[128,512]{1,0:T(8,128)(2,1)S(1)} %get-tuple-element.39), channel_id=1, source_target_pairs={{0,16},{4,20},{8,24},{12,28},{16,0},{20,4},{24,8},{28,12},{1,17},{... | collective-permute-start | bytes 393224 | tf_op jit(solution)/shard_map/ppermute | solution.py:382
  15.6 31.2 %collective-permute-start = (bf16[512,1024]{1,0:T(8,128)(2,1)}, bf16[512,1024]{1,0:T(8,128)(2,1)}, u32[]{:S(2)}, u32[]{:S(2)}) collective-permute-start(bf16[512,1024]{1,0:T(8,128)(2,1)} %param.6), channel_id=1, source_target_pairs={{0,4},{4,0},{8,12},{12,8},{16,20},{20,16},{24,28},{28,24},{1,5},{5... | collective-permute-start | bytes 3145736 | tf_op jit(solution)/shard_map/ppermute | solution.py:382
  19.6 1.4 copy-start
  23.1 10.8 %collective-permute-start.3 = (bf16[32,1024]{1,0:T(8,128)(2,1)S(1)}, bf16[32,1024]{1,0:T(8,128)(2,1)S(1)}, u32[]{:S(2)}, u32[]{:S(2)}) collective-permute-start(bf16[32,1024]{1,0:T(8,128)(2,1)S(1)} %convert_element_type.68), channel_id=1, source_target_pairs={{12,0},{16,4},{20,8},{24,12},{28,16},{13,1},{17,5},{21,9},{25,13},... | collective-permute-start | bytes 196616 | tf_op jit(solution)/shard_map/ppermute | solution.py:280
  24.4 9.5 %collective-permute-start.2 = (bf16[32,1024]{1,0:T(8,128)(2,1)S(1)}, bf16[32,1024]{1,0:T(8,128)(2,1)S(1)}, u32[]{:S(2)}, u32[]{:S(2)}) collective-permute-start(bf16[32,1024]{1,0:T(8,128)(2,1)S(1)} %convert_element_type.68), channel_id=1, source_target_pairs={{8,0},{12,4},{16,8},{20,12},{24,16},{28,20},{9,1},{13,5},{17,9},{2... | collective-permute-start | bytes 196616 | tf_op jit(solution)/shard_map/ppermute | solution.py:280
  25.7 17.1 %collective-permute-start.1 = (bf16[32,1024]{1,0:T(8,128)(2,1)S(1)}, bf16[32,1024]{1,0:T(8,128)(2,1)S(1)}, u32[]{:S(2)}, u32[]{:S(2)}) collective-permute-start(bf16[32,1024]{1,0:T(8,128)(2,1)S(1)} %convert_element_type.68), channel_id=1, source_target_pairs={{4,0},{8,4},{12,8},{16,12},{20,16},{24,20},{28,24},{5,1},{9,5},{13... | collective-permute-start | bytes 196616 | tf_op jit(solution)/shard_map/ppermute | solution.py:280
  33.8 9.7 %copy-start.17 = (f32[32,1024]{1,0:T(8,128)}, f32[32,1024]{1,0:T(8,128)S(1)}, u32[]{:S(2)}) copy-start(f32[32,1024]{1,0:T(8,128)S(1)} %convert_element_type.71) | copy-start | bytes 393220
  42.8 0.7 copy-start.11
  43.5 2.1 %collective-permute-start.7 = (bf16[384,512]{1,0:T(8,128)(2,1)}, bf16[384,512]{1,0:T(8,128)(2,1)}, u32[]{:S(2)}, u32[]{:S(2)}) collective-permute-start(bf16[384,512]{1,0:T(8,128)(2,1)} %pad_maximum_fusion.6), channel_id=1, source_target_pairs={{0,1},{1,0},{2,3},{3,2},{4,5},{5,4},{6,7},{7,6},{8,9},{9,8},{10,11... | collective-permute-start | bytes 1179656 | tf_op jit(solution)/shard_map/ppermute | solution.py:382
  43.7 4.9 %copy-start.3 = (bf16[512,1024]{1,0:T(8,128)(2,1)S(1)}, bf16[512,1024]{1,0:T(8,128)(2,1)}, u32[]{:S(2)}) copy-start(bf16[512,1024]{1,0:T(8,128)(2,1)} %param.6) | copy-start | bytes 3145732
  43.7 9.5 %collective-permute-start.9 = (bf16[16,1024]{1,0:T(8,128)(2,1)S(1)}, bf16[16,1024]{1,0:T(8,128)(2,1)S(1)}, u32[]{:S(2)}, u32[]{:S(2)}) collective-permute-start(bf16[16,1024]{1,0:T(8,128)(2,1)S(1)} %get-tuple-element.18), channel_id=1, source_target_pairs={{16,0},{20,4},{24,8},{28,12},{17,1},{21,5},{25,9},{29,13},{18,2},{... | collective-permute-start | bytes 98312 | tf_op jit(solution)/shard_map/ppermute | solution.py:280
  48.5 4.7 %copy-start.12 = (f32[32,1024]{1,0:T(8,128)S(1)}, f32[32,1024]{1,0:T(8,128)}, u32[]{:S(2)}) copy-start(f32[32,1024]{1,0:T(8,128)} %copy-done.11) | copy-start | bytes 393220
  48.5 4.7 %copy-start.18 = (f32[32,1024]{1,0:T(8,128)S(1)}, f32[32,1024]{1,0:T(8,128)}, u32[]{:S(2)}) copy-start(f32[32,1024]{1,0:T(8,128)} %copy-done.17) | copy-start | bytes 393220
  49.0 18.3 %collective-permute-start.8 = (bf16[256,1024]{1,0:T(8,128)(2,1)S(1)}, bf16[256,1024]{1,0:T(8,128)(2,1)S(1)}, u32[]{:S(2)}, u32[]{:S(2)}) collective-permute-start(bf16[256,1024]{1,0:T(8,128)(2,1)S(1)} %fusion.2), channel_id=1, source_target_pairs={{0,8},{4,12},{8,0},{12,4},{16,24},{20,28},{24,16},{28,20},{1,9},{5... | collective-permute-start | bytes 1572872 | tf_op jit(solution)/shard_map/ppermute | solution.py:382
  51.5 23.2 %collective-permute-start.14 = (bf16[32,1024]{1,0:T(8,128)(2,1)}, bf16[32,1024]{1,0:T(8,128)(2,1)}, u32[]{:S(2)}, u32[]{:S(2)}) collective-permute-start(bf16[32,1024]{1,0:T(8,128)(2,1)} %get-tuple-element.45), channel_id=1, source_target_pairs={{0,3},{1,0},{2,1},{3,2},{4,7},{5,4},{6,5},{7,6},{8,11},{9,8},{10,9... | collective-permute-start | bytes 196616 | tf_op jit(solution)/shard_map/ppermute | solution.py:311
  52.4 22.2 %collective-permute-start.13 = (bf16[32,1024]{1,0:T(8,128)(2,1)}, bf16[32,1024]{1,0:T(8,128)(2,1)}, u32[]{:S(2)}, u32[]{:S(2)}) collective-permute-start(bf16[32,1024]{1,0:T(8,128)(2,1)} %get-tuple-element.46), channel_id=1, source_target_pairs={{0,2},{1,3},{2,0},{3,1},{4,6},{5,7},{6,4},{7,5},{8,10},{9,11},{10,... | collective-permute-start | bytes 196616 | tf_op jit(solution)/shard_map/ppermute | solution.py:311
  53.0 21.7 %collective-permute-start.12 = (bf16[32,1024]{1,0:T(8,128)(2,1)}, bf16[32,1024]{1,0:T(8,128)(2,1)}, u32[]{:S(2)}, u32[]{:S(2)}) collective-permute-start(bf16[32,1024]{1,0:T(8,128)(2,1)} %get-tuple-element.47), channel_id=1, source_target_pairs={{0,1},{1,2},{2,3},{3,0},{4,5},{5,6},{6,7},{7,4},{8,9},{9,10},{10,1... | collective-permute-start | bytes 196616 | tf_op jit(solution)/shard_map/ppermute | solution.py:311
  56.6 24.0 %copy-start.1 = (bf16[128,1024]{1,0:T(8,128)(2,1)}, bf16[128,1024]{1,0:T(8,128)(2,1)S(1)}, u32[]{:S(2)}) copy-start(bf16[128,1024]{1,0:T(8,128)(2,1)S(1)} %shard_map.77) | copy-start | bytes 786436
  56.6 15.2 %collective-permute-start.10 = (bf16[128,1024]{1,0:T(8,128)(2,1)S(1)}, bf16[128,1024]{1,0:T(8,128)(2,1)S(1)}, u32[]{:S(2)}, u32[]{:S(2)}) collective-permute-start(bf16[128,1024]{1,0:T(8,128)(2,1)S(1)} %shard_map.77), channel_id=1, source_target_pairs={{0,16},{4,20},{8,24},{12,28},{16,0},{20,4},{24,8},{28,12},{1,17},{... | collective-permute-start | bytes 786440 | tf_op jit(solution)/shard_map/ppermute | solution.py:382
  61.2 13.4 %copy-start.23 = (bf16[32,1024]{1,0:T(8,128)(2,1)S(1)}, bf16[32,1024]{1,0:T(8,128)(2,1)}, u32[]{:S(2)}) copy-start(bf16[32,1024]{1,0:T(8,128)(2,1)} %get-tuple-element.44) | copy-start | bytes 196612
  67.3 4.6 %copy-start.15 = (bf16[256,1024]{1,0:T(8,128)(2,1)}, bf16[256,1024]{1,0:T(8,128)(2,1)S(1)}, u32[]{:S(2)}) copy-start(bf16[256,1024]{1,0:T(8,128)(2,1)S(1)} %collective-permute-done.8) | copy-start | bytes 1572868
  71.9 0.7 copy-start.21
  71.9 15.6 %collective-permute-start.11 = (bf16[128,1024]{1,0:T(8,128)(2,1)}, bf16[128,1024]{1,0:T(8,128)(2,1)}, u32[]{:S(2)}, u32[]{:S(2)}) collective-permute-start(bf16[128,1024]{1,0:T(8,128)(2,1)} %fusion.6), channel_id=1, source_target_pairs={{0,16},{4,20},{8,24},{12,28},{16,0},{20,4},{24,8},{28,12},{1,17},{... | collective-permute-start | bytes 786440 | tf_op jit(solution)/shard_map/ppermute | solution.py:382
  76.3 4.3 %copy-start.22 = (bf16[128,1024]{1,0:T(8,128)(2,1)S(1)}, bf16[128,1024]{1,0:T(8,128)(2,1)}, u32[]{:S(2)}) copy-start(bf16[128,1024]{1,0:T(8,128)(2,1)} %copy-done.21) | copy-start | bytes 786436
  76.3 11.2 %copy-start.7 = (f32[128,1024]{1,0:T(8,128)S(1)}, f32[128,1024]{1,0:T(8,128)}, u32[]{:S(2)}) copy-start(f32[128,1024]{1,0:T(8,128)} %fusion.18) | copy-start | bytes 1572868
  76.3 11.2 %copy-start.16 = (bf16[256,1024]{1,0:T(8,128)(2,1)S(1)}, bf16[256,1024]{1,0:T(8,128)(2,1)}, u32[]{:S(2)}) copy-start(bf16[256,1024]{1,0:T(8,128)(2,1)} %copy-done.15) | copy-start | bytes 1572868
  80.6 22.4 %collective-permute-start.18 = (bf16[256,1024]{1,0:T(8,128)(2,1)S(1)}, bf16[256,1024]{1,0:T(8,128)(2,1)S(1)}, u32[]{:S(2)}, u32[]{:S(2)}) collective-permute-start(bf16[256,1024]{1,0:T(8,128)(2,1)S(1)} %pad_maximum_fusion.5), channel_id=1, source_target_pairs={{0,8},{4,12},{8,0},{12,4},{16,24},{20,28},{24,16},{28,20},{1,9},{5... | collective-permute-start | bytes 1572872 | tf_op jit(solution)/shard_map/ppermute | solution.py:382
  89.1 11.0 %copy-start.4 = (bf16[512,1024]{1,0:T(8,128)(2,1)S(1)}, bf16[512,1024]{1,0:T(8,128)(2,1)}, u32[]{:S(2)}) copy-start(bf16[512,1024]{1,0:T(8,128)(2,1)} %param.6) | copy-start | bytes 3145732
  91.1 12.0 %copy-start.2 = (bf16[128,1024]{1,0:T(8,128)(2,1)S(1)}, bf16[128,1024]{1,0:T(8,128)(2,1)}, u32[]{:S(2)}) copy-start(bf16[128,1024]{1,0:T(8,128)(2,1)} %copy-done.1) | copy-start | bytes 786436
  91.1 10.5 %collective-permute-start.17 = (bf16[32,1024]{1,0:T(8,128)(2,1)S(1)}, bf16[32,1024]{1,0:T(8,128)(2,1)S(1)}, u32[]{:S(2)}, u32[]{:S(2)}) collective-permute-start(bf16[32,1024]{1,0:T(8,128)(2,1)S(1)} %pad_maximum_fusion.8), channel_id=1, source_target_pairs={{0,12},{4,16},{8,20},{12,24},{16,28},{1,13},{5,17},{9,21},{13,25},... | collective-permute-start | bytes 196616 | tf_op jit(solution)/shard_map/ppermute | solution.py:280
  92.5 9.1 %collective-permute-start.16 = (bf16[32,1024]{1,0:T(8,128)(2,1)S(1)}, bf16[32,1024]{1,0:T(8,128)(2,1)S(1)}, u32[]{:S(2)}, u32[]{:S(2)}) collective-permute-start(bf16[32,1024]{1,0:T(8,128)(2,1)S(1)} %pad_maximum_fusion.8), channel_id=1, source_target_pairs={{0,8},{4,12},{8,16},{12,20},{16,24},{20,28},{1,9},{5,13},{9,17},{1... | collective-permute-start | bytes 196616 | tf_op jit(solution)/shard_map/ppermute | solution.py:280
  94.1 8.0 %collective-permute-start.15 = (bf16[32,1024]{1,0:T(8,128)(2,1)S(1)}, bf16[32,1024]{1,0:T(8,128)(2,1)S(1)}, u32[]{:S(2)}, u32[]{:S(2)}) collective-permute-start(bf16[32,1024]{1,0:T(8,128)(2,1)S(1)} %pad_maximum_fusion.8), channel_id=1, source_target_pairs={{0,4},{4,8},{8,12},{12,16},{16,20},{20,24},{24,28},{1,5},{5,9},{9,... | collective-permute-start | bytes 196616 | tf_op jit(solution)/shard_map/ppermute | solution.py:280
  101.6 3.3 %copy-start.8 = (bf16[512,1024]{1,0:T(8,128)(2,1)}, bf16[512,1024]{1,0:T(8,128)(2,1)S(1)}, u32[]{:S(2)}) copy-start(bf16[512,1024]{1,0:T(8,128)(2,1)S(1)} %get-tuple-element.35) | copy-start | bytes 3145732
  101.6 3.3 %copy-start.9 = (bf16[512,1024]{1,0:T(8,128)(2,1)}, bf16[512,1024]{1,0:T(8,128)(2,1)S(1)}, u32[]{:S(2)}) copy-start(bf16[512,1024]{1,0:T(8,128)(2,1)S(1)} %get-tuple-element.36) | copy-start | bytes 3145732
  101.6 3.3 %copy-start.19 = (f32[32,1024]{1,0:T(8,128)}, f32[32,1024]{1,0:T(8,128)S(1)}, u32[]{:S(2)}) copy-start(f32[32,1024]{1,0:T(8,128)S(1)} %convert_element_type.81) | copy-start | bytes 393220
  101.7 1.4 copy-start.13
  102.1 0.9 copy-start.14
  103.0 1.8 %copy-start.26 = (bf16[256,1024]{1,0:T(8,128)(2,1)}, bf16[256,1024]{1,0:T(8,128)(2,1)S(1)}, u32[]{:S(2)}) copy-start(bf16[256,1024]{1,0:T(8,128)(2,1)S(1)} %collective-permute-done.18) | copy-start | bytes 1572868
  103.0 7.3 %copy-start.20 = (f32[16,1024]{1,0:T(8,128)S(1)}, f32[16,1024]{1,0:T(8,128)}, u32[]{:S(2)}) copy-start(f32[16,1024]{1,0:T(8,128)} %get-tuple-element.32) | copy-start | bytes 196612
  104.9 6.4 %collective-permute-start.19 = (f32[256,1024]{1,0:T(8,128)}, f32[256,1024]{1,0:T(8,128)}, u32[]{:S(2)}, u32[]{:S(2)}) collective-permute-start(f32[256,1024]{1,0:T(8,128)} %fusion), channel_id=1, source_target_pairs={{0,1},{1,0},{2,3},{3,2},{4,5},{5,4},{6,7},{7,6},{8,9},{9,8},{10,11... | collective-permute-start | bytes 3145736 | tf_op jit(solution)/shard_map/ppermute | solution.py:382
  104.9 4.8 %collective-permute-start.20 = (bf16[16,1024]{1,0:T(8,128)(2,1)}, bf16[16,1024]{1,0:T(8,128)(2,1)S(1)}, u32[]{:S(2)}, u32[]{:S(2)}) collective-permute-start(bf16[16,1024]{1,0:T(8,128)(2,1)} %get-tuple-element.25), channel_id=1, source_target_pairs={{0,16},{4,20},{8,24},{12,28},{1,17},{5,21},{9,25},{13,29},{2,18},{... | collective-permute-start | bytes 98312 | tf_op jit(solution)/shard_map/ppermute | solution.py:280
  109.7 0.6 copy-start.24
  114.9 28.8 %collective-permute-start.21 = (bf16[128,1024]{1,0:T(8,128)(2,1)}, bf16[128,1024]{1,0:T(8,128)(2,1)}, u32[]{:S(2)}, u32[]{:S(2)}) collective-permute-start(bf16[128,1024]{1,0:T(8,128)(2,1)} %get-tuple-element.42), channel_id=1, source_target_pairs={{0,0},{1,8},{2,16},{3,24},{4,4},{5,12},{6,20},{7,28},{8,9},{9,1},{... | collective-permute-start | bytes 786440 | tf_op jit(solution)/shard_map/ppermute | solution.py:430
  118.5 14.7 %copy-start.6 = (bf16[128,4096]{1,0:T(8,128)(2,1)S(1)}, bf16[128,4096]{1,0:T(8,128)(2,1)}, u32[]{:S(2)}) copy-start(bf16[128,4096]{1,0:T(8,128)(2,1)} %param.5) | copy-start | bytes 3145732
  118.5 25.2 %collective-permute-start.22 = (bf16[128,1024]{1,0:T(8,128)(2,1)}, bf16[128,1024]{1,0:T(8,128)(2,1)}, u32[]{:S(2)}, u32[]{:S(2)}) collective-permute-start(bf16[128,1024]{1,0:T(8,128)(2,1)} %get-tuple-element.43), channel_id=1, source_target_pairs={{0,16},{1,24},{2,0},{3,8},{4,20},{5,28},{6,4},{7,12},{8,25},{9,17}... | collective-permute-start | bytes 786440 | tf_op jit(solution)/shard_map/ppermute | solution.py:430
  134.2 13.1 %all-to-all-start.1 = ((bf16[8,32,512]{2,1,0:T(8,128)(2,1)}), bf16[8,32,512]{2,1,0:T(8,128)(2,1)S(1)}, u32[]{:S(2)}, u32[]{:S(2)}) async-start(bf16[8,32,512]{2,1,0:T(8,128)(2,1)} %bitcast.34), calls=%async_computation.1 | async-start | bytes 524288 | tf_op jit(solution)/shard_map/all_to_all | solution.py:518
  138.0 5.8 %copy-start.10 = (bf16[128,1024]{1,0:T(8,128)(2,1)S(1)}, bf16[128,1024]{1,0:T(8,128)(2,1)}, u32[]{:S(2)}) copy-start(bf16[128,1024]{1,0:T(8,128)(2,1)} %pad_maximum_fusion.7) | copy-start | bytes 786436
  138.0 5.7 %collective-permute-start.25 = (bf16[128,32]{1,0:T(8,128)(2,1)S(1)}, bf16[128,32]{1,0:T(8,128)(2,1)S(1)}, u32[]{:S(2)}, u32[]{:S(2)}) collective-permute-start(bf16[128,32]{1,0:T(8,128)(2,1)S(1)} %slice.180), channel_id=1, source_target_pairs={{0,3},{1,0},{2,1},{3,2},{4,7},{5,4},{6,5},{7,6},{8,11},{9,8},{10,9... | collective-permute-start | bytes 24584 | tf_op jit(solution)/shard_map/ppermute | solution.py:311
  138.0 5.7 %collective-permute-start.24 = (bf16[128,32]{1,0:T(8,128)(2,1)S(1)}, bf16[128,32]{1,0:T(8,128)(2,1)S(1)}, u32[]{:S(2)}, u32[]{:S(2)}) collective-permute-start(bf16[128,32]{1,0:T(8,128)(2,1)S(1)} %slice.180), channel_id=1, source_target_pairs={{0,2},{1,3},{2,0},{3,1},{4,6},{5,7},{6,4},{7,5},{8,10},{9,11},{10,... | collective-permute-start | bytes 24584 | tf_op jit(solution)/shard_map/ppermute | solution.py:311
  139.6 4.1 %collective-permute-start.23 = (bf16[128,32]{1,0:T(8,128)(2,1)S(1)}, bf16[128,32]{1,0:T(8,128)(2,1)S(1)}, u32[]{:S(2)}, u32[]{:S(2)}) collective-permute-start(bf16[128,32]{1,0:T(8,128)(2,1)S(1)} %slice.180), channel_id=1, source_target_pairs={{0,1},{1,2},{2,3},{3,0},{4,5},{5,6},{6,7},{7,4},{8,9},{9,10},{10,1... | collective-permute-start | bytes 24584 | tf_op jit(solution)/shard_map/ppermute | solution.py:311

commit v6 on v5

--- a/solution.py
+++ b/solution.py
@@ -446,6 +446,35 @@
     plan = (Exchanged if short else Gathered)(tokens, w_inner)
     kq_parts = gathered(w_keyquery.reshape(-1, kq_cols).T, "seq")
     full_kq = side_by_side(kq_parts)
+    keyquery = dot_t(tokens, full_kq)
+    keys = keyquery[:, :NS]
+    sumsq = jnp.sum(keys * keys, axis=1)
+    eps = rate[None, :] / (1.0 + rate[None, :] * sumsq[:, None])
+    spread = jnp.broadcast_to(keyquery[:, :, None], (count, 2 * NS, LANES))
+    rows_f = pltpu.VMEM((count, block), F32)
+    run = functools.partial(call, tokens=count, width=width, block=block)
+
+    (pair,) = run(
+        adjoint_totals_kernel,
+        ins=["kq", "rows", "rows16"], outs=["pair"], scratch=[rows_f],
+        args=(spread, eps, grad_out), work=4,
+    )
+    end_adjoint, plan.came = carried(pair, -1, plan.came)
+    beside, rest = plan.partials()
+    near, far, beside = plan.spread(beside, rest)
+    (inner_grad,) = run(
+        inner_grad_kernel,
+        ins=["kq", "rows", "rows16", "state"], outs=["rows16"], scratch=[rows_f, rows_f],
+        args=(spread, eps, grad_out, end_adjoint), work=8,
+    )
+    (adjoints,) = run(
+        adjoint_kernel,
+        ins=["kq", "rows", "rows16", "state"], outs=["states"], scratch=[rows_f],
+        args=(spread, eps, grad_out, lax.optimization_barrier((end_adjoint, inner_grad))[0]),
+        work=10,
+    )
+    beside, _ = lax.optimization_barrier((beside, inner_grad))
+    full_kq, _ = lax.optimization_barrier((full_kq, inner_grad))
     group = lax.axis_index("chan")
     kq_rows = []
     for m in range(chans):
@@ -453,34 +482,6 @@
             full_kq, (group + m) % chans * (full_kq.shape[1] // chans), full_kq.shape[1] // chans, 1
         )
         kq_rows.append(along_chan(rows, m))
-    keyquery = dot_t(tokens, full_kq)
-    keys = keyquery[:, :NS]
-    sumsq = jnp.sum(keys * keys, axis=1)
-    eps = rate[None, :] / (1.0 + rate[None, :] * sumsq[:, None])
-    spread = jnp.broadcast_to(keyquery[:, :, None], (count, 2 * NS, LANES))
-    rows_f = pltpu.VMEM((count, block), F32)
-    run = functools.partial(call, tokens=count, width=width, block=block)
-
-    (pair,) = run(
-        adjoint_totals_kernel,
-        ins=["kq", "rows", "rows16"], outs=["pair"], scratch=[rows_f],
-        args=(spread, eps, grad_out), work=4,
-    )
-    end_adjoint, plan.came = carried(pair, -1, plan.came)
-    beside, rest = plan.partials()
-    near, far, beside = plan.spread(beside, rest)
-    (inner_grad,) = run(
-        inner_grad_kernel,
-        ins=["kq", "rows", "rows16", "state"], outs=["rows16"], scratch=[rows_f, rows_f],
-        args=(spread, eps, grad_out, end_adjoint), work=8,
-    )
-    (adjoints,) = run(
-        adjoint_kernel,
-        ins=["kq", "rows", "rows16", "state"], outs=["states"], scratch=[rows_f],
-        args=(spread, eps, grad_out, lax.optimization_barrier((end_adjoint, inner_grad))[0]),
-        work=10,
-    )
-    beside, _ = lax.optimization_barrier((beside, inner_grad))
     inner, even, odd = plan.inner(near, far, beside, inner_grad)
     inner, kq_rows, adjoints = lax.optimization_barrier(
         (inner, jnp.concatenate(kq_rows, axis=0), adjoints)

time: 149 us -> 148 us (level)
  starting transfers between devices: 53.9 us -> 58.2 us
  waiting for transfers between devices: 34.4 us -> 30.2 us
    ppermute x10, waiting for transfers between devices: 19.2 us -> 14 us  [trade(): return lax.ppermute(value, axis, pairs)]
    ppermute x8, starting transfers between devices: 17.3 us -> 19.5 us  [shifted(): return lax.ppermute(value, axis, pairs)]
    ppermute x10, starting transfers between devices: 13.8 us -> 15.8 us  [trade(): return lax.ppermute(value, axis, pairs)]
where the time goes in v6:
time: 148 us; the launch traced here: 146 us
  starting transfers between devices  58.2 us (39%)
  waiting for transfers between devices  30.2 us (20%)
  Pallas kernels  25.5 us (17%)
  matrix products  15.7 us (11%)
  other arithmetic  8.58 us (6%)
  local copies, waits for them, and re-layouts  7.01 us (5%)
    pallas_call x6, Pallas kernels, call(): pl.pallas_call(kernel, grid=(width // block,), in_specs=[spec(kind) for k...  25.5 us
    ppermute x8, starting transfers between devices, shifted(): return lax.ppermute(value, axis, pairs)  19.5 us
    ppermute x10, starting transfers between devices, trade(): return lax.ppermute(value, axis, pairs)  15.8 us
    ppermute x10, waiting for transfers between devices, trade(): return lax.ppermute(value, axis, pairs)  14 us
    ppermute x8, waiting for transfers between devices, shifted(): return lax.ppermute(value, axis, pairs)  11.9 us
    ppermute x2, starting transfers between devices, grad_tokens(): piece = lax.ppermute(piece, ('seq', 'chan'), route).astype(F32)  8.58 us
    all_to_all x1, starting transfers between devices, gathered(): return lax.all_to_all(copies, axis, 0, 0, tiled=True)  7.25 us
    dot_general x3, matrix products, dot_t(): lax.dot_general(left, right, (((1,), (1,)), ((), ())), preferred_element_...  5.03 us
  transfers between devices with their start and end apart: 28, of which 10 were waited for; matrix products, arithmetic and copies ran while one was open for 16% of the time, Pallas kernels for 17%

profile of v6, /device:TPU:0, one launch (start us, length us, event | category | flops | bytes accessed | tf_op | source)
XLA Modules:
  0.0 146.5 jit_solution(8857095038610893007)
XLA Ops:
  0.7 1.6 %broadcast_in_dim.4 = bf16[8,32,512]{2,1,0:T(8,128)(2,1)} broadcast(bf16[32,512]{1,0:T(8,128)(2,1)} %bitcast.38), dimensions={1,2} | broadcast | bytes 294912 | tf_op jit(solution)/shard_map/broadcast_in_dim | solution.py:315
  2.2 7.3 %all-to-all-start = ((bf16[8,32,512]{2,1,0:T(8,128)(2,1)}), bf16[8,32,512]{2,1,0:T(8,128)(2,1)S(1)}, u32[]{:S(2)}, u32[]{:S(2)}) async-start(bf16[8,32,512]{2,1,0:T(8,128)(2,1)} %broadcast_in_dim.4), calls=%async_computation | async-start | bytes 524288 | tf_op jit(solution)/shard_map/all_to_all | solution.py:316
  9.5 1.7 %constant_dynamic-slice_fusion.6 = (bf16[128,512]{1,0:T(8,128)(2,1)}, bf16[128,512]{1,0:T(8,128)(2,1)S(1)}, bf16[128,512]{1,0:T(8,128)(2,1)S(1)}) fusion(bf16[128,4096]{1,0:T(8,128)(2,1)} %param.5, s32[]{:T(128)S(6)} %select_n.114, s32[]{:T(128)S(6)} %select_n.115, s32[]{:T(128)S(6)} %select_n.116), kind=kLoop, calls=%fused_computation.77 | loop fusion | bytes 786444 | tf_op jit(solution)/shard_map/dynamic_slice | solution.py:378
  11.2 2.0 %collective-permute-start.4 = (bf16[128,512]{1,0:T(8,128)(2,1)}, bf16[128,512]{1,0:T(8,128)(2,1)S(1)}, u32[]{:S(2)}, u32[]{:S(2)}) collective-permute-start(bf16[128,512]{1,0:T(8,128)(2,1)} %get-tuple-element.39), channel_id=1, source_target_pairs={{0,8},{4,12},{8,0},{12,4},{16,24},{20,28},{24,16},{28,20},{1,9},{5... | collective-permute-start | bytes 393224 | tf_op jit(solution)/shard_map/ppermute | solution.py:382
  13.2 2.4 %collective-permute-start.5 = (bf16[128,512]{1,0:T(8,128)(2,1)S(1)}, bf16[128,512]{1,0:T(8,128)(2,1)S(1)}, u32[]{:S(2)}, u32[]{:S(2)}) collective-permute-start(bf16[128,512]{1,0:T(8,128)(2,1)S(1)} %get-tuple-element.40), channel_id=1, source_target_pairs={{0,24},{4,28},{8,16},{12,20},{16,8},{20,12},{24,0},{28,4},{1,25},{... | collective-permute-start | bytes 393224 | tf_op jit(solution)/shard_map/ppermute | solution.py:382
  15.6 1.5 collective-permute-start
  17.0 2.7 %all-to-all-done = bf16[8,32,512]{2,1,0:T(8,128)(2,1)S(1)} async-done(((bf16[8,32,512]{2,1,0:T(8,128)(2,1)}), bf16[8,32,512]{2,1,0:T(8,128)(2,1)S(1)}, u32[]{:S(2)}, u32[]{:S(2)}) %all-to-all-start) | async-done | bytes 262176 | tf_op jit(solution)/shard_map/all_to_all | solution.py:316
  19.8 0.4 fusion.48
  20.6 0.6 broadcast_in_dim.5.kq
  21.2 2.1 %shard_map.76 = f32[32,1024]{1,0:T(8,128)S(1)} custom-call(f32[128,32,128]{2,1,0:T(8,128)S(1)} %broadcast_in_dim.5.kq, f32[128,1024]{1,0:T(8,128)S(1)} %add_divide_fusion.eps, bf16[128,1024]{1,0:T(8,128)(2,1)S(1)} %copy-done), custom_call_target="tpu_custom_call" | custom-call | flops 8388608 | bytes 1024 | tf_op jit(solution)/shard_map/pallas_call | solution.py:261
  23.3 1.3 collective-permute-start.3
  24.6 1.3 collective-permute-start.2
  25.9 1.3 collective-permute-start.1
  27.2 5.0 %collective-permute-done.6 = bf16[128,512]{1,0:T(8,128)(2,1)} collective-permute-done((bf16[128,512]{1,0:T(8,128)(2,1)S(1)}, bf16[128,512]{1,0:T(8,128)(2,1)}, u32[]{:S(2)}, u32[]{:S(2)}) %collective-permute-start.6) | collective-permute-done | bytes 131104 | tf_op jit(solution)/shard_map/ppermute | solution.py:382
  32.3 1.0 pad_maximum_fusion.6
  33.3 9.4 %collective-permute-done.1 = bf16[32,1024]{1,0:T(8,128)(2,1)S(1)} collective-permute-done((bf16[32,1024]{1,0:T(8,128)(2,1)S(1)}, bf16[32,1024]{1,0:T(8,128)(2,1)S(1)}, u32[]{:S(2)}, u32[]{:S(2)}) %collective-permute-start.1) | collective-permute-done | bytes 65568 | tf_op jit(solution)/shard_map/ppermute | solution.py:280
  42.8 0.7 fusion.28
  43.6 1.4 collective-permute-start.9
  45.0 0.3 collective-permute-done.7
  45.3 1.1 broadcast_select_fusion.3
  46.4 1.7 %fusion.11 = f32[256,1024]{1,0:T(8,128)S(1)} fusion(bf16[512,1024]{1,0:T(8,128)(2,1)} %collective-permute-done, bf16[384,512]{1,0:T(8,128)(2,1)S(1)} %get-tuple-element.43), kind=kOutput, calls=%fused_computation.27 | convolution fusion | flops 268435456 | bytes 2359296 | tf_op jit(solution)/shard_map/dot_general | solution.py:393
  48.2 0.4 fusion.2
  48.6 1.8 %collective-permute-start.8 = (bf16[256,1024]{1,0:T(8,128)(2,1)S(1)}, bf16[256,1024]{1,0:T(8,128)(2,1)S(1)}, u32[]{:S(2)}, u32[]{:S(2)}) collective-permute-start(bf16[256,1024]{1,0:T(8,128)(2,1)S(1)} %fusion.2), channel_id=1, source_target_pairs={{0,8},{4,12},{8,0},{12,4},{16,24},{20,28},{24,16},{28,20},{1,9},{5... | collective-permute-start | bytes 1572872 | tf_op jit(solution)/shard_map/ppermute | solution.py:382
  50.7 3.4 %shard_map.77 = bf16[128,1024]{1,0:T(8,128)(2,1)S(1)} custom-call(f32[128,32,128]{2,1,0:T(8,128)S(1)} %broadcast_in_dim.5.kq, f32[128,1024]{1,0:T(8,128)S(1)} %add_divide_fusion.eps, bf16[128,1024]{1,0:T(8,128)(2,1)S(1)} %copy-done, f32[16,1024]{1,0:T(8,128)S(1)} %fusion.25.start), custom_call_target="tpu_custom_call" | custom-call | flops 16777216 | bytes 1024 | tf_op jit(solution)/shard_map/pallas_call | solution.py:261
  54.0 3.1 %collective-permute-start.10 = (bf16[128,1024]{1,0:T(8,128)(2,1)S(1)}, bf16[128,1024]{1,0:T(8,128)(2,1)S(1)}, u32[]{:S(2)}, u32[]{:S(2)}) collective-permute-start(bf16[128,1024]{1,0:T(8,128)(2,1)S(1)} %shard_map.77), channel_id=1, source_target_pairs={{0,16},{4,20},{8,24},{12,28},{16,0},{20,4},{24,8},{28,12},{1,17},{... | collective-permute-start | bytes 786440 | tf_op jit(solution)/shard_map/ppermute | solution.py:382
  57.1 0.6 constant_dynamic-slice_fusion.3
  57.8 0.7 collective-permute-start.14
  58.5 0.8 collective-permute-start.13
  59.3 0.2 collective-permute-start.12
  59.5 1.5 %fusion.14 = f32[128,1024]{1,0:T(8,128)S(1)} fusion(bf16[512,1024]{1,0:T(8,128)(2,1)} %collective-permute-done, bf16[384,512]{1,0:T(8,128)(2,1)S(1)} %get-tuple-element.43), kind=kOutput, calls=%fused_computation.33 | convolution fusion | flops 134217728 | bytes 1703936 | tf_op jit(solution)/shard_map/dot_general | solution.py:393
  61.1 7.2 %collective-permute-done.8 = bf16[256,1024]{1,0:T(8,128)(2,1)S(1)} collective-permute-done((bf16[256,1024]{1,0:T(8,128)(2,1)S(1)}, bf16[256,1024]{1,0:T(8,128)(2,1)S(1)}, u32[]{:S(2)}, u32[]{:S(2)}) %collective-permute-start.8) | collective-permute-done | bytes 524320 | tf_op jit(solution)/shard_map/ppermute | solution.py:382
  68.3 1.0 fusion.6
  69.3 2.5 %collective-permute-start.11 = (bf16[128,1024]{1,0:T(8,128)(2,1)}, bf16[128,1024]{1,0:T(8,128)(2,1)}, u32[]{:S(2)}, u32[]{:S(2)}) collective-permute-start(bf16[128,1024]{1,0:T(8,128)(2,1)} %fusion.6), channel_id=1, source_target_pairs={{0,16},{4,20},{8,24},{12,28},{16,0},{20,4},{24,8},{28,12},{1,17},{... | collective-permute-start | bytes 786440 | tf_op jit(solution)/shard_map/ppermute | solution.py:382
  71.8 2.0 %fusion.18 = f32[128,1024]{1,0:T(8,128)} fusion(bf16[512,1024]{1,0:T(8,128)(2,1)S(1)} %copy-done.3, bf16[128,4096]{1,0:T(8,128)(2,1)} %param.5, s32[]{:T(128)S(6)} %select_n.109), kind=kOutput, calls=%fused_computation.37 | convolution fusion | flops 134217728 | bytes 1703940 | tf_op jit(solution)/shard_map/dot_general | solution.py:393
  73.9 4.3 %shard_map.78.adj_in = f32[128,16,1024]{2,1,0:T(8,128)} custom-call(f32[128,32,128]{2,1,0:T(8,128)S(1)} %broadcast_in_dim.5.kq, f32[128,1024]{1,0:T(8,128)S(1)} %add_divide_fusion.eps, bf16[128,1024]{1,0:T(8,128)(2,1)S(1)} %copy-done, f32[16,1024]{1,0:T(8,128)S(1)} %fusion.25.start), custom_call_target="tpu_custom_call" | custom-call | flops 20971520 | bytes 1024 | tf_op jit(solution)/shard_map/pallas_call | solution.py:261
  78.2 1.6 %pad_maximum_fusion.7 = bf16[128,1024]{1,0:T(8,128)(2,1)} fusion(bf16[32,1024]{1,0:T(8,128)(2,1)} %collective-permute-done.14, bf16[32,1024]{1,0:T(8,128)(2,1)} %collective-permute-done.13, bf16[32,1024]{1,0:T(8,128)(2,1)} %collective-permute-done.12, bf16[32,1024]{1,0:T(8,128)(2,1)S(1)} %get-tuple-element.46), kind=kLoop, calls=%fused_computation.30 | loop fusion | flops 1048576 | bytes 524288 | tf_op jit(solution)/shard_map/concatenate | solution.py:487
  79.9 2.5 %collective-permute-start.18 = (bf16[256,1024]{1,0:T(8,128)(2,1)S(1)}, bf16[256,1024]{1,0:T(8,128)(2,1)S(1)}, u32[]{:S(2)}, u32[]{:S(2)}) collective-permute-start(bf16[256,1024]{1,0:T(8,128)(2,1)S(1)} %pad_maximum_fusion.5), channel_id=1, source_target_pairs={{0,8},{4,12},{8,0},{12,4},{16,24},{20,28},{24,16},{28,20},{1,9},{5... | collective-permute-start | bytes 1572872 | tf_op jit(solution)/shard_map/ppermute | solution.py:382
  82.4 1.4 collective-permute-done.11
  83.8 1.6 %fusion.4.inner = f32[128,1024]{1,0:T(8,128)S(1)} fusion(f32[128,1024]{1,0:T(8,128)S(1)} %copy-done.9, bf16[512,1024]{1,0:T(8,128)(2,1)} %collective-permute-done, bf16[128,1024]{1,0:T(8,128)(2,1)} %collective-permute-done.11, bf16[256,1024]{1,0:T(8,128)(2,1)S(1)} %copy-done.18, bf16[128,4096]{1,0:T(8,128)(2,1)} %param.5, s32[]{:T(128)S(6)} %select_n.110), kind=kOutput, calls=%fused_computation.10 | convolution fusion | flops 134873088 | bytes 2752516 | tf_op jit(solution)/shard_map/dot_general | solution.py:393
  85.5 1.9 %shard_map.79 = f32[16,1024]{1,0:T(8,128)S(1)} custom-call(f32[128,32,128]{2,1,0:T(8,128)S(1)} %broadcast_in_dim.5.kq, f32[128,1024]{1,0:T(8,128)S(1)} %add_divide_fusion.eps, f32[128,1024]{1,0:T(8,128)S(1)} %fusion.4.inner), custom_call_target="tpu_custom_call" | custom-call | flops 8388608 | bytes 1024 | tf_op jit(solution)/shard_map/pallas_call | solution.py:261
  87.4 1.5 %collective-permute-start.17 = (bf16[32,1024]{1,0:T(8,128)(2,1)S(1)}, bf16[32,1024]{1,0:T(8,128)(2,1)S(1)}, u32[]{:S(2)}, u32[]{:S(2)}) collective-permute-start(bf16[32,1024]{1,0:T(8,128)(2,1)S(1)} %pad_maximum_fusion.8), channel_id=1, source_target_pairs={{0,12},{4,16},{8,20},{12,24},{16,28},{1,13},{5,17},{9,21},{13,25},... | collective-permute-start | bytes 196616 | tf_op jit(solution)/shard_map/ppermute | solution.py:280
  88.9 2.3 %collective-permute-start.16 = (bf16[32,1024]{1,0:T(8,128)(2,1)S(1)}, bf16[32,1024]{1,0:T(8,128)(2,1)S(1)}, u32[]{:S(2)}, u32[]{:S(2)}) collective-permute-start(bf16[32,1024]{1,0:T(8,128)(2,1)S(1)} %pad_maximum_fusion.8), channel_id=1, source_target_pairs={{0,8},{4,12},{8,16},{12,20},{16,24},{20,28},{1,9},{5,13},{9,17},{1... | collective-permute-start | bytes 196616 | tf_op jit(solution)/shard_map/ppermute | solution.py:280
  91.2 7.4 %collective-permute-start.15 = (bf16[32,1024]{1,0:T(8,128)(2,1)S(1)}, bf16[32,1024]{1,0:T(8,128)(2,1)S(1)}, u32[]{:S(2)}, u32[]{:S(2)}) collective-permute-start(bf16[32,1024]{1,0:T(8,128)(2,1)S(1)} %pad_maximum_fusion.8), channel_id=1, source_target_pairs={{0,4},{4,8},{8,12},{12,16},{16,20},{20,24},{24,28},{1,5},{5,9},{9,... | collective-permute-start | bytes 196616 | tf_op jit(solution)/shard_map/ppermute | solution.py:280
  98.7 1.4 broadcast_select_fusion.1
  100.2 0.4 collective-permute-done.15
  100.6 0.9 add_convert_fusion.1
  101.5 1.8 %fusion = f32[256,1024]{1,0:T(8,128)} fusion(bf16[512,1024]{1,0:T(8,128)(2,1)S(1)} %get-tuple-element.38, bf16[512,1024]{1,0:T(8,128)(2,1)S(1)} %get-tuple-element.37, bf16[256,1024]{1,0:T(8,128)(2,1)S(1)} %collective-permute-done.18, pred[]{:T(512)S(6)} %eq.14, bf16[128,1024]{1,0:T(8,128)(2,1)S(1)} %copy-done.25, bf16[128,1024]{1,0:T(8,128)(2,1)S(1)} %copy-done.2), kind=kOutput, calls=%fused_computation.4 | convolution fusion | flops 542375936 | bytes 4194305 | tf_op jit(solution)/shard_map/dot_general | solution.py:436
  103.4 2.9 %collective-permute-start.20 = (bf16[16,1024]{1,0:T(8,128)(2,1)}, bf16[16,1024]{1,0:T(8,128)(2,1)S(1)}, u32[]{:S(2)}, u32[]{:S(2)}) collective-permute-start(bf16[16,1024]{1,0:T(8,128)(2,1)} %get-tuple-element.27), channel_id=1, source_target_pairs={{0,16},{4,20},{8,24},{12,28},{1,17},{5,21},{9,25},{13,29},{2,18},{... | collective-permute-start | bytes 98312 | tf_op jit(solution)/shard_map/ppermute | solution.py:280
  106.4 1.9 %collective-permute-done.20 = bf16[16,1024]{1,0:T(8,128)(2,1)S(1)} collective-permute-done((bf16[16,1024]{1,0:T(8,128)(2,1)}, bf16[16,1024]{1,0:T(8,128)(2,1)S(1)}, u32[]{:S(2)}, u32[]{:S(2)}) %collective-permute-start.20) | collective-permute-done | bytes 32800 | tf_op jit(solution)/shard_map/ppermute | solution.py:280
  108.2 0.6 copy-done.27
  108.9 0.9 fusion.21.start
  109.8 2.8 %fusion.1 = bf16[256,1024]{1,0:T(8,128)(2,1)S(1)} fusion(f32[256,1024]{1,0:T(8,128)} %collective-permute-done.19, bf16[512,1024]{1,0:T(8,128)(2,1)} %copy-done.11, bf16[512,1024]{1,0:T(8,128)(2,1)} %copy-done.10, bf16[256,1024]{1,0:T(8,128)(2,1)} %copy-done.29, pred[]{:T(512)S(6)} %eq.14, bf16[128,1024]{1,0:T(8,128)(2,1)} %copy-done.24, ...), kind=kOutput, calls=%fused_computation.5 | convolution fusion | flops 542900224 | bytes 4718593 | tf_op jit(solution)/shard_map/dot_general | solution.py:436
  112.6 0.8 dynamic-slice_bitcast_fusion.1
  113.4 3.6 %collective-permute-start.21 = (bf16[128,1024]{1,0:T(8,128)(2,1)}, bf16[128,1024]{1,0:T(8,128)(2,1)}, u32[]{:S(2)}, u32[]{:S(2)}) collective-permute-start(bf16[128,1024]{1,0:T(8,128)(2,1)} %get-tuple-element.44), channel_id=1, source_target_pairs={{0,0},{1,8},{2,16},{3,24},{4,4},{5,12},{6,20},{7,28},{8,9},{9,1},{... | collective-permute-start | bytes 786440 | tf_op jit(solution)/shard_map/ppermute | solution.py:430
  117.0 5.0 %collective-permute-start.22 = (bf16[128,1024]{1,0:T(8,128)(2,1)}, bf16[128,1024]{1,0:T(8,128)(2,1)}, u32[]{:S(2)}, u32[]{:S(2)}) collective-permute-start(bf16[128,1024]{1,0:T(8,128)(2,1)} %get-tuple-element.45), channel_id=1, source_target_pairs={{0,16},{1,24},{2,0},{3,8},{4,20},{5,28},{6,4},{7,12},{8,25},{9,17}... | collective-permute-start | bytes 786440 | tf_op jit(solution)/shard_map/ppermute | solution.py:430
  122.0 9.7 %shard_map.80 = f32[128,128]{1,0:T(8,128)S(1)} custom-call(f32[128,32,128]{2,1,0:T(8,128)S(1)} %broadcast_in_dim.5.kq, f32[128,1024]{1,0:T(8,128)S(1)} %add_divide_fusion.eps, f32[128,1024]{1,0:T(8,128)S(1)} %fusion.4.inner, bf16[128,1024]{1,0:T(8,128)(2,1)S(1)} %copy-done, f32[128,16,1024]{2,1,0:T(8,128)} %shard_map.78.adj_in, f32[16,1024]{1,0:T(8,128)S(1)} %fusion.21.start), custom_call_target="tpu_custom_call" | custom-call | flops 46137344 | bytes 1024 | tf_op jit(solution)/shard_map/pallas_call | solution.py:261
  131.8 0.3 convolution_convert_fusion
  132.1 0.7 copy.16
  132.8 3.6 %all-to-all-start.1 = ((bf16[8,32,512]{2,1,0:T(8,128)(2,1)}), bf16[8,32,512]{2,1,0:T(8,128)(2,1)S(1)}, u32[]{:S(2)}, u32[]{:S(2)}) async-start(bf16[8,32,512]{2,1,0:T(8,128)(2,1)} %bitcast.34), calls=%async_computation.1 | async-start | bytes 524288 | tf_op jit(solution)/shard_map/all_to_all | solution.py:519
  136.5 1.6 %collective-permute-start.24 = (bf16[128,32]{1,0:T(8,128)(2,1)S(1)}, bf16[128,32]{1,0:T(8,128)(2,1)S(1)}, u32[]{:S(2)}, u32[]{:S(2)}) collective-permute-start(bf16[128,32]{1,0:T(8,128)(2,1)S(1)} %slice.180), channel_id=1, source_target_pairs={{0,2},{1,3},{2,0},{3,1},{4,6},{5,7},{6,4},{7,5},{8,10},{9,11},{10,... | collective-permute-start | bytes 24584 | tf_op jit(solution)/shard_map/ppermute | solution.py:311
  138.1 4.1 %shard_map.81 = bf16[128,1024]{1,0:T(8,128)(2,1)} custom-call(f32[128,32,128]{2,1,0:T(8,128)S(1)} %broadcast_in_dim.5.kq, f32[128,1024]{1,0:T(8,128)S(1)} %add_divide_fusion.eps, f32[128,1024]{1,0:T(8,128)S(1)} %fusion.4.inner, f32[16,1024]{1,0:T(8,128)S(1)} %fusion.21.start), custom_call_target="tpu_custom_call" | custom-call | flops 16777216 | bytes 1024 | tf_op jit(solution)/shard_map/pallas_call | solution.py:261
  142.3 2.0 %add_convert_fusion = bf16[128,1024]{1,0:T(8,128)(2,1)} fusion(bf16[128,1024]{1,0:T(8,128)(2,1)} %collective-permute-done.22, bf16[128,1024]{1,0:T(8,128)(2,1)} %collective-permute-done.21, bf16[128,1024]{1,0:T(8,128)(2,1)S(1)} %copy-done.12, bf16[128,32]{1,0:T(8,128)(2,1)S(1)} %collective-permute-done.25, bf16[128,32]{1,0:T(8,128)(2,1)S(1)} %collective-permute-done.24, ...), kind=kOutput, calls=%fused_computation.17 | convolution fusion | flops 34340864 | bytes 1081344 | tf_op jit(solution)/shard_map/dot_general | solution.py:513
  144.3 1.5 %all-to-all-done.1 = bf16[8,32,512]{2,1,0:T(8,128)(2,1)S(1)} async-done(((bf16[8,32,512]{2,1,0:T(8,128)(2,1)}), bf16[8,32,512]{2,1,0:T(8,128)(2,1)S(1)}, u32[]{:S(2)}, u32[]{:S(2)}) %all-to-all-start.1) | async-done | bytes 262176 | tf_op jit(solution)/shard_map/all_to_all | solution.py:519
  145.8 0.7 convert_reduce_fusion
  (100 shorter events, 1.0 us)
Async XLA Ops:
  0.6 19.2 %copy-start.5 = (bf16[128,4096]{1,0:T(8,128)(2,1)S(1)}, bf16[128,4096]{1,0:T(8,128)(2,1)}, u32[]{:S(2)}) copy-start(bf16[128,4096]{1,0:T(8,128)(2,1)} %param.5) | copy-start | bytes 3145732
  0.6 19.7 %copy-start.28 = (f32[1024]{0:T(1024)S(1)}, f32[1024]{0:T(1024)}, u32[]{:S(2)}) copy-start(f32[1024]{0:T(1024)} %param.8) | copy-start | bytes 12292
  2.2 17.5 %all-to-all-start = ((bf16[8,32,512]{2,1,0:T(8,128)(2,1)}), bf16[8,32,512]{2,1,0:T(8,128)(2,1)S(1)}, u32[]{:S(2)}, u32[]{:S(2)}) async-start(bf16[8,32,512]{2,1,0:T(8,128)(2,1)} %broadcast_in_dim.4), calls=%async_computation | async-start | bytes 524288 | tf_op jit(solution)/shard_map/all_to_all | solution.py:316
  11.2 13.4 %collective-permute-start.4 = (bf16[128,512]{1,0:T(8,128)(2,1)}, bf16[128,512]{1,0:T(8,128)(2,1)S(1)}, u32[]{:S(2)}, u32[]{:S(2)}) collective-permute-start(bf16[128,512]{1,0:T(8,128)(2,1)} %get-tuple-element.39), channel_id=1, source_target_pairs={{0,8},{4,12},{8,0},{12,4},{16,24},{20,28},{24,16},{28,20},{1,9},{5... | collective-permute-start | bytes 393224 | tf_op jit(solution)/shard_map/ppermute | solution.py:382
  13.2 12.7 %collective-permute-start.5 = (bf16[128,512]{1,0:T(8,128)(2,1)S(1)}, bf16[128,512]{1,0:T(8,128)(2,1)S(1)}, u32[]{:S(2)}, u32[]{:S(2)}) collective-permute-start(bf16[128,512]{1,0:T(8,128)(2,1)S(1)} %get-tuple-element.40), channel_id=1, source_target_pairs={{0,24},{4,28},{8,16},{12,20},{16,8},{20,12},{24,0},{28,4},{1,25},{... | collective-permute-start | bytes 393224 | tf_op jit(solution)/shard_map/ppermute | solution.py:382
  15.6 16.7 %collective-permute-start.6 = (bf16[128,512]{1,0:T(8,128)(2,1)S(1)}, bf16[128,512]{1,0:T(8,128)(2,1)}, u32[]{:S(2)}, u32[]{:S(2)}) collective-permute-start(bf16[128,512]{1,0:T(8,128)(2,1)S(1)} %get-tuple-element.41), channel_id=1, source_target_pairs={{0,16},{4,20},{8,24},{12,28},{16,0},{20,4},{24,8},{28,12},{1,17},{... | collective-permute-start | bytes 393224 | tf_op jit(solution)/shard_map/ppermute | solution.py:382
  15.6 30.8 %collective-permute-start = (bf16[512,1024]{1,0:T(8,128)(2,1)}, bf16[512,1024]{1,0:T(8,128)(2,1)}, u32[]{:S(2)}, u32[]{:S(2)}) collective-permute-start(bf16[512,1024]{1,0:T(8,128)(2,1)} %param.6), channel_id=1, source_target_pairs={{0,4},{4,0},{8,12},{12,8},{16,20},{20,16},{24,28},{28,24},{1,5},{5... | collective-permute-start | bytes 3145736 | tf_op jit(solution)/shard_map/ppermute | solution.py:382
  19.8 0.7 copy-start.7
  19.8 1.4 copy-start
  23.3 10.0 %collective-permute-start.3 = (bf16[32,1024]{1,0:T(8,128)(2,1)S(1)}, bf16[32,1024]{1,0:T(8,128)(2,1)S(1)}, u32[]{:S(2)}, u32[]{:S(2)}) collective-permute-start(bf16[32,1024]{1,0:T(8,128)(2,1)S(1)} %convert_element_type.68), channel_id=1, source_target_pairs={{12,0},{16,4},{20,8},{24,12},{28,16},{13,1},{17,5},{21,9},{25,13},... | collective-permute-start | bytes 196616 | tf_op jit(solution)/shard_map/ppermute | solution.py:280
  24.6 8.7 %collective-permute-start.2 = (bf16[32,1024]{1,0:T(8,128)(2,1)S(1)}, bf16[32,1024]{1,0:T(8,128)(2,1)S(1)}, u32[]{:S(2)}, u32[]{:S(2)}) collective-permute-start(bf16[32,1024]{1,0:T(8,128)(2,1)S(1)} %convert_element_type.68), channel_id=1, source_target_pairs={{8,0},{12,4},{16,8},{20,12},{24,16},{28,20},{9,1},{13,5},{17,9},{2... | collective-permute-start | bytes 196616 | tf_op jit(solution)/shard_map/ppermute | solution.py:280
  25.9 1.3 copy-start.26
  25.9 16.8 %collective-permute-start.1 = (bf16[32,1024]{1,0:T(8,128)(2,1)S(1)}, bf16[32,1024]{1,0:T(8,128)(2,1)S(1)}, u32[]{:S(2)}, u32[]{:S(2)}) collective-permute-start(bf16[32,1024]{1,0:T(8,128)(2,1)S(1)} %convert_element_type.68), channel_id=1, source_target_pairs={{4,0},{8,4},{12,8},{16,12},{20,16},{24,20},{28,24},{5,1},{9,5},{13... | collective-permute-start | bytes 196616 | tf_op jit(solution)/shard_map/ppermute | solution.py:280
  33.3 10.2 %copy-start.19 = (f32[32,1024]{1,0:T(8,128)}, f32[32,1024]{1,0:T(8,128)S(1)}, u32[]{:S(2)}) copy-start(f32[32,1024]{1,0:T(8,128)S(1)} %convert_element_type.71) | copy-start | bytes 393220
  42.8 0.7 copy-start.13
  43.5 1.9 %collective-permute-start.7 = (bf16[384,512]{1,0:T(8,128)(2,1)S(1)}, bf16[384,512]{1,0:T(8,128)(2,1)}, u32[]{:S(2)}, u32[]{:S(2)}) collective-permute-start(bf16[384,512]{1,0:T(8,128)(2,1)S(1)} %pad_maximum_fusion.6), channel_id=1, source_target_pairs={{0,1},{1,0},{2,3},{3,2},{4,5},{5,4},{6,7},{7,6},{8,9},{9,8},{10,11... | collective-permute-start | bytes 1179656 | tf_op jit(solution)/shard_map/ppermute | solution.py:382
  43.6 4.6 %copy-start.3 = (bf16[512,1024]{1,0:T(8,128)(2,1)S(1)}, bf16[512,1024]{1,0:T(8,128)(2,1)}, u32[]{:S(2)}) copy-start(bf16[512,1024]{1,0:T(8,128)(2,1)} %param.6) | copy-start | bytes 3145732
  43.6 7.0 %collective-permute-start.9 = (bf16[16,1024]{1,0:T(8,128)(2,1)}, bf16[16,1024]{1,0:T(8,128)(2,1)S(1)}, u32[]{:S(2)}, u32[]{:S(2)}) collective-permute-start(bf16[16,1024]{1,0:T(8,128)(2,1)} %get-tuple-element.19), channel_id=1, source_target_pairs={{16,0},{20,4},{24,8},{28,12},{17,1},{21,5},{25,9},{29,13},{18,2},{... | collective-permute-start | bytes 98312 | tf_op jit(solution)/shard_map/ppermute | solution.py:280
  46.4 4.2 %copy-start.14 = (f32[32,1024]{1,0:T(8,128)S(1)}, f32[32,1024]{1,0:T(8,128)}, u32[]{:S(2)}) copy-start(f32[32,1024]{1,0:T(8,128)} %copy-done.13) | copy-start | bytes 393220
  46.4 4.2 %copy-start.20 = (f32[32,1024]{1,0:T(8,128)S(1)}, f32[32,1024]{1,0:T(8,128)}, u32[]{:S(2)}) copy-start(f32[32,1024]{1,0:T(8,128)} %copy-done.19) | copy-start | bytes 393220
  46.4 4.2 %copy-start.22 = (f32[16,1024]{1,0:T(8,128)S(1)}, f32[16,1024]{1,0:T(8,128)}, u32[]{:S(2)}) copy-start(f32[16,1024]{1,0:T(8,128)} %get-tuple-element.36) | copy-start | bytes 196612
  48.6 8.5 %copy-start.8 = (bf16[8,4,8,512]{3,2,0,1:T(8,128)(2,1)S(1)}, bf16[8,4,8,512]{3,2,0,1:T(8,128)(2,1)}, u32[]{:S(2)}) copy-start(bf16[8,4,8,512]{3,2,0,1:T(8,128)(2,1)} %copy-done.7) | copy-start | bytes 786436
  48.6 19.6 %collective-permute-start.8 = (bf16[256,1024]{1,0:T(8,128)(2,1)S(1)}, bf16[256,1024]{1,0:T(8,128)(2,1)S(1)}, u32[]{:S(2)}, u32[]{:S(2)}) collective-permute-start(bf16[256,1024]{1,0:T(8,128)(2,1)S(1)} %fusion.2), channel_id=1, source_target_pairs={{0,8},{4,12},{8,0},{12,4},{16,24},{20,28},{24,16},{28,20},{1,9},{5... | collective-permute-start | bytes 1572872 | tf_op jit(solution)/shard_map/ppermute | solution.py:382
  54.0 25.8 %copy-start.1 = (bf16[128,1024]{1,0:T(8,128)(2,1)}, bf16[128,1024]{1,0:T(8,128)(2,1)S(1)}, u32[]{:S(2)}) copy-start(bf16[128,1024]{1,0:T(8,128)(2,1)S(1)} %shard_map.77) | copy-start | bytes 786436
  54.0 15.2 %collective-permute-start.10 = (bf16[128,1024]{1,0:T(8,128)(2,1)S(1)}, bf16[128,1024]{1,0:T(8,128)(2,1)S(1)}, u32[]{:S(2)}, u32[]{:S(2)}) collective-permute-start(bf16[128,1024]{1,0:T(8,128)(2,1)S(1)} %shard_map.77), channel_id=1, source_target_pairs={{0,16},{4,20},{8,24},{12,28},{16,0},{20,4},{24,8},{28,12},{1,17},{... | collective-permute-start | bytes 786440 | tf_op jit(solution)/shard_map/ppermute | solution.py:382
  57.8 20.4 %collective-permute-start.14 = (bf16[32,1024]{1,0:T(8,128)(2,1)}, bf16[32,1024]{1,0:T(8,128)(2,1)}, u32[]{:S(2)}, u32[]{:S(2)}) collective-permute-start(bf16[32,1024]{1,0:T(8,128)(2,1)} %get-tuple-element.47), channel_id=1, source_target_pairs={{0,3},{1,0},{2,1},{3,2},{4,7},{5,4},{6,5},{7,6},{8,11},{9,8},{10,9... | collective-permute-start | bytes 196616 | tf_op jit(solution)/shard_map/ppermute | solution.py:311
  58.5 19.7 %collective-permute-start.13 = (bf16[32,1024]{1,0:T(8,128)(2,1)S(1)}, bf16[32,1024]{1,0:T(8,128)(2,1)}, u32[]{:S(2)}, u32[]{:S(2)}) collective-permute-start(bf16[32,1024]{1,0:T(8,128)(2,1)S(1)} %get-tuple-element.48), channel_id=1, source_target_pairs={{0,2},{1,3},{2,0},{3,1},{4,6},{5,7},{6,4},{7,5},{8,10},{9,11},{10,... | collective-permute-start | bytes 196616 | tf_op jit(solution)/shard_map/ppermute | solution.py:311
  59.3 18.9 %collective-permute-start.12 = (bf16[32,1024]{1,0:T(8,128)(2,1)S(1)}, bf16[32,1024]{1,0:T(8,128)(2,1)}, u32[]{:S(2)}, u32[]{:S(2)}) collective-permute-start(bf16[32,1024]{1,0:T(8,128)(2,1)S(1)} %get-tuple-element.49), channel_id=1, source_target_pairs={{0,1},{1,2},{2,3},{3,0},{4,5},{5,6},{6,7},{7,4},{8,9},{9,10},{10,1... | collective-permute-start | bytes 196616 | tf_op jit(solution)/shard_map/ppermute | solution.py:311
  68.3 1.0 copy-start.17
  69.3 2.5 %copy-start.24 = (bf16[128,1024]{1,0:T(8,128)(2,1)}, bf16[128,1024]{1,0:T(8,128)(2,1)S(1)}, u32[]{:S(2)}) copy-start(bf16[128,1024]{1,0:T(8,128)(2,1)S(1)} %collective-permute-done.10) | copy-start | bytes 786436
  69.3 14.5 %collective-permute-start.11 = (bf16[128,1024]{1,0:T(8,128)(2,1)}, bf16[128,1024]{1,0:T(8,128)(2,1)}, u32[]{:S(2)}, u32[]{:S(2)}) collective-permute-start(bf16[128,1024]{1,0:T(8,128)(2,1)} %fusion.6), channel_id=1, source_target_pairs={{0,16},{4,20},{8,24},{12,28},{16,0},{20,4},{24,8},{28,12},{1,17},{... | collective-permute-start | bytes 786440 | tf_op jit(solution)/shard_map/ppermute | solution.py:382
  73.8 6.0 %copy-start.25 = (bf16[128,1024]{1,0:T(8,128)(2,1)S(1)}, bf16[128,1024]{1,0:T(8,128)(2,1)}, u32[]{:S(2)}) copy-start(bf16[128,1024]{1,0:T(8,128)(2,1)} %copy-done.24) | copy-start | bytes 786436
  73.9 10.0 %copy-start.9 = (f32[128,1024]{1,0:T(8,128)S(1)}, f32[128,1024]{1,0:T(8,128)}, u32[]{:S(2)}) copy-start(f32[128,1024]{1,0:T(8,128)} %fusion.18) | copy-start | bytes 1572868
  73.9 10.0 %copy-start.18 = (bf16[256,1024]{1,0:T(8,128)(2,1)S(1)}, bf16[256,1024]{1,0:T(8,128)(2,1)}, u32[]{:S(2)}) copy-start(bf16[256,1024]{1,0:T(8,128)(2,1)} %copy-done.17) | copy-start | bytes 1572868
  79.9 21.6 %collective-permute-start.18 = (bf16[256,1024]{1,0:T(8,128)(2,1)S(1)}, bf16[256,1024]{1,0:T(8,128)(2,1)S(1)}, u32[]{:S(2)}, u32[]{:S(2)}) collective-permute-start(bf16[256,1024]{1,0:T(8,128)(2,1)S(1)} %pad_maximum_fusion.5), channel_id=1, source_target_pairs={{0,8},{4,12},{8,0},{12,4},{16,24},{20,28},{24,16},{28,20},{1,9},{5... | collective-permute-start | bytes 1572872 | tf_op jit(solution)/shard_map/ppermute | solution.py:382
  85.5 13.2 %copy-start.4 = (bf16[512,1024]{1,0:T(8,128)(2,1)S(1)}, bf16[512,1024]{1,0:T(8,128)(2,1)}, u32[]{:S(2)}) copy-start(bf16[512,1024]{1,0:T(8,128)(2,1)} %param.6) | copy-start | bytes 3145732
  87.4 14.1 %copy-start.2 = (bf16[128,1024]{1,0:T(8,128)(2,1)S(1)}, bf16[128,1024]{1,0:T(8,128)(2,1)}, u32[]{:S(2)}) copy-start(bf16[128,1024]{1,0:T(8,128)(2,1)} %copy-done.1) | copy-start | bytes 786436
  87.4 12.7 %collective-permute-start.17 = (bf16[32,1024]{1,0:T(8,128)(2,1)S(1)}, bf16[32,1024]{1,0:T(8,128)(2,1)S(1)}, u32[]{:S(2)}, u32[]{:S(2)}) collective-permute-start(bf16[32,1024]{1,0:T(8,128)(2,1)S(1)} %pad_maximum_fusion.8), channel_id=1, source_target_pairs={{0,12},{4,16},{8,20},{12,24},{16,28},{1,13},{5,17},{9,21},{13,25},... | collective-permute-start | bytes 196616 | tf_op jit(solution)/shard_map/ppermute | solution.py:280
  88.9 11.2 %collective-permute-start.16 = (bf16[32,1024]{1,0:T(8,128)(2,1)S(1)}, bf16[32,1024]{1,0:T(8,128)(2,1)S(1)}, u32[]{:S(2)}, u32[]{:S(2)}) collective-permute-start(bf16[32,1024]{1,0:T(8,128)(2,1)S(1)} %pad_maximum_fusion.8), channel_id=1, source_target_pairs={{0,8},{4,12},{8,16},{12,20},{16,24},{20,28},{1,9},{5,13},{9,17},{1... | collective-permute-start | bytes 196616 | tf_op jit(solution)/shard_map/ppermute | solution.py:280
  91.2 9.3 %collective-permute-start.15 = (bf16[32,1024]{1,0:T(8,128)(2,1)S(1)}, bf16[32,1024]{1,0:T(8,128)(2,1)S(1)}, u32[]{:S(2)}, u32[]{:S(2)}) collective-permute-start(bf16[32,1024]{1,0:T(8,128)(2,1)S(1)} %pad_maximum_fusion.8), channel_id=1, source_target_pairs={{0,4},{4,8},{8,12},{12,16},{16,20},{20,24},{24,28},{1,5},{5,9},{9,... | collective-permute-start | bytes 196616 | tf_op jit(solution)/shard_map/ppermute | solution.py:280
  100.1 3.3 %copy-start.10 = (bf16[512,1024]{1,0:T(8,128)(2,1)}, bf16[512,1024]{1,0:T(8,128)(2,1)S(1)}, u32[]{:S(2)}) copy-start(bf16[512,1024]{1,0:T(8,128)(2,1)S(1)} %get-tuple-element.37) | copy-start | bytes 3145732
  100.1 3.3 %copy-start.11 = (bf16[512,1024]{1,0:T(8,128)(2,1)}, bf16[512,1024]{1,0:T(8,128)(2,1)S(1)}, u32[]{:S(2)}) copy-start(bf16[512,1024]{1,0:T(8,128)(2,1)S(1)} %get-tuple-element.38) | copy-start | bytes 3145732
  100.1 3.3 %copy-start.21 = (f32[32,1024]{1,0:T(8,128)}, f32[32,1024]{1,0:T(8,128)S(1)}, u32[]{:S(2)}) copy-start(f32[32,1024]{1,0:T(8,128)S(1)} %convert_element_type.81) | copy-start | bytes 393220
  100.1 1.4 copy-start.15
  100.6 0.9 copy-start.16
  101.5 1.8 %copy-start.29 = (bf16[256,1024]{1,0:T(8,128)(2,1)}, bf16[256,1024]{1,0:T(8,128)(2,1)S(1)}, u32[]{:S(2)}) copy-start(bf16[256,1024]{1,0:T(8,128)(2,1)S(1)} %collective-permute-done.18) | copy-start | bytes 1572868
  101.5 7.3 %copy-start.23 = (f32[16,1024]{1,0:T(8,128)S(1)}, f32[16,1024]{1,0:T(8,128)}, u32[]{:S(2)}) copy-start(f32[16,1024]{1,0:T(8,128)} %get-tuple-element.34) | copy-start | bytes 196612
  103.4 6.5 %collective-permute-start.19 = (f32[256,1024]{1,0:T(8,128)}, f32[256,1024]{1,0:T(8,128)}, u32[]{:S(2)}, u32[]{:S(2)}) collective-permute-start(f32[256,1024]{1,0:T(8,128)} %fusion), channel_id=1, source_target_pairs={{0,1},{1,0},{2,3},{3,2},{4,5},{5,4},{6,7},{7,6},{8,9},{9,8},{10,11... | collective-permute-start | bytes 3145736 | tf_op jit(solution)/shard_map/ppermute | solution.py:382
  103.4 4.8 %collective-permute-start.20 = (bf16[16,1024]{1,0:T(8,128)(2,1)}, bf16[16,1024]{1,0:T(8,128)(2,1)S(1)}, u32[]{:S(2)}, u32[]{:S(2)}) collective-permute-start(bf16[16,1024]{1,0:T(8,128)(2,1)} %get-tuple-element.27), channel_id=1, source_target_pairs={{0,16},{4,20},{8,24},{12,28},{1,17},{5,21},{9,25},{13,29},{2,18},{... | collective-permute-start | bytes 98312 | tf_op jit(solution)/shard_map/ppermute | solution.py:280
  108.2 0.6 copy-start.27
  113.4 28.8 %collective-permute-start.21 = (bf16[128,1024]{1,0:T(8,128)(2,1)}, bf16[128,1024]{1,0:T(8,128)(2,1)}, u32[]{:S(2)}, u32[]{:S(2)}) collective-permute-start(bf16[128,1024]{1,0:T(8,128)(2,1)} %get-tuple-element.44), channel_id=1, source_target_pairs={{0,0},{1,8},{2,16},{3,24},{4,4},{5,12},{6,20},{7,28},{8,9},{9,1},{... | collective-permute-start | bytes 786440 | tf_op jit(solution)/shard_map/ppermute | solution.py:430
  117.0 14.7 %copy-start.6 = (bf16[128,4096]{1,0:T(8,128)(2,1)S(1)}, bf16[128,4096]{1,0:T(8,128)(2,1)}, u32[]{:S(2)}) copy-start(bf16[128,4096]{1,0:T(8,128)(2,1)} %param.5) | copy-start | bytes 3145732
  117.0 25.2 %collective-permute-start.22 = (bf16[128,1024]{1,0:T(8,128)(2,1)}, bf16[128,1024]{1,0:T(8,128)(2,1)}, u32[]{:S(2)}, u32[]{:S(2)}) collective-permute-start(bf16[128,1024]{1,0:T(8,128)(2,1)} %get-tuple-element.45), channel_id=1, source_target_pairs={{0,16},{1,24},{2,0},{3,8},{4,20},{5,28},{6,4},{7,12},{8,25},{9,17}... | collective-permute-start | bytes 786440 | tf_op jit(solution)/shard_map/ppermute | solution.py:430
  132.8 13.0 %all-to-all-start.1 = ((bf16[8,32,512]{2,1,0:T(8,128)(2,1)}), bf16[8,32,512]{2,1,0:T(8,128)(2,1)S(1)}, u32[]{:S(2)}, u32[]{:S(2)}) async-start(bf16[8,32,512]{2,1,0:T(8,128)(2,1)} %bitcast.34), calls=%async_computation.1 | async-start | bytes 524288 | tf_op jit(solution)/shard_map/all_to_all | solution.py:519
  136.5 5.8 %copy-start.12 = (bf16[128,1024]{1,0:T(8,128)(2,1)S(1)}, bf16[128,1024]{1,0:T(8,128)(2,1)}, u32[]{:S(2)}) copy-start(bf16[128,1024]{1,0:T(8,128)(2,1)} %pad_maximum_fusion.7) | copy-start | bytes 786436
  136.5 5.7 %collective-permute-start.25 = (bf16[128,32]{1,0:T(8,128)(2,1)S(1)}, bf16[128,32]{1,0:T(8,128)(2,1)S(1)}, u32[]{:S(2)}, u32[]{:S(2)}) collective-permute-start(bf16[128,32]{1,0:T(8,128)(2,1)S(1)} %slice.180), channel_id=1, source_target_pairs={{0,3},{1,0},{2,1},{3,2},{4,7},{5,4},{6,5},{7,6},{8,11},{9,8},{10,9... | collective-permute-start | bytes 24584 | tf_op jit(solution)/shard_map/ppermute | solution.py:311
  136.5 5.7 %collective-permute-start.24 = (bf16[128,32]{1,0:T(8,128)(2,1)S(1)}, bf16[128,32]{1,0:T(8,128)(2,1)S(1)}, u32[]{:S(2)}, u32[]{:S(2)}) collective-permute-start(bf16[128,32]{1,0:T(8,128)(2,1)S(1)} %slice.180), channel_id=1, source_target_pairs={{0,2},{1,3},{2,0},{3,1},{4,6},{5,7},{6,4},{7,5},{8,10},{9,11},{10,... | collective-permute-start | bytes 24584 | tf_op jit(solution)/shard_map/ppermute | solution.py:311
  138.1 4.1 %collective-permute-start.23 = (bf16[128,32]{1,0:T(8,128)(2,1)S(1)}, bf16[128,32]{1,0:T(8,128)(2,1)S(1)}, u32[]{:S(2)}, u32[]{:S(2)}) collective-permute-start(bf16[128,32]{1,0:T(8,128)(2,1)S(1)} %slice.180), channel_id=1, source_target_pairs={{0,1},{1,2},{2,3},{3,0},{4,5},{5,6},{6,7},{7,4},{8,9},{9,10},{10,1... | collective-permute-start | bytes 24584 | tf_op jit(solution)/shard_map/ppermute | solution.py:311
